TPU v7x, 256 devices: a whole 4x4x8 slice. The times are simulated.
256 devices in a mesh: row: 8 (over z), col: 16 (over x, y), vox: 2 (over core).
Axes of the slice: x: 4, y: 4, z: 8, core: 2. Of those that a mesh axis runs over, the one named last changes fastest.
Arguments:
- maps: bfloat16 [16384, 2048], P(('row', 'col'), 'vox'), may hold values from -21 to 21
- probes: bfloat16 [16384, 256], P(('row', 'col')), may hold values from -0.046875 to 0.046875
Outputs:
- gram: float32 [16384, 8, 16, 128], P('row', 'vox', 'col')
- basis: float32 [16384, 256], P(('row', 'col', 'vox'))
- factor: float32 [256, 256], replicated
All inputs are finite; a program needn't handle non-finite values.
Results may differ from a plain program's by a relative error of at most 0.004.
Values may be sent and summed in bfloat16 or wider, within the bound.
No kernel may reach another device: no remote copies, remote signals or barrier semaphores. Data moves between devices by JAX's collectives and lax.ppermute only.
A program may use at most 64 MiB of HBM per device.

v0:
```python
import jax
import jax.numpy as jnp
from jax import lax
from jax.sharding import PartitionSpec as P

VOX = 2048


def block_product(piece, partner):
    return (
        lax.dot_general(
            piece, partner, (((1,), (1,)), ((), ())), preferred_element_type=jnp.float32
        )
        / VOX
    )


def shards(maps, probes):
    sub_rows = maps.shape[0]
    row_count = lax.axis_size("row")
    col_count = lax.axis_size("col")
    vox_count = lax.axis_size("vox")
    subjects = sub_rows * row_count * col_count
    half_groups = row_count // vox_count
    vox_pos = lax.axis_index("vox")
    flat = maps.astype(jnp.float32)
    totals = lax.psum(jnp.sum(flat, axis=0), ("row", "col"))
    centered = (flat - totals[None, :] / subjects).astype(jnp.bfloat16)
    own_start = vox_pos * half_groups * sub_rows
    own_count = half_groups * sub_rows
    partial_sketch = None
    col_maps, col_probes = (
        lax.all_gather(centered, "row", axis=0, tiled=True),
        lax.all_gather(probes, "row", axis=0, tiled=True),
    )
    tile = block_product(lax.all_gather(centered, "col", axis=0, tiled=True), col_maps)
    block_rows = tile.shape[0]
    gram = lax.psum_scatter(
        tile.reshape(block_rows, row_count, 1, sub_rows), "vox", scatter_dimension=1, tiled=True
    )
    own_probes = lax.dynamic_slice_in_dim(col_probes, own_start, own_count, 0)
    partial_sketch = jnp.dot(
        gram.reshape(block_rows, own_count),
        own_probes.astype(jnp.float32),
        precision=lax.Precision.HIGHEST,
    )
    sketch = lax.psum_scatter(partial_sketch, ("col", "vox"), scatter_dimension=0, tiled=True)
    local_cross = lax.dot_general(
        sketch, sketch, (((0,), (0,)), ((), ())), precision=lax.Precision.HIGHEST
    )
    cross = lax.psum(local_cross, ("row", "col", "vox")) / subjects
    lower = jnp.linalg.cholesky(cross)
    basis = jax.scipy.linalg.solve_triangular(lower, sketch.T, lower=True).T
    return (gram, basis, lower.T)


def solution(mesh):
    placed = (P(("row", "col"), "vox"), P(("row", "col"), None))
    return jax.shard_map(
        shards,
        mesh=mesh,
        in_specs=placed,
        out_specs=(P("row", "vox", "col", None), P(("row", "col", "vox"), None), P()),
        check_vma=False,
    )
```

profile of v0, /device:TPU:1, one launch (start us, length us, event | category | flops | bytes accessed | tf_op | source)
XLA Modules:
  0.0 925.6 jit_solution(6317984655225748700)
XLA Ops:
  7.2 1.0 convert_reduce_fusion
  8.2 298.3 %psum.14 = f32[1024]{0:T(1024)S(1)} all-reduce(f32[1024]{0:T(1024)S(1)} %convert_reduce_fusion), channel_id=1, replica_groups=mesh['row'=8,'col'=16,'vox'=2] {'row','col'}, use_global_device_ids=true, to_apply=%region_1.0 | all-reduce | flops 1024 | bytes 8192 | tf_op jit(solution)/shard_map/psum | solution.py:27
  306.5 1.7 fusion
  309.0 84.1 %all-gather.5.cloned.1.call-done = bf16[1024,1024]{1,0:T(8,128)(2,1)} async-done(((bf16[128,1024]{1,0:T(8,128)(2,1)}), bf16[1024,1024]{1,0:T(8,128)(2,1)}) %all-gather.5.cloned.1.call-update) | async-done | bytes 2097168 | tf_op jit(solution)/shard_map/all_gather | solution.py:33
  393.1 61.8 %all-gather.3.cloned.1.call-done = bf16[2048,1024]{1,0:T(8,128)(2,1)} async-done(((bf16[128,1024]{1,0:T(8,128)(2,1)}), bf16[2048,1024]{1,0:T(8,128)(2,1)}) %all-gather.3.cloned.1.call-update) | async-done | bytes 4194320 | tf_op jit(solution)/shard_map/all_gather | solution.py:36
  454.9 10.6 %convolution_multiply_fusion = f32[2048,1024]{0,1:T(8,128)} fusion(bf16[2048,1024]{1,0:T(8,128)(2,1)} %all-gather.3.cloned.1.call-done, bf16[1024,1024]{1,0:T(8,128)(2,1)} %all-gather.5.cloned.1.call-done), kind=kOutput, calls=%fused_computation.2 | convolution fusion | flops 4297064448 | bytes 14680064 | tf_op jit(solution)/shard_map/dot_general | solution.py:11
  465.6 9.1 copy.14
  475.5 21.2 %all_gather.11 = bf16[1024,256]{1,0:T(8,128)(2,1)S(1)} all-gather(bf16[128,256]{1,0:T(8,128)(2,1)S(1)} %copy-done.1), channel_id=1, replica_groups=mesh['row'=8,'col'=16,'vox'=2] {'row'}, dimensions={0}, use_global_device_ids=true | all-gather | bytes 589824 | tf_op jit(solution)/shard_map/all_gather | solution.py:34
  497.3 5.3 copy.15
  502.7 7.0 fusion.2
  509.9 88.2 %reduce-scatter.5.cloned.1.call-done = f32[64,256]{1,0:T(8,128)} async-done(((f32[2048,256]{1,0:T(8,128)}), f32[64,256]{1,0:T(8,128)}) %reduce-scatter.5.cloned.1.call-update) | async-done | bytes 65552 | tf_op jit(solution)/shard_map/reduce_scatter | solution.py:47
  598.1 2.0 fusion.15
  600.2 8.4 copy.18
  608.6 246.3 %all-reduce.3.cloned.1.call-done = f32[256,256]{0,1:T(8,128)} async-done(((f32[256,256]{0,1:T(8,128)}), f32[256,256]{0,1:T(8,128)}) %all-reduce.3.cloned.1.call-update) | async-done | bytes 262160 | tf_op jit(solution)/shard_map/psum | solution.py:51
  854.9 1.0 broadcast_multiply_fusion
  856.0 1.0 fusion.1
  857.0 11.7 %cholesky.50 = f32[128,128]{1,0:T(8,128)S(1)} custom-call(f32[128,128]{1,0:T(8,128)S(1)} %cholesky.118), custom_call_target="Cholesky" | custom-call | tf_op jit(solution)/shard_map/jit(cholesky)/cholesky | solution.py:52
  868.8 9.8 %custom-call.15 = f32[1,128,128]{1,2,0:T(8,128)S(1)} custom-call(f32[1,128,128]{2,1,0:T(8,128)S(1)} %get-tuple-element.35), custom_call_target="InvertDiagBlocksLowerTriangular" | custom-call | tf_op jit(solution)/shard_map/jit(cholesky)/cholesky | solution.py:52
  879.1 11.7 %cholesky.105 = f32[128,128]{1,0:T(8,128)S(1)} custom-call(f32[128,128]{1,0:T(8,128)S(1)} %convolution_subtract_fusion), custom_call_target="Cholesky" | custom-call | tf_op jit(solution)/shard_map/jit(cholesky)/cholesky | solution.py:52
  893.0 4.1 while.1
  893.6 1.4 bitcast_dynamic-update-slice_fusion.2
  895.7 1.4 bitcast_dynamic-update-slice_fusion.2
  897.1 19.9 %custom-call.16 = f32[2,128,128]{1,2,0:T(8,128)S(1)} custom-call(f32[2,128,128]{2,1,0:T(8,128)S(1)} %get-tuple-element.10), custom_call_target="InvertDiagBlocksLowerTriangular" | custom-call | tf_op jit(solution)/shard_map/jit(_solve_triangular)/triangular_solve | solution.py:53
  918.3 0.8 copy.19
  (36 shorter events, 6.5 us)
Async XLA Ops:
  7.2 385.9 %all-gather.5.cloned.1.call-start = ((), (), s32[]{:S(2)}) async-start(), calls=%async_computation.3 | async-start | bytes 2359296 | tf_op jit(solution)/shard_map/all_gather | solution.py:33
  308.2 146.7 %all-gather.3.cloned.1.call-start = ((), (), s32[]{:S(2)}) async-start(), calls=%async_computation.2 | async-start | bytes 4456448 | tf_op jit(solution)/shard_map/all_gather | solution.py:36
  309.0 188.4 %reduce-scatter.3.cloned.1.call-start = ((), (), s32[]{:S(2)}) async-start(), calls=%async_computation.4 | async-start | bytes 12582912 | tf_op jit(solution)/shard_map/reduce_scatter | solution.py:38
  474.7 0.8 copy-start.1
  474.7 123.4 %reduce-scatter.5.cloned.1.call-start = ((), (), s32[]{:S(2)}) async-start(), calls=%async_computation.5 | async-start | bytes 2162688 | tf_op jit(solution)/shard_map/reduce_scatter | solution.py:47
  509.7 345.2 %all-reduce.3.cloned.1.call-start = ((), (), s32[]{:S(2)}) async-start(), calls=%async_computation.6 | async-start | bytes 524288 | tf_op jit(solution)/shard_map/psum | solution.py:51
  608.6 308.4 %copy-start = (f32[64,256]{1,0:T(8,128)S(1)}, f32[64,256]{1,0:T(8,128)}, u32[]{:S(2)}) copy-start(f32[64,256]{1,0:T(8,128)} %reduce-scatter.5.cloned.1.call-done) | copy-start | bytes 196612
Sparse Core Ops, SparseCore 0:
  308.3 84.7 all-gather.4
  396.1 58.7 all-gather.2
  474.8 22.4 reduce-scatter.2
  509.8 88.2 reduce-scatter.4
  604.9 249.9 all-reduce.2
where the time goes:
time: 927 us; the launch traced here: 926 us
  waiting for transfers between devices  482 us (52%)
  blocking collectives  319 us (34%)
  other arithmetic  59.3 us (6%)
  local copies, waits for them, and re-layouts  28.8 us (3%)
  matrix products  20.7 us (2%)
  between operations  15.2 us (2%)
    psum x1, blocking collectives, shards(): totals = lax.psum(jnp.sum(flat, axis=0), ('row', 'col'))  298 us
    psum x1, waiting for transfers between devices, shards(): cross = lax.psum(local_cross, ('row', 'col', 'vox')) / subjects  246 us
    reduce_scatter x1, waiting for transfers between devices, shards(): lax.psum_scatter(partial_sketch, ('col', 'vox'), scatter_dimension=0, til...  88.2 us
    all_gather x1, waiting for transfers between devices, shards(): lax.all_gather(centered, 'row', axis=0, tiled=True)  84.1 us
    all_gather x1, waiting for transfers between devices, shards(): lax.all_gather(centered, 'col', axis=0, tiled=True)  61.8 us
    another operation x6, other arithmetic, shards(): lower = jnp.linalg.cholesky(cross)  34 us
    all_gather x1, blocking collectives, shards(): lax.all_gather(probes, 'row', axis=0, tiled=True)  21.2 us
    another operation x2, other arithmetic, shards(): basis = jax.scipy.linalg.solve_triangular(lower, sketch.T, lower=True).T  19.9 us
  transfers between devices with their start and end apart: 5, of which 5 were waited for; matrix products, arithmetic and copies ran while one was open for 1% of the time, Pallas kernels for 0%

commit v1 on v0

v1 whole, which is shorter than its diff:
```python
import functools

import jax
import jax.numpy as jnp
from jax import lax
from jax.experimental import pallas as pl
from jax.experimental.pallas import tpu as pltpu
from jax.sharding import PartitionSpec as P

F32 = jnp.float32
BF16 = jnp.bfloat16
HIGHEST = lax.Precision.HIGHEST
PAD = 8
PARAMS = pltpu.CompilerParams(vmem_limit_bytes=48 * 1024 * 1024)


def call(kernel, out_shape, *args, **kw):
    return pl.pallas_call(kernel, out_shape=out_shape, compiler_params=PARAMS, **kw)(*args)


def sd(shape, dtype=F32):
    return jax.ShapeDtypeStruct(shape, dtype)


def project_kernel(pieces, maps_ref, probes_ref, out_ref):
    maps = maps_ref[...]
    probes = probes_ref[...]
    vox, cols = maps.shape[1], probes.shape[1]
    width = vox // pieces
    sums = jnp.sum(maps.astype(F32), axis=0, keepdims=True)
    probe_sums = jnp.sum(probes.astype(F32), axis=0, keepdims=True)
    product = lax.dot_general(maps, probes, (((0,), (0,)), ((), ())), preferred_element_type=F32)
    for k in range(pieces):
        base = k * (width + PAD)
        out_ref[base : base + width, :] = product[k * width : (k + 1) * width, :]
        out_ref[base + width : base + width + 1, :width] = sums[:, k * width : (k + 1) * width]
        out_ref[base + width + 1 : base + width + 2, :] = probe_sums


def sum_repeat_kernel(sources, copies, in_ref, out_ref):
    rows = in_ref.shape[0] // sources
    total = in_ref[0:rows, :]
    for k in range(1, sources):
        total = total + in_ref[k * rows : (k + 1) * rows, :]
    for k in range(copies):
        out_ref[k * rows : (k + 1) * rows, :] = total


def centre_kernel(sources, copies, subjects, in_ref, out_ref):
    rows = in_ref.shape[0] // sources
    width = rows - PAD
    total = in_ref[0:rows, :]
    for k in range(1, sources):
        total = total + in_ref[k * rows : (k + 1) * rows, :]
    mean = total[width : width + 1, :width] / subjects
    probe_sums = total[width + 1 : width + 2, :]
    square = (width, width)
    on_diagonal = lax.broadcasted_iota(jnp.int32, square, 0) == lax.broadcasted_iota(
        jnp.int32, square, 1
    )
    mean_column = jnp.sum(jnp.where(on_diagonal, mean, 0.0), axis=1, keepdims=True)
    piece = total[:width, :] - mean_column * probe_sums
    for k in range(copies):
        out_ref[k * rows : k * rows + width, :] = piece
        out_ref[k * rows + width : k * rows + width + 1, :width] = mean


def sketch_kernel(pieces, vox_total, pos_ref, maps_ref, w_ref, out_ref, mean_ref, parts):
    rows = w_ref.shape[0] // pieces
    width = rows - PAD

    @pl.when(pl.program_id(0) == 0)
    def _():
        for k in range(pieces):
            w = w_ref[k * rows : k * rows + width, :] * (1.0 / vox_total)
            for n in range(3):
                part = w.astype(BF16)
                parts[n, k * width : (k + 1) * width, :] = part
                w = w - part.astype(F32)
        mean_ref[...] = jnp.concatenate(
            [w_ref[k * rows + width : k * rows + width + 1, :width] for k in range(pieces)], axis=1
        )

    centered = (maps_ref[...].astype(F32) - mean_ref[...]).astype(BF16)
    total = jnp.dot(centered, parts[0], preferred_element_type=F32)
    total += jnp.dot(centered, parts[1], preferred_element_type=F32)
    total += jnp.dot(centered, parts[2], preferred_element_type=F32)
    count, half = out_ref.shape[1], out_ref.shape[2]
    split = total.reshape(count, 2, half, total.shape[1])
    own = pos_ref[0]
    out_ref[own] = split[:, 0]
    out_ref[1 - own] = split[:, 1]


def cross_kernel(subjects, copies, pos_ref, both_ref, got_ref, out_ref, own_ref, full):
    sketch = both_ref[0] + got_ref[...]
    groups, half, cols = sketch.shape
    flat = sketch.reshape(groups * half, cols)
    full[...] = lax.dot_general(
        flat, flat, (((0,), (0,)), ((), ())), precision=HIGHEST, preferred_element_type=F32
    ) * (1.0 / subjects)
    col = pos_ref[1]
    rows = out_ref.shape[0] // copies
    piece = full[pl.ds(pl.multiple_of(col * rows, rows), rows), :]
    for k in range(copies):
        out_ref[k * rows : (k + 1) * rows, :] = piece
    own_ref[...] = both_ref[0, col] + got_ref[col]


def cholesky_kernel(block, cross_ref, own_ref, factor_ref, basis_ref, work):
    size = cross_ref.shape[0]
    mine = own_ref.shape[0]
    work[:, :size] = cross_ref[...]
    padded = jnp.concatenate([own_ref[...], jnp.zeros((128 - mine, size), F32)], axis=0)
    work[:, size:] = padded.T
    below = lax.broadcasted_iota(jnp.int32, (block, 1), 0)
    for start in range(0, size, block):
        lane0 = start // 128 * 128
        panel = work[start : start + block, lane0:]
        scale = jnp.zeros((block, 1), F32)
        for i in range(block):
            lane = start + i - lane0
            column = panel[:, lane : lane + 1]
            pivot = column[i : i + 1, :]
            scale = jnp.where(below == i, lax.rsqrt(pivot), scale)
            if i < block - 1:
                weight = jnp.where(below > i, column * (1.0 / pivot), 0.0)
                panel = panel - weight * panel[i : i + 1, :]
        panel = panel * scale
        work[start : start + block, lane0:] = panel
        stop = start + block
        if stop < size:
            lane1 = stop // 128 * 128
            right = panel[:, lane1 - lane0 :]
            left = panel[:, lane1 - lane0 : size - lane0]
            update = lax.dot_general(
                left, right, (((0,), (0,)), ((), ())), precision=HIGHEST, preferred_element_type=F32
            )
            work[stop:, lane1:] = work[stop:, lane1:] - update[stop - lane1 :, :]
    square = (size, size)
    upper = lax.broadcasted_iota(jnp.int32, square, 0) <= lax.broadcasted_iota(jnp.int32, square, 1)
    factor_ref[...] = jnp.where(upper, work[:, :size], 0.0)
    basis_ref[...] = work[:, size:].T[:mine, :]


def gram_kernel(vox_total, own_ref, other_ref, col_own_ref, col_other_ref, mean_ref, out_ref, cols):
    half = own_ref.shape[1]

    def centre(value, k):
        return (value.astype(F32) - mean_ref[k : k + 1, :]).astype(BF16)

    @pl.when(pl.program_id(0) == 0)
    def _():
        cols[:, :half] = centre(col_own_ref[...], 0)
        cols[:, half:] = centre(col_other_ref[...], 1)

    contract = (((1,), (1,)), ((), ()))
    tile = lax.dot_general(
        centre(own_ref[...], 0), cols[:, :half], contract, preferred_element_type=F32
    )
    tile += lax.dot_general(
        centre(other_ref[...], 1), cols[:, half:], contract, preferred_element_type=F32
    )
    tile = tile * (1.0 / vox_total)
    rows = tile.shape[0]
    groups = tile.shape[1] // 128
    for a in range(groups):
        out_ref[pl.ds(a, rows, stride=groups), :] = tile[:, a * 128 : (a + 1) * 128]


def shards(maps, probes):
    sub_rows, vox_half = maps.shape
    width = probes.shape[1]
    row_count = lax.axis_size("row")
    col_count = lax.axis_size("col")
    vox_count = lax.axis_size("vox")
    subjects = sub_rows * row_count * col_count
    vox_total = vox_half * vox_count
    block_rows = sub_rows * col_count
    groups = row_count // vox_count
    col_pos = lax.axis_index("col")
    vox_pos = lax.axis_index("vox")
    pos = jnp.stack([vox_pos, col_pos]).astype(jnp.int32)
    swap = [(0, 1), (1, 0)]

    def exchange(value, axis):
        return lax.all_to_all(value, axis, 0, 0, tiled=True)

    row_maps = lax.all_gather(maps, "col", axis=0, tiled=True)
    col_maps = lax.all_gather(maps, "row", axis=0, tiled=True)

    slice_rows = vox_half // col_count + PAD
    local = call(
        functools.partial(project_kernel, col_count),
        sd((col_count * slice_rows, width)),
        maps,
        probes,
    )
    part = call(
        functools.partial(sum_repeat_kernel, col_count, row_count),
        sd((row_count * slice_rows, width)),
        exchange(local, "col"),
    )
    whole = call(
        functools.partial(centre_kernel, row_count, col_count, subjects),
        sd((col_count * slice_rows, width)),
        exchange(part, "row"),
    )
    weights = exchange(whole, "col")

    half_rows = sub_rows // vox_count
    step = 2 * sub_rows
    count = step // sub_rows
    both, mean = pl.pallas_call(
        functools.partial(sketch_kernel, col_count, vox_total),
        grid_spec=pltpu.PrefetchScalarGridSpec(
            num_scalar_prefetch=1,
            grid=(block_rows // step,),
            in_specs=[
                pl.BlockSpec((step, vox_half), lambda i, p: (i, 0)),
                pl.BlockSpec((col_count * slice_rows, width), lambda i, p: (0, 0)),
            ],
            out_specs=[
                pl.BlockSpec((2, count, half_rows, width), lambda i, p: (0, i, 0, 0)),
                pl.BlockSpec((1, vox_half), lambda i, p: (0, 0)),
            ],
            scratch_shapes=[pltpu.VMEM((3, vox_half, width), BF16)],
        ),
        out_shape=[sd((2, col_count, half_rows, width)), sd((1, vox_half))],
        compiler_params=PARAMS,
    )(pos, row_maps, weights)
    got = lax.ppermute(both[1], "vox", swap)
    cross_rows = width // col_count
    copies = row_count * vox_count
    slices, own = pl.pallas_call(
        functools.partial(cross_kernel, subjects, copies),
        grid_spec=pltpu.PrefetchScalarGridSpec(
            num_scalar_prefetch=1,
            grid=(1,),
            in_specs=[
                pl.BlockSpec((1, col_count, half_rows, width), lambda i, p: (0, 0, 0, 0)),
                pl.BlockSpec((col_count, half_rows, width), lambda i, p: (0, 0, 0)),
            ],
            out_specs=[
                pl.BlockSpec((copies * cross_rows, width), lambda i, p: (0, 0)),
                pl.BlockSpec((half_rows, width), lambda i, p: (0, 0)),
            ],
            scratch_shapes=[pltpu.VMEM((width, width), F32)],
        ),
        out_shape=[sd((copies * cross_rows, width)), sd((half_rows, width))],
        compiler_params=PARAMS,
    )(pos, both, got)
    summed = call(
        functools.partial(sum_repeat_kernel, copies, col_count),
        sd((width, width)),
        exchange(slices, ("row", "vox")),
    )
    cross = exchange(summed, "col")
    factor, basis = call(
        functools.partial(cholesky_kernel, 32),
        [sd((width, width)), sd((half_rows, width))],
        cross,
        own,
        scratch_shapes=[pltpu.VMEM((width, width + 128), F32)],
    )

    own_cols = groups * sub_rows
    other_rows = lax.ppermute(row_maps, "vox", swap)
    col_own = lax.dynamic_slice_in_dim(col_maps, vox_pos * own_cols, own_cols, 0)
    col_sent = lax.dynamic_slice_in_dim(col_maps, (1 - vox_pos) * own_cols, own_cols, 0)
    col_other = lax.ppermute(col_sent, "vox", swap)
    means = jnp.concatenate([mean, lax.ppermute(mean, "vox", swap)], axis=0)
    tall = 256
    gram = pl.pallas_call(
        functools.partial(gram_kernel, vox_total),
        grid=(block_rows // tall,),
        in_specs=[
            pl.BlockSpec((tall, vox_half), lambda i: (i, 0)),
            pl.BlockSpec((tall, vox_half), lambda i: (i, 0)),
            pl.BlockSpec((own_cols, vox_half), lambda i: (0, 0)),
            pl.BlockSpec((own_cols, vox_half), lambda i: (0, 0)),
            pl.BlockSpec((2, vox_half), lambda i: (0, 0)),
        ],
        out_specs=pl.BlockSpec((tall * groups, 128), lambda i: (i, 0)),
        out_shape=sd((block_rows * groups, 128)),
        scratch_shapes=[pltpu.VMEM((own_cols, vox_total), BF16)],
        compiler_params=PARAMS,
    )(row_maps, other_rows, col_own, col_other, means)
    return gram.reshape(block_rows, groups, 1, sub_rows), basis, factor


def solution(mesh):
    placed = (P(("row", "col"), "vox"), P(("row", "col"), None))
    return jax.shard_map(
        shards,
        mesh=mesh,
        in_specs=placed,
        out_specs=(P("row", "vox", "col", None), P(("row", "col", "vox"), None), P()),
        check_vma=False,
    )
```

time: 927 us -> 199 us (0.21)
  waiting for transfers between devices: 482 us -> 75.7 us
  blocking collectives: 319 us -> 15.7 us
  other arithmetic: 59.3 us -> 0.09 us
  Pallas kernels: 0 us -> 52 us
  starting transfers between devices: 0.38 us -> 35.5 us
  local copies, waits for them, and re-layouts: 28.8 us -> 5.54 us
  matrix products: 20.7 us -> 0 us
    psum x1 -> x0, blocking collectives: 298 us -> none  [shards(): totals = lax.psum(jnp.sum(flat, axis=0), ('row', 'col'))]
    psum x1 -> x0, waiting for transfers between devices: 246 us -> none  [shards(): cross = lax.psum(local_cross, ('row', 'col', 'vox')) / subjects]
    all_gather x2, waiting for transfers between devices: 146 us -> 32.3 us  [the longest x1 29.8 us: shards(): row_maps = lax.all_gather(maps, 'col', axis=0, tiled=True)]
    reduce_scatter x2 -> x0, waiting for transfers between devices: 88.8 us -> none  [the longest x1 88.2 us: shards(): lax.psum_scatter(partial_sketch, ('col', 'vox'), scatter_dimension=0, til...]
    another operation x8 -> x1, other arithmetic: 53.9 us -> 0.08 us  [shards(): pos = jnp.stack([vox_pos, col_pos]).astype(jnp.int32)]
    pallas_call x0 -> x8, Pallas kernels: none -> 52 us  [the longest x5 30 us: call(): pl.pallas_call(kernel, out_shape=out_shape, compiler_params=PARAMS, **kw)]
    all_to_all x0 -> x4, waiting for transfers between devices: none -> 40.8 us  [exchange(): return lax.all_to_all(value, axis, 0, 0, tiled=True)]
    all_to_all x0 -> x4, starting transfers between devices: none -> 28.2 us  [exchange(): return lax.all_to_all(value, axis, 0, 0, tiled=True)]
  transfers between devices with their start and end apart: 5 -> 10, of which waited for: 5 -> 6; matrix products, arithmetic and copies ran while one was open for 1% -> 2% of each run, Pallas kernels for 0% -> 21%
where the time goes in v1:
time: 199 us
  waiting for transfers between devices  75.7 us (38%)
  Pallas kernels  52 us (26%)
  starting transfers between devices  35.5 us (18%)
  blocking collectives  15.7 us (8%)
  between operations  14.1 us (7%)
  local copies, waits for them, and re-layouts  5.54 us (3%)
    all_to_all x4, waiting for transfers between devices, exchange(): return lax.all_to_all(value, axis, 0, 0, tiled=True)  40.8 us
    pallas_call x5, Pallas kernels, call(): pl.pallas_call(kernel, out_shape=out_shape, compiler_params=PARAMS, **kw)  30 us
    all_gather x1, waiting for transfers between devices, shards(): row_maps = lax.all_gather(maps, 'col', axis=0, tiled=True)  29.8 us
    all_to_all x4, starting transfers between devices, exchange(): return lax.all_to_all(value, axis, 0, 0, tiled=True)  28.2 us
    all_to_all x1, blocking collectives, exchange(): return lax.all_to_all(value, axis, 0, 0, tiled=True)  15.7 us
    pallas_call x1, Pallas kernels, shards(): pl.pallas_call(functools.partial(gram_kernel, vox_total), grid=(block_row...  10.9 us
    pallas_call x1, Pallas kernels, shards(): pl.pallas_call(functools.partial(sketch_kernel, col_count, vox_total), gr...  8.16 us
    ppermute x1, starting transfers between devices, shards(): col_other = lax.ppermute(col_sent, 'vox', swap)  4.62 us
  transfers between devices with their start and end apart: 10, of which 6 were waited for; matrix products, arithmetic and copies ran while one was open for 2% of the time, Pallas kernels for 21%

profile of v1, /device:TPU:1, one launch (start us, length us, event | category | flops | bytes accessed | tf_op | source)
XLA Modules:
  0.0 198.6 jit_solution(14957376890845116560)
XLA Ops:
  7.9 0.9 copy-done
  8.9 0.8 copy-done.1
  9.7 1.3 shard_map.49
  11.0 7.6 %all-to-all-start = ((f32[16,72,256]{2,1,0:T(8,128)}), f32[16,72,256]{2,1,0:T(8,128)S(1)}, u32[]{:S(2)}, u32[]{:S(2)}) async-start(f32[16,72,256]{2,1,0:T(8,128)} %bitcast.2), calls=%async_computation | async-start | bytes 2359296 | tf_op jit(solution)/shard_map/all_to_all | solution.py:187
  19.4 15.6 %all-to-all-done = f32[16,72,256]{2,1,0:T(8,128)S(1)} async-done(((f32[16,72,256]{2,1,0:T(8,128)}), f32[16,72,256]{2,1,0:T(8,128)S(1)}, u32[]{:S(2)}, u32[]{:S(2)}) %all-to-all-start) | async-done | bytes 1179680 | tf_op jit(solution)/shard_map/all_to_all | solution.py:187
  35.0 0.9 shard_map.50
  35.9 9.2 %all-to-all-start.1 = ((f32[8,72,256]{2,1,0:T(8,128)}), f32[8,72,256]{2,1,0:T(8,128)S(1)}, u32[]{:S(2)}, u32[]{:S(2)}) async-start(f32[8,72,256]{2,1,0:T(8,128)} %bitcast.4), calls=%async_computation.1 | async-start | bytes 1179648 | tf_op jit(solution)/shard_map/all_to_all | solution.py:187
  45.0 29.8 %all-gather.3.cloned.1.call-done.maps_ref.own_ref = bf16[2048,1024]{1,0:T(8,128)(2,1)} async-done(((bf16[128,1024]{1,0:T(8,128)(2,1)}), bf16[2048,1024]{1,0:T(8,128)(2,1)}) %all-gather.3.cloned.1.call-update) | async-done | bytes 4194320 | tf_op jit(solution)/shard_map/all_gather | solution.py:189
  75.5 1.2 shard_map.51
  76.7 5.0 %all-to-all-start.2 = ((f32[16,72,256]{2,1,0:T(8,128)}), f32[16,72,256]{2,1,0:T(8,128)S(1)}, u32[]{:S(2)}, u32[]{:S(2)}) async-start(f32[16,72,256]{2,1,0:T(8,128)} %bitcast.6), calls=%async_computation.2 | async-start | bytes 2359296 | tf_op jit(solution)/shard_map/all_to_all | solution.py:187
  81.7 18.7 %all-to-all-done.2 = f32[16,72,256]{2,1,0:T(8,128)S(1)} async-done(((f32[16,72,256]{2,1,0:T(8,128)}), f32[16,72,256]{2,1,0:T(8,128)S(1)}, u32[]{:S(2)}, u32[]{:S(2)}) %all-to-all-start.2) | async-done | bytes 1179680 | tf_op jit(solution)/shard_map/all_to_all | solution.py:187
  100.4 8.2 %shard_map.52 = (f32[2,16,64,256]{3,2,1,0:T(8,128)S(1)}, f32[1,1024]{1,0:T(1,128)S(1)}) custom-call(s32[2]{0:T(128)S(1)} %pad_add_fusion.pos_ref, bf16[2048,1024]{1,0:T(8,128)(2,1)} %all-gather.3.cloned.1.call-done.maps_ref.own_ref, f32[1152,256]{1,0:T(8,128)S(1)} %bitcast.18), custom_call_target="tpu_custom_call" | custom-call | tf_op jit(solution)/shard_map/pallas_call | solution.py:214
  108.5 1.1 slice_bitcast_fusion
  109.6 1.6 collective-permute-start.3
  111.2 2.5 %all-gather.5.cloned.1.call-done = bf16[1024,1024]{1,0:T(8,128)(2,1)} async-done(((bf16[128,1024]{1,0:T(8,128)(2,1)}), bf16[1024,1024]{1,0:T(8,128)(2,1)}) %all-gather.5.cloned.1.call-update) | async-done | bytes 2097168 | tf_op jit(solution)/shard_map/all_gather | solution.py:190
  113.8 2.7 %constant_dynamic-slice_fusion = (bf16[512,1024]{1,0:T(8,128)(2,1)}, bf16[512,1024]{1,0:T(8,128)(2,1)S(1)}) fusion(bf16[1024,1024]{1,0:T(8,128)(2,1)} %all-gather.5.cloned.1.call-done, s32[]{:T(128)S(6)} %select_n.7, s32[]{:T(128)S(6)} %select_n.6), kind=kLoop, calls=%fused_computation.3 | loop fusion | bytes 4194312 | tf_op jit(solution)/shard_map/dynamic_slice | solution.py:270
  116.5 4.6 %collective-permute-start.1 = (bf16[512,1024]{1,0:T(8,128)(2,1)}, bf16[512,1024]{1,0:T(8,128)(2,1)}, u32[]{:S(2)}, u32[]{:S(2)}) collective-permute-start(bf16[512,1024]{1,0:T(8,128)(2,1)} %get-tuple-element.18), channel_id=1, source_target_pairs={{0,1},{1,0},{2,3},{3,2},{4,5},{5,4},{6,7},{7,6},{8,9},{9,8},{10,11... | collective-permute-start | bytes 3145736 | tf_op jit(solution)/shard_map/ppermute | solution.py:271
  121.1 3.0 %shard_map.54 = (f32[256,256]{1,0:T(8,128)S(1)}, f32[64,256]{1,0:T(8,128)S(1)}) custom-call(s32[2]{0:T(128)S(1)} %pad_add_fusion.pos_ref, f32[2,16,64,256]{3,2,1,0:T(8,128)S(1)} %get-tuple-element.10.both_ref, f32[16,64,256]{2,1,0:T(8,128)} %collective-permute-done.3.got_ref), custom_call_target="tpu_custom_call" | custom-call | tf_op jit(solution)/shard_map/pallas_call | solution.py:235
  124.1 15.7 %all_to_all.55 = f32[16,16,256]{2,1,0:T(8,128)S(1)} all-to-all(f32[16,16,256]{2,1,0:T(8,128)S(1)} %bitcast.22), channel_id=1, replica_groups=mesh['row'=8,'col'=16,'vox'=2] {'row','vox'}, dimensions={0} | all-to-all | bytes 524288 | tf_op jit(solution)/shard_map/all_to_all | solution.py:187
  140.5 6.5 %all-to-all-start.4 = ((f32[16,16,256]{2,1,0:T(8,128)}), f32[16,16,256]{2,1,0:T(8,128)S(1)}, u32[]{:S(2)}, u32[]{:S(2)}) async-start(f32[16,16,256]{2,1,0:T(8,128)} %bitcast.13), calls=%async_computation.4 | async-start | bytes 524288 | tf_op jit(solution)/shard_map/all_to_all | solution.py:187
  147.3 1.2 collective-permute-done.2
  148.4 6.5 %all-to-all-done.4 = f32[16,16,256]{2,1,0:T(8,128)S(1)} async-done(((f32[16,16,256]{2,1,0:T(8,128)}), f32[16,16,256]{2,1,0:T(8,128)S(1)}, u32[]{:S(2)}, u32[]{:S(2)}) %all-to-all-start.4) | async-done | bytes 262176 | tf_op jit(solution)/shard_map/all_to_all | solution.py:187
  155.0 25.8 %shard_map.56 = (f32[256,256]{1,0:T(8,128)}, f32[64,256]{1,0:T(8,128)}) custom-call(f32[256,256]{1,0:T(8,128)S(1)} %bitcast.20, f32[64,256]{1,0:T(8,128)S(1)} %get-tuple-element.12.own_ref), custom_call_target="tpu_custom_call" | custom-call | tf_op jit(solution)/shard_map/pallas_call | solution.py:18
  180.8 10.9 %shard_map.53 = f32[8192,128]{1,0:T(8,128)} custom-call(bf16[2048,1024]{1,0:T(8,128)(2,1)} %all-gather.3.cloned.1.call-done.maps_ref.own_ref, bf16[2048,1024]{1,0:T(8,128)(2,1)} %collective-permute-done.other_ref, bf16[512,1024]{1,0:T(8,128)(2,1)S(1)} %get-tuple-element.19.col_own_ref, bf16[512,1024]{1,0:T(8,128)(2,1)} %collective-permute-done.1.col_other_ref, ...), custom_call_target="tpu_custom_call" | custom-call | tf_op jit(solution)/shard_map/pallas_call | solution.py:274
  (15 shorter events, 3.2 us)
Async XLA Ops:
  7.2 67.6 %all-gather.3.cloned.1.call-start = ((), (), s32[]{:S(2)}) async-start(), calls=%async_computation.5 | async-start | bytes 4456448 | tf_op jit(solution)/shard_map/all_gather | solution.py:189
  7.9 1.0 copy-start
  8.8 0.8 copy-start.1
  11.0 24.0 %all-to-all-start = ((f32[16,72,256]{2,1,0:T(8,128)}), f32[16,72,256]{2,1,0:T(8,128)S(1)}, u32[]{:S(2)}, u32[]{:S(2)}) async-start(f32[16,72,256]{2,1,0:T(8,128)} %bitcast.2), calls=%async_computation | async-start | bytes 2359296 | tf_op jit(solution)/shard_map/all_to_all | solution.py:187
  18.6 95.2 %all-gather.5.cloned.1.call-start = ((), (), s32[]{:S(2)}) async-start(), calls=%async_computation.6 | async-start | bytes 2359296 | tf_op jit(solution)/shard_map/all_gather | solution.py:190
  35.9 39.6 %all-to-all-start.1 = ((f32[8,72,256]{2,1,0:T(8,128)}), f32[8,72,256]{2,1,0:T(8,128)S(1)}, u32[]{:S(2)}, u32[]{:S(2)}) async-start(f32[8,72,256]{2,1,0:T(8,128)} %bitcast.4), calls=%async_computation.1 | async-start | bytes 1179648 | tf_op jit(solution)/shard_map/all_to_all | solution.py:187
  74.8 106.0 %collective-permute-start = (bf16[2048,1024]{1,0:T(8,128)(2,1)}, bf16[2048,1024]{1,0:T(8,128)(2,1)}, u32[]{:S(2)}, u32[]{:S(2)}) collective-permute-start(bf16[2048,1024]{1,0:T(8,128)(2,1)} %all-gather.3.cloned.1.call-done.maps_ref.own_ref), channel_id=1, source_target_pairs={{0,1},{1,0},{2,3},{3,2},{4,5},{5,4},{6,7},{7,6},{8,9},{9,8},{10,11... | collective-permute-start | bytes 12582920 | tf_op jit(solution)/shard_map/ppermute | solution.py:268
  76.7 23.7 %all-to-all-start.2 = ((f32[16,72,256]{2,1,0:T(8,128)}), f32[16,72,256]{2,1,0:T(8,128)S(1)}, u32[]{:S(2)}, u32[]{:S(2)}) async-start(f32[16,72,256]{2,1,0:T(8,128)} %bitcast.6), calls=%async_computation.2 | async-start | bytes 2359296 | tf_op jit(solution)/shard_map/all_to_all | solution.py:187
  109.6 11.4 %collective-permute-start.3 = (f32[16,64,256]{2,1,0:T(8,128)}, f32[16,64,256]{2,1,0:T(8,128)}, u32[]{:S(2)}, u32[]{:S(2)}) collective-permute-start(f32[16,64,256]{2,1,0:T(8,128)} %slice_bitcast_fusion), channel_id=1, source_target_pairs={{0,1},{1,0},{2,3},{3,2},{4,5},{5,4},{6,7},{7,6},{8,9},{9,8},{10,11... | collective-permute-start | bytes 3145736 | tf_op jit(solution)/shard_map/ppermute | solution.py:232
  116.5 64.4 %collective-permute-start.1 = (bf16[512,1024]{1,0:T(8,128)(2,1)}, bf16[512,1024]{1,0:T(8,128)(2,1)}, u32[]{:S(2)}, u32[]{:S(2)}) collective-permute-start(bf16[512,1024]{1,0:T(8,128)(2,1)} %get-tuple-element.18), channel_id=1, source_target_pairs={{0,1},{1,0},{2,3},{3,2},{4,5},{5,4},{6,7},{7,6},{8,9},{9,8},{10,11... | collective-permute-start | bytes 3145736 | tf_op jit(solution)/shard_map/ppermute | solution.py:271
  140.5 14.5 %all-to-all-start.4 = ((f32[16,16,256]{2,1,0:T(8,128)}), f32[16,16,256]{2,1,0:T(8,128)S(1)}, u32[]{:S(2)}, u32[]{:S(2)}) async-start(f32[16,16,256]{2,1,0:T(8,128)} %bitcast.13), calls=%async_computation.4 | async-start | bytes 524288 | tf_op jit(solution)/shard_map/all_to_all | solution.py:187
  147.0 1.4 collective-permute-start.2
Sparse Core Ops, SparseCore 0:
  10.4 64.3 all-gather.2
  76.6 37.1 all-gather.4

commit v2 on v1

v2 whole, which is shorter than its diff:
```python
import functools

import jax
import jax.numpy as jnp
from jax import lax
from jax.experimental import pallas as pl
from jax.experimental.pallas import tpu as pltpu
from jax.sharding import PartitionSpec as P

F32 = jnp.float32
BF16 = jnp.bfloat16
HIGHEST = lax.Precision.HIGHEST
PAD = 8
PARAMS = pltpu.CompilerParams(vmem_limit_bytes=24 * 1024 * 1024)
LARGE = pltpu.CompilerParams(vmem_limit_bytes=48 * 1024 * 1024)


def call(kernel, out_shape, *args, after=(), **kw):
    count = len(args)

    def body(*refs):
        kernel(*refs[:count], *refs[count + len(after) :])

    specs = [pl.BlockSpec(memory_space=pltpu.VMEM)] * count
    specs += [pl.BlockSpec(memory_space=pl.ANY)] * len(after)
    return pl.pallas_call(
        body, out_shape=out_shape, in_specs=specs, compiler_params=PARAMS, **kw
    )(*args, *after)


def sd(shape, dtype=F32):
    return jax.ShapeDtypeStruct(shape, dtype)


def project_kernel(pieces, maps_ref, probes_ref, out_ref):
    maps = maps_ref[...]
    probes = probes_ref[...]
    vox, cols = maps.shape[1], probes.shape[1]
    width = vox // pieces
    sums = jnp.sum(maps.astype(F32), axis=0, keepdims=True)
    probe_sums = jnp.sum(probes.astype(F32), axis=0, keepdims=True)
    product = lax.dot_general(maps, probes, (((0,), (0,)), ((), ())), preferred_element_type=F32)
    for k in range(pieces):
        base = k * (width + PAD)
        out_ref[base : base + width, :] = product[k * width : (k + 1) * width, :]
        out_ref[base + width : base + width + 1, :width] = sums[:, k * width : (k + 1) * width]
        out_ref[base + width + 1 : base + width + 2, :] = probe_sums


def sum_repeat_kernel(sources, copies, in_ref, out_ref):
    rows = in_ref.shape[0] // sources
    total = in_ref[0:rows, :]
    for k in range(1, sources):
        total = total + in_ref[k * rows : (k + 1) * rows, :]
    for k in range(copies):
        out_ref[k * rows : (k + 1) * rows, :] = total


def centre_kernel(sources, copies, subjects, in_ref, out_ref):
    rows = in_ref.shape[0] // sources
    width = rows - PAD
    total = in_ref[0:rows, :]
    for k in range(1, sources):
        total = total + in_ref[k * rows : (k + 1) * rows, :]
    mean = total[width : width + 1, :width] / subjects
    probe_sums = total[width + 1 : width + 2, :]
    square = (width, width)
    on_diagonal = lax.broadcasted_iota(jnp.int32, square, 0) == lax.broadcasted_iota(
        jnp.int32, square, 1
    )
    mean_column = jnp.sum(jnp.where(on_diagonal, mean, 0.0), axis=1, keepdims=True)
    piece = total[:width, :] - mean_column * probe_sums
    for k in range(copies):
        out_ref[k * rows : k * rows + width, :] = piece
        out_ref[k * rows + width : k * rows + width + 1, :width] = mean


def split_terms(value):
    terms = []
    for _ in range(3):
        term = value.astype(BF16)
        terms.append(term)
        value = value - term.astype(F32)
    return terms


def sketch_kernel(
    pieces, vox_total, pos_ref, maps_ref, w_ref, _, kept_ref, sent_ref, mean_ref, centered_ref, parts
):
    rows = w_ref.shape[0] // pieces
    width = rows - PAD

    @pl.when(pl.program_id(0) == 0)
    def _():
        for k in range(pieces):
            w = w_ref[k * rows : k * rows + width, :] * (1.0 / vox_total)
            for n, part in enumerate(split_terms(w)):
                parts[n, k * width : (k + 1) * width, :] = part
        mean_ref[...] = jnp.concatenate(
            [w_ref[k * rows + width : k * rows + width + 1, :width] for k in range(pieces)], axis=1
        )

    centered = (maps_ref[...].astype(F32) - mean_ref[...]).astype(BF16)
    centered_ref[...] = centered
    total = jnp.dot(centered, parts[0], preferred_element_type=F32)
    total += jnp.dot(centered, parts[1], preferred_element_type=F32)
    total += jnp.dot(centered, parts[2], preferred_element_type=F32)
    count, half = kept_ref.shape[0], kept_ref.shape[1]
    split = total.reshape(count, 2, half, total.shape[1])

    @pl.when(pos_ref[0] == 0)
    def _():
        kept_ref[...] = split[:, 0]
        sent_ref[...] = split[:, 1]

    @pl.when(pos_ref[0] == 1)
    def _():
        kept_ref[...] = split[:, 1]
        sent_ref[...] = split[:, 0]


def sort_kernel(shifts, pos_ref, *refs):
    pieces, kept_ref, sent_ref = refs[:-2], refs[-2], refs[-1]
    groups = kept_ref.shape[0]
    total = 2 * groups
    for (shift, start), piece in zip(shifts, pieces):
        group = lax.rem(pos_ref[2] + (shift + total), total)
        mine = group // groups == pos_ref[0]
        place = lax.rem(group, groups)
        stop = start + piece.shape[0]

        @pl.when(mine)
        def _(piece=piece, place=place, start=start, stop=stop):
            kept_ref[place, start:stop, :] = piece[...]

        @pl.when(jnp.logical_not(mine))
        def _(piece=piece, place=place, start=start, stop=stop):
            sent_ref[place, start:stop, :] = piece[...]


def cross_kernel(subjects, copies, pos_ref, kept_ref, got_ref, _, out_ref, own_ref, __, full):
    sketch = kept_ref[...] + got_ref[...]
    groups, half, cols = sketch.shape
    flat = sketch.reshape(groups * half, cols)
    full[...] = lax.dot_general(
        flat, flat, (((0,), (0,)), ((), ())), precision=HIGHEST, preferred_element_type=F32
    ) * (1.0 / subjects)
    col = pos_ref[1]
    rows = out_ref.shape[0] // copies
    piece = full[pl.ds(pl.multiple_of(col * rows, rows), rows), :]
    for k in range(copies):
        out_ref[k * rows : (k + 1) * rows, :] = piece
    own_ref[...] = kept_ref[col] + got_ref[col]


def cholesky_kernel(block, cross_ref, own_ref, factor_ref, basis_ref, work):
    size = cross_ref.shape[0]
    mine = own_ref.shape[0]
    work[:, :size] = cross_ref[...]
    padded = jnp.concatenate([own_ref[...], jnp.zeros((128 - mine, size), F32)], axis=0)
    work[:, size:] = padded.T
    shape = (block, 128)
    row_id = lax.broadcasted_iota(jnp.int32, shape, 0)

    def spread(value):
        return jnp.broadcast_to(value, shape)

    for start in range(0, size, block):
        lane0 = start // 128 * 128
        chunks = [work[start : start + block, k : k + 128] for k in range(lane0, size + 128, 128)]
        first = start - lane0
        columns = [spread(chunks[0][:, first + j : first + j + 1]) for j in range(block)]
        scale = jnp.zeros(shape, F32)
        for i in range(block):
            pivot = spread(columns[i][i : i + 1, :])
            scale = jnp.where(row_id == i, lax.rsqrt(pivot), scale)
            if i < block - 1:
                weight = jnp.where(row_id > i, columns[i] * (1.0 / pivot), 0.0)
                for j in range(i + 1, block):
                    columns[j] = columns[j] - weight * spread(columns[j][i : i + 1, :])
                chunks = [c - weight * spread(c[i : i + 1, :]) for c in chunks]
        panel = jnp.concatenate([c * scale for c in chunks], axis=1)
        work[start : start + block, lane0:] = panel
        stop = start + block
        if stop < size:
            lane1 = stop // 128 * 128
            right = split_terms(panel[:, lane1 - lane0 :])
            left = [part[:, : size - lane1] for part in right]
            update = lax.dot_general(
                jnp.concatenate([left[k] for k in (0, 0, 1, 0, 2, 1)], axis=0),
                jnp.concatenate([right[k] for k in (0, 1, 0, 2, 0, 1)], axis=0),
                (((0,), (0,)), ((), ())),
                preferred_element_type=F32,
            )
            work[stop:, lane1:] = work[stop:, lane1:] - update[stop - lane1 :, :]
    square = (size, size)
    upper = lax.broadcasted_iota(jnp.int32, square, 0) <= lax.broadcasted_iota(jnp.int32, square, 1)
    factor_ref[...] = jnp.where(upper, work[:, :size], 0.0)
    basis_ref[...] = work[:, size:].T[:mine, :]


def gram_kernel(vox_total, own_ref, other_ref, col_own_ref, col_other_ref, means_ref, out_ref, done_ref, cols):
    half = own_ref.shape[1]

    @pl.when(pl.program_id(0) == 0)
    def _():
        for k, ref in enumerate((col_own_ref, col_other_ref)):
            mean = means_ref[k : k + 1, :]
            cols[:, k * half : (k + 1) * half] = (ref[...].astype(F32) - mean).astype(BF16)

    contract = (((1,), (1,)), ((), ()))
    tile = lax.dot_general(own_ref[...], cols[:, :half], contract, preferred_element_type=F32)
    tile += lax.dot_general(other_ref[...], cols[:, half:], contract, preferred_element_type=F32)
    tile = tile * (1.0 / vox_total)
    done_ref[...] = jnp.zeros(done_ref.shape, F32)
    rows = tile.shape[0]
    groups = tile.shape[1] // 128
    for a in range(groups):
        out_ref[pl.ds(a, rows, stride=groups), :] = tile[:, a * 128 : (a + 1) * 128]


def ring_gather(block, axis, size):
    ahead = [(i, (i + 1) % size) for i in range(size)]
    back = [(i, (i - 1) % size) for i in range(size)]
    found = [((0, 0), block)]
    up = down = block
    half = block.shape[0] // 2
    for k in range(1, size // 2):
        up = lax.ppermute(up, axis, ahead)
        down = lax.ppermute(down, axis, back)
        found += [((-k, 0), up), ((k, 0), down)]
    far = size // 2
    found += [((-far, 0), lax.ppermute(up[:half], axis, ahead))]
    found += [((far, half), lax.ppermute(down[half:], axis, back))]
    return found


def shards(maps, probes):
    sub_rows, vox_half = maps.shape
    width = probes.shape[1]
    row_count = lax.axis_size("row")
    col_count = lax.axis_size("col")
    vox_count = lax.axis_size("vox")
    subjects = sub_rows * row_count * col_count
    vox_total = vox_half * vox_count
    block_rows = sub_rows * col_count
    groups = row_count // vox_count
    col_pos = lax.axis_index("col")
    vox_pos = lax.axis_index("vox")
    pos = jnp.stack([vox_pos, col_pos, lax.axis_index("row")]).astype(jnp.int32)
    swap = [(0, 1), (1, 0)]

    def exchange(value, axis):
        return lax.all_to_all(value, axis, 0, 0, tiled=True)

    row_maps = lax.all_gather(maps, "col", axis=0, tiled=True)
    ring = ring_gather(maps, "row", row_count)
    group_shape = (groups, sub_rows, vox_half)
    whole_block = pl.BlockSpec(group_shape, lambda i, p: (0, 0, 0))
    col_kept, col_sent = pl.pallas_call(
        functools.partial(sort_kernel, [key for key, _ in ring]),
        grid_spec=pltpu.PrefetchScalarGridSpec(
            num_scalar_prefetch=1,
            grid=(1,),
            in_specs=[pl.BlockSpec(piece.shape, lambda i, p: (0, 0)) for _, piece in ring],
            out_specs=[whole_block, whole_block],
        ),
        out_shape=[sd(group_shape, BF16)] * 2,
        compiler_params=PARAMS,
    )(pos, *[piece for _, piece in ring])
    col_other = lax.ppermute(col_sent, "vox", swap)

    slice_rows = vox_half // col_count + PAD
    local = call(
        functools.partial(project_kernel, col_count),
        sd((col_count * slice_rows, width)),
        maps,
        probes,
    )
    part = call(
        functools.partial(sum_repeat_kernel, col_count, row_count),
        sd((row_count * slice_rows, width)),
        exchange(local, "col"),
        after=[piece for _, piece in ring[1:5]],
    )
    whole = call(
        functools.partial(centre_kernel, row_count, col_count, subjects),
        sd((col_count * slice_rows, width)),
        exchange(part, "row"),
    )
    weights = exchange(whole, "col")

    half_rows = sub_rows // vox_count
    step = 4 * sub_rows
    half_spec = pl.BlockSpec((step // sub_rows, half_rows, width), lambda i, p: (i, 0, 0))
    kept, sent, mean, centered = pl.pallas_call(
        functools.partial(sketch_kernel, col_count, vox_total),
        grid_spec=pltpu.PrefetchScalarGridSpec(
            num_scalar_prefetch=1,
            grid=(block_rows // step,),
            in_specs=[
                pl.BlockSpec((step, vox_half), lambda i, p: (i, 0)),
                pl.BlockSpec((col_count * slice_rows, width), lambda i, p: (0, 0)),
                pl.BlockSpec(memory_space=pl.ANY),
            ],
            out_specs=[
                half_spec,
                half_spec,
                pl.BlockSpec((1, vox_half), lambda i, p: (0, 0)),
                pl.BlockSpec((step, vox_half), lambda i, p: (i, 0)),
            ],
            scratch_shapes=[pltpu.VMEM((3, vox_half, width), BF16)],
        ),
        out_shape=[
            sd((col_count, half_rows, width)),
            sd((col_count, half_rows, width)),
            sd((1, vox_half)),
            sd((block_rows, vox_half), BF16),
        ],
        compiler_params=LARGE,
    )(pos, row_maps, weights, col_other)
    got = lax.ppermute(sent, "vox", swap)
    cross_rows = width // col_count
    copies = row_count * vox_count
    slices, own, centered = pl.pallas_call(
        functools.partial(cross_kernel, subjects, copies),
        grid_spec=pltpu.PrefetchScalarGridSpec(
            num_scalar_prefetch=1,
            grid=(1,),
            in_specs=[
                pl.BlockSpec((col_count, half_rows, width), lambda i, p: (0, 0, 0)),
                pl.BlockSpec((col_count, half_rows, width), lambda i, p: (0, 0, 0)),
                pl.BlockSpec(memory_space=pl.ANY),
            ],
            out_specs=[
                pl.BlockSpec((copies * cross_rows, width), lambda i, p: (0, 0)),
                pl.BlockSpec((half_rows, width), lambda i, p: (0, 0)),
                pl.BlockSpec(memory_space=pl.ANY),
            ],
            scratch_shapes=[pltpu.VMEM((width, width), F32)],
        ),
        out_shape=[
            sd((copies * cross_rows, width)),
            sd((half_rows, width)),
            sd((block_rows, vox_half), BF16),
        ],
        input_output_aliases={3: 2},
        compiler_params=PARAMS,
    )(pos, kept, got, centered)
    summed = call(
        functools.partial(sum_repeat_kernel, copies, col_count),
        sd((width, width)),
        exchange(slices, ("row", "vox")),
    )
    cross = exchange(summed, "col")
    other = lax.ppermute(centered, "vox", swap)
    means = jnp.concatenate([mean, lax.ppermute(mean, "vox", swap)], axis=0)
    own_cols = groups * sub_rows
    tall = 256
    gram, done = pl.pallas_call(
        functools.partial(gram_kernel, vox_total),
        grid=(block_rows // tall,),
        in_specs=[
            pl.BlockSpec((tall, vox_half), lambda i: (i, 0)),
            pl.BlockSpec((tall, vox_half), lambda i: (i, 0)),
            pl.BlockSpec((own_cols, vox_half), lambda i: (0, 0)),
            pl.BlockSpec((own_cols, vox_half), lambda i: (0, 0)),
            pl.BlockSpec((2, vox_half), lambda i: (0, 0)),
        ],
        out_specs=[
            pl.BlockSpec((tall * groups, 128), lambda i: (i, 0)),
            pl.BlockSpec((8, 128), lambda i: (0, 0)),
        ],
        out_shape=[sd((block_rows * groups, 128)), sd((8, 128))],
        scratch_shapes=[pltpu.VMEM((own_cols, vox_total), BF16)],
        compiler_params=PARAMS,
    )(
        centered,
        other,
        col_kept.reshape(own_cols, vox_half),
        col_other.reshape(own_cols, vox_half),
        means,
    )
    factor, basis = call(
        functools.partial(cholesky_kernel, 16),
        [sd((width, width)), sd((half_rows, width))],
        cross,
        own,
        after=[done],
        scratch_shapes=[pltpu.VMEM((width, width + 128), F32)],
    )
    return gram.reshape(block_rows, groups, 1, sub_rows), basis, factor


def solution(mesh):
    placed = (P(("row", "col"), "vox"), P(("row", "col"), None))
    return jax.shard_map(
        shards,
        mesh=mesh,
        in_specs=placed,
        out_specs=(P("row", "vox", "col", None), P(("row", "col", "vox"), None), P()),
        check_vma=False,
    )
```

time: 199 us -> 158 us (0.79)
  waiting for transfers between devices: 75.7 us -> 34.1 us
  Pallas kernels: 52 us -> 33.4 us
  starting transfers between devices: 35.5 us -> 48 us
  local copies, waits for them, and re-layouts: 5.54 us -> 9.71 us
    all_to_all x4, waiting for transfers between devices: 40.8 us -> 2.04 us  [exchange(): return lax.all_to_all(value, axis, 0, 0, tiled=True)]
    all_gather x1, waiting for transfers between devices: 29.8 us -> 0.01 us  [shards(): row_maps = lax.all_gather(maps, 'col', axis=0, tiled=True)]
    ppermute x2 -> x10, waiting for transfers between devices: 0.01 us -> 27.9 us  [the longest x3 25.5 us: ring_gather(): up = lax.ppermute(up, axis, ahead)]
    pallas_call x5 -> x6, Pallas kernels: 30 us -> 13.3 us  [the longest x5 12.4 us: call(): pl.pallas_call(body, out_shape=out_shape, in_specs=specs, compiler_params...]
    ppermute x2 -> x10, starting transfers between devices: 2.28 us -> 18 us  [the longest x3 7.93 us: ring_gather(): down = lax.ppermute(down, axis, back)]
    unnamed x4 -> x34, local copies, waits for them, and re-layouts: 1.78 us -> 9.69 us
    dynamic_slice x1 -> x0, local copies, waits for them, and re-layouts: 2.68 us -> none  [shards(): lax.dynamic_slice_in_dim(col_maps, (1 - vox_pos) * own_cols, own_cols, 0)]
    all_gather x1 -> x0, waiting for transfers between devices: 2.55 us -> none  [shards(): col_maps = lax.all_gather(maps, 'row', axis=0, tiled=True)]
  transfers between devices with their start and end apart: 10 -> 17, of which waited for: 6 -> 8; matrix products, arithmetic and copies ran while one was open for 2% -> 0% of each run, Pallas kernels for 21% -> 10%
where the time goes in v2:
time: 158 us; the launch traced here: 157 us
  starting transfers between devices  48 us (30%)
  waiting for transfers between devices  34.1 us (22%)
  Pallas kernels  33.4 us (21%)
  blocking collectives  17.1 us (11%)
  between operations  14.2 us (9%)
  local copies, waits for them, and re-layouts  9.71 us (6%)
    all_to_all x4, starting transfers between devices, exchange(): return lax.all_to_all(value, axis, 0, 0, tiled=True)  27.3 us
    ppermute x3, waiting for transfers between devices, ring_gather(): up = lax.ppermute(up, axis, ahead)  25.5 us
    all_to_all x1, blocking collectives, exchange(): return lax.all_to_all(value, axis, 0, 0, tiled=True)  17.1 us
    pallas_call x5, Pallas kernels, call(): pl.pallas_call(body, out_shape=out_shape, in_specs=specs, compiler_params...  12.4 us
    pallas_call x1, Pallas kernels, shards(): pl.pallas_call(functools.partial(gram_kernel, vox_total), grid=(block_row...  10.5 us
    unnamed x34, local copies, waits for them, and re-layouts  9.69 us
    ppermute x3, starting transfers between devices, ring_gather(): down = lax.ppermute(down, axis, back)  7.93 us
    pallas_call x1, Pallas kernels, shards(): pl.pallas_call(functools.partial(sketch_kernel, col_count, vox_total), gr...  7.9 us
  transfers between devices with their start and end apart: 17, of which 8 were waited for; matrix products, arithmetic and copies ran while one was open for 0% of the time, Pallas kernels for 10%

profile of v2, /device:TPU:1, one launch (start us, length us, event | category | flops | bytes accessed | tf_op | source)
XLA Modules:
  0.0 156.6 jit_solution(12494738610232779190)
XLA Ops:
  9.7 1.3 shard_map.49
  11.0 7.6 %all-to-all-start = ((f32[16,72,256]{2,1,0:T(8,128)}), f32[16,72,256]{2,1,0:T(8,128)S(1)}, u32[]{:S(2)}, u32[]{:S(2)}) async-start(f32[16,72,256]{2,1,0:T(8,128)} %bitcast.3), calls=%async_computation | async-start | bytes 2359296 | tf_op jit(solution)/shard_map/all_to_all | solution.py:254
  18.6 1.7 %collective-permute-start = (bf16[128,1024]{1,0:T(8,128)(2,1)}, bf16[128,1024]{1,0:T(8,128)(2,1)S(1)}, u32[]{:S(2)}, u32[]{:S(2)}) collective-permute-start(bf16[128,1024]{1,0:T(8,128)(2,1)} %refs_0_.3), channel_id=1, source_target_pairs={{0,32},{32,64},{64,96},{96,128},{128,160},{160,192},{192,224},{224... | collective-permute-start | bytes 786440 | tf_op jit(solution)/shard_map/ppermute | solution.py:229
  20.3 4.0 %collective-permute-start.1 = (bf16[128,1024]{1,0:T(8,128)(2,1)}, bf16[128,1024]{1,0:T(8,128)(2,1)S(1)}, u32[]{:S(2)}, u32[]{:S(2)}) collective-permute-start(bf16[128,1024]{1,0:T(8,128)(2,1)} %refs_0_.3), channel_id=1, source_target_pairs={{0,224},{32,0},{64,32},{96,64},{128,96},{160,128},{192,160},{224,1... | collective-permute-start | bytes 786440 | tf_op jit(solution)/shard_map/ppermute | solution.py:230
  24.4 5.8 %collective-permute-done.refs_1_ = bf16[128,1024]{1,0:T(8,128)(2,1)S(1)} collective-permute-done((bf16[128,1024]{1,0:T(8,128)(2,1)}, bf16[128,1024]{1,0:T(8,128)(2,1)S(1)}, u32[]{:S(2)}, u32[]{:S(2)}) %collective-permute-start) | collective-permute-done | bytes 262176 | tf_op jit(solution)/shard_map/ppermute | solution.py:229
  30.2 2.7 %collective-permute-start.3 = (bf16[128,1024]{1,0:T(8,128)(2,1)S(1)}, bf16[128,1024]{1,0:T(8,128)(2,1)S(1)}, u32[]{:S(2)}, u32[]{:S(2)}) collective-permute-start(bf16[128,1024]{1,0:T(8,128)(2,1)S(1)} %collective-permute-done.1.refs_2_), channel_id=1, source_target_pairs={{0,224},{32,0},{64,32},{96,64},{128,96},{160,128},{192,160},{224,1... | collective-permute-start | bytes 786440 | tf_op jit(solution)/shard_map/ppermute | solution.py:230
  32.9 4.9 %collective-permute-done.2.refs_3_ = bf16[128,1024]{1,0:T(8,128)(2,1)S(1)} collective-permute-done((bf16[128,1024]{1,0:T(8,128)(2,1)S(1)}, bf16[128,1024]{1,0:T(8,128)(2,1)S(1)}, u32[]{:S(2)}, u32[]{:S(2)}) %collective-permute-start.2) | collective-permute-done | bytes 262176 | tf_op jit(solution)/shard_map/ppermute | solution.py:229
  38.7 6.3 %all-to-all-start.1 = ((f32[8,72,256]{2,1,0:T(8,128)}), f32[8,72,256]{2,1,0:T(8,128)S(1)}, u32[]{:S(2)}, u32[]{:S(2)}) async-start(f32[8,72,256]{2,1,0:T(8,128)} %bitcast.5), calls=%async_computation.1 | async-start | bytes 1179648 | tf_op jit(solution)/shard_map/all_to_all | solution.py:254
  45.0 1.5 collective-permute-start.4
  46.5 1.2 collective-permute-start.5
  47.7 14.8 %collective-permute-done.4.refs_5_ = bf16[128,1024]{1,0:T(8,128)(2,1)S(1)} collective-permute-done((bf16[128,1024]{1,0:T(8,128)(2,1)S(1)}, bf16[128,1024]{1,0:T(8,128)(2,1)S(1)}, u32[]{:S(2)}, u32[]{:S(2)}) %collective-permute-start.4) | collective-permute-done | bytes 262176 | tf_op jit(solution)/shard_map/ppermute | solution.py:229
  62.7 2.6 %collective-permute-start.7 = (bf16[64,1024]{1,0:T(8,128)(2,1)S(1)}, bf16[64,1024]{1,0:T(8,128)(2,1)S(1)}, u32[]{:S(2)}, u32[]{:S(2)}) collective-permute-start(bf16[64,1024]{1,0:T(8,128)(2,1)S(1)} %slice.9), channel_id=1, source_target_pairs={{0,224},{32,0},{64,32},{96,64},{128,96},{160,128},{192,160},{224,1... | collective-permute-start | bytes 393224 | tf_op jit(solution)/shard_map/ppermute | solution.py:234
  66.6 9.8 %all-to-all-start.2 = ((f32[16,72,256]{2,1,0:T(8,128)}), f32[16,72,256]{2,1,0:T(8,128)S(1)}, u32[]{:S(2)}, u32[]{:S(2)}) async-start(f32[16,72,256]{2,1,0:T(8,128)} %bitcast.7), calls=%async_computation.2 | async-start | bytes 2359296 | tf_op jit(solution)/shard_map/all_to_all | solution.py:254
  85.2 2.6 %collective-permute-start.8 = (bf16[4,128,1024]{2,1,0:T(8,128)(2,1)S(1)}, bf16[4,128,1024]{2,1,0:T(8,128)(2,1)S(1)}, u32[]{:S(2)}, u32[]{:S(2)}) collective-permute-start(bf16[4,128,1024]{2,1,0:T(8,128)(2,1)S(1)} %get-tuple-element.16), channel_id=1, source_target_pairs={{0,1},{1,0},{2,3},{3,2},{4,5},{5,4},{6,7},{7,6},{8,9},{9,8},{10,11... | collective-permute-start | bytes 3145736 | tf_op jit(solution)/shard_map/ppermute | solution.py:271
  87.8 2.3 %collective-permute-done.8._ = bf16[4,128,1024]{2,1,0:T(8,128)(2,1)S(1)} collective-permute-done((bf16[4,128,1024]{2,1,0:T(8,128)(2,1)S(1)}, bf16[4,128,1024]{2,1,0:T(8,128)(2,1)S(1)}, u32[]{:S(2)}, u32[]{:S(2)}) %collective-permute-start.8) | collective-permute-done | bytes 1048608 | tf_op jit(solution)/shard_map/ppermute | solution.py:271
  90.1 2.0 %all-to-all-done.2 = f32[16,72,256]{2,1,0:T(8,128)S(1)} async-done(((f32[16,72,256]{2,1,0:T(8,128)}), f32[16,72,256]{2,1,0:T(8,128)S(1)}, u32[]{:S(2)}, u32[]{:S(2)}) %all-to-all-start.2) | async-done | bytes 1179680 | tf_op jit(solution)/shard_map/all_to_all | solution.py:254
  92.1 7.9 %shard_map.53 = (f32[16,64,256]{2,1,0:T(8,128)S(1)}, f32[16,64,256]{2,1,0:T(8,128)S(1)}, f32[1,1024]{1,0:T(1,128)S(1)}, bf16[2048,1024]{1,0:T(8,128)(2,1)}) custom-call(s32[3]{0:T(128)S(1)} %pad_add_fusion.pos_ref, bf16[2048,1024]{1,0:T(8,128)(2,1)} %all-gather.2.cloned.1.call-done.maps_ref, f32[1152,256]{1,0:T(8,128)S(1)} %bitcast.18, ...), custom_call_target="tpu_custom_call" | custom-call | tf_op jit(solution)/shard_map/pallas_call | solution.py:296
  100.0 3.7 %collective-permute-start.9 = (f32[16,64,256]{2,1,0:T(8,128)S(1)}, f32[16,64,256]{2,1,0:T(8,128)S(1)}, u32[]{:S(2)}, u32[]{:S(2)}) collective-permute-start(f32[16,64,256]{2,1,0:T(8,128)S(1)} %get-tuple-element.18), channel_id=1, source_target_pairs={{0,1},{1,0},{2,3},{3,2},{4,5},{5,4},{6,7},{7,6},{8,9},{9,8},{10,11... | collective-permute-start | bytes 3145736 | tf_op jit(solution)/shard_map/ppermute | solution.py:322
  103.7 2.3 %collective-permute-done.9.got_ref = f32[16,64,256]{2,1,0:T(8,128)S(1)} collective-permute-done((f32[16,64,256]{2,1,0:T(8,128)S(1)}, f32[16,64,256]{2,1,0:T(8,128)S(1)}, u32[]{:S(2)}, u32[]{:S(2)}) %collective-permute-start.9) | collective-permute-done | bytes 1048608 | tf_op jit(solution)/shard_map/ppermute | solution.py:322
  106.0 1.7 %shard_map.54 = (f32[256,256]{1,0:T(8,128)S(1)}, f32[64,256]{1,0:T(8,128)S(1)}, bf16[2048,1024]{1,0:T(8,128)(2,1)}) custom-call(s32[3]{0:T(128)S(1)} %pad_add_fusion.pos_ref, f32[16,64,256]{2,1,0:T(8,128)S(1)} %get-tuple-element.17.kept_ref, f32[16,64,256]{2,1,0:T(8,128)S(1)} %collective-permute-done.9.got_ref, ...), custom_call_target="tpu_custom_call", output_to_operand_aliasing={{2}: (3, {})} | custom-call | tf_op jit(solution)/shard_map/pallas_call | solution.py:325
  108.2 17.1 %all_to_all.55 = f32[16,16,256]{2,1,0:T(8,128)S(1)} all-to-all(f32[16,16,256]{2,1,0:T(8,128)S(1)} %bitcast.25), channel_id=1, replica_groups=mesh['row'=8,'col'=16,'vox'=2] {'row','vox'}, dimensions={0} | all-to-all | bytes 524288 | tf_op jit(solution)/shard_map/all_to_all | solution.py:254
  126.1 3.5 %all-to-all-start.4 = ((f32[16,16,256]{2,1,0:T(8,128)}), f32[16,16,256]{2,1,0:T(8,128)S(1)}, u32[]{:S(2)}, u32[]{:S(2)}) async-start(f32[16,16,256]{2,1,0:T(8,128)} %bitcast.15), calls=%async_computation.4 | async-start | bytes 524288 | tf_op jit(solution)/shard_map/all_to_all | solution.py:254
  130.9 10.5 %shard_map.55 = (f32[8192,128]{1,0:T(8,128)}, f32[8,128]{1,0:T(8,128)S(1)}) custom-call(bf16[2048,1024]{1,0:T(8,128)(2,1)} %get-tuple-element.20.own_ref, bf16[2048,1024]{1,0:T(8,128)(2,1)} %collective-permute-done.10.other_ref, bf16[512,1024]{1,0:T(8,128)(2,1)S(1)} %bitcast.22, bf16[512,1024]{1,0:T(8,128)(2,1)S(1)} %bitcast.20, ...), custom_call_target="tpu_custom_call" | custom-call | tf_op jit(solution)/shard_map/pallas_call | solution.py:360
  141.4 8.3 %shard_map.57 = (f32[256,256]{1,0:T(8,128)}, f32[64,256]{1,0:T(8,128)}) custom-call(f32[256,256]{1,0:T(8,128)S(1)} %bitcast.23, f32[64,256]{1,0:T(8,128)S(1)} %get-tuple-element.25.refs_1_, f32[8,128]{1,0:T(8,128)S(1)} %get-tuple-element.26.refs_2_), custom_call_target="tpu_custom_call" | custom-call | tf_op jit(solution)/shard_map/pallas_call | solution.py:26
  (59 shorter events, 16.1 us)
Async XLA Ops:
  7.2 85.0 %all-gather.2.cloned.1.call-start = ((), (), s32[]{:S(2)}) async-start(), calls=%async_computation.5 | async-start | bytes 4456448 | tf_op jit(solution)/shard_map/all_gather | solution.py:256
  7.9 1.0 copy-start
  11.0 26.7 %all-to-all-start = ((f32[16,72,256]{2,1,0:T(8,128)}), f32[16,72,256]{2,1,0:T(8,128)S(1)}, u32[]{:S(2)}, u32[]{:S(2)}) async-start(f32[16,72,256]{2,1,0:T(8,128)} %bitcast.3), calls=%async_computation | async-start | bytes 2359296 | tf_op jit(solution)/shard_map/all_to_all | solution.py:254
  18.6 11.6 %collective-permute-start = (bf16[128,1024]{1,0:T(8,128)(2,1)}, bf16[128,1024]{1,0:T(8,128)(2,1)S(1)}, u32[]{:S(2)}, u32[]{:S(2)}) collective-permute-start(bf16[128,1024]{1,0:T(8,128)(2,1)} %refs_0_.3), channel_id=1, source_target_pairs={{0,32},{32,64},{64,96},{96,128},{128,160},{160,192},{192,224},{224... | collective-permute-start | bytes 786440 | tf_op jit(solution)/shard_map/ppermute | solution.py:229
  20.3 9.9 %collective-permute-start.1 = (bf16[128,1024]{1,0:T(8,128)(2,1)}, bf16[128,1024]{1,0:T(8,128)(2,1)S(1)}, u32[]{:S(2)}, u32[]{:S(2)}) collective-permute-start(bf16[128,1024]{1,0:T(8,128)(2,1)} %refs_0_.3), channel_id=1, source_target_pairs={{0,224},{32,0},{64,32},{96,64},{128,96},{160,128},{192,160},{224,1... | collective-permute-start | bytes 786440 | tf_op jit(solution)/shard_map/ppermute | solution.py:230
  30.2 36.3 %copy-start.2 = (bf16[128,1024]{1,0:T(8,128)(2,1)}, bf16[128,1024]{1,0:T(8,128)(2,1)S(1)}, u32[]{:S(2)}) copy-start(bf16[128,1024]{1,0:T(8,128)(2,1)S(1)} %collective-permute-done.refs_1_) | copy-start | bytes 786436
  30.2 7.6 %collective-permute-start.2 = (bf16[128,1024]{1,0:T(8,128)(2,1)S(1)}, bf16[128,1024]{1,0:T(8,128)(2,1)S(1)}, u32[]{:S(2)}, u32[]{:S(2)}) collective-permute-start(bf16[128,1024]{1,0:T(8,128)(2,1)S(1)} %collective-permute-done.refs_1_), channel_id=1, source_target_pairs={{0,32},{32,64},{64,96},{96,128},{128,160},{160,192},{192,224},{224... | collective-permute-start | bytes 786440 | tf_op jit(solution)/shard_map/ppermute | solution.py:229
  30.2 36.3 %copy-start.4 = (bf16[128,1024]{1,0:T(8,128)(2,1)}, bf16[128,1024]{1,0:T(8,128)(2,1)S(1)}, u32[]{:S(2)}) copy-start(bf16[128,1024]{1,0:T(8,128)(2,1)S(1)} %collective-permute-done.1.refs_2_) | copy-start | bytes 786436
  30.2 7.5 %collective-permute-start.3 = (bf16[128,1024]{1,0:T(8,128)(2,1)S(1)}, bf16[128,1024]{1,0:T(8,128)(2,1)S(1)}, u32[]{:S(2)}, u32[]{:S(2)}) collective-permute-start(bf16[128,1024]{1,0:T(8,128)(2,1)S(1)} %collective-permute-done.1.refs_2_), channel_id=1, source_target_pairs={{0,224},{32,0},{64,32},{96,64},{128,96},{160,128},{192,160},{224,1... | collective-permute-start | bytes 786440 | tf_op jit(solution)/shard_map/ppermute | solution.py:230
  37.8 28.8 %copy-start.6 = (bf16[128,1024]{1,0:T(8,128)(2,1)}, bf16[128,1024]{1,0:T(8,128)(2,1)S(1)}, u32[]{:S(2)}) copy-start(bf16[128,1024]{1,0:T(8,128)(2,1)S(1)} %collective-permute-done.2.refs_3_) | copy-start | bytes 786436
  37.8 28.8 %copy-start.8 = (bf16[128,1024]{1,0:T(8,128)(2,1)}, bf16[128,1024]{1,0:T(8,128)(2,1)S(1)}, u32[]{:S(2)}) copy-start(bf16[128,1024]{1,0:T(8,128)(2,1)S(1)} %collective-permute-done.3.refs_4_) | copy-start | bytes 786436
  37.8 40.0 %copy-start.1 = (bf16[128,1024]{1,0:T(8,128)(2,1)S(1)}, bf16[128,1024]{1,0:T(8,128)(2,1)}, u32[]{:S(2)}) copy-start(bf16[128,1024]{1,0:T(8,128)(2,1)} %refs_0_.3) | copy-start | bytes 786436
  38.7 26.7 %all-to-all-start.1 = ((f32[8,72,256]{2,1,0:T(8,128)}), f32[8,72,256]{2,1,0:T(8,128)S(1)}, u32[]{:S(2)}, u32[]{:S(2)}) async-start(f32[8,72,256]{2,1,0:T(8,128)} %bitcast.5), calls=%async_computation.1 | async-start | bytes 1179648 | tf_op jit(solution)/shard_map/all_to_all | solution.py:254
  45.0 17.5 %collective-permute-start.4 = (bf16[128,1024]{1,0:T(8,128)(2,1)S(1)}, bf16[128,1024]{1,0:T(8,128)(2,1)S(1)}, u32[]{:S(2)}, u32[]{:S(2)}) collective-permute-start(bf16[128,1024]{1,0:T(8,128)(2,1)S(1)} %collective-permute-done.2.refs_3_), channel_id=1, source_target_pairs={{0,32},{32,64},{64,96},{96,128},{128,160},{160,192},{192,224},{224... | collective-permute-start | bytes 786440 | tf_op jit(solution)/shard_map/ppermute | solution.py:229
  46.5 16.2 %collective-permute-start.5 = (bf16[128,1024]{1,0:T(8,128)(2,1)S(1)}, bf16[128,1024]{1,0:T(8,128)(2,1)S(1)}, u32[]{:S(2)}, u32[]{:S(2)}) collective-permute-start(bf16[128,1024]{1,0:T(8,128)(2,1)S(1)} %collective-permute-done.3.refs_4_), channel_id=1, source_target_pairs={{0,224},{32,0},{64,32},{96,64},{128,96},{160,128},{192,160},{224,1... | collective-permute-start | bytes 786440 | tf_op jit(solution)/shard_map/ppermute | solution.py:230
  62.5 14.0 %collective-permute-start.6 = (bf16[64,1024]{1,0:T(8,128)(2,1)S(1)}, bf16[64,1024]{1,0:T(8,128)(2,1)S(1)}, u32[]{:S(2)}, u32[]{:S(2)}) collective-permute-start(bf16[64,1024]{1,0:T(8,128)(2,1)S(1)} %slice.8), channel_id=1, source_target_pairs={{0,32},{32,64},{64,96},{96,128},{128,160},{160,192},{192,224},{224... | collective-permute-start | bytes 393224 | tf_op jit(solution)/shard_map/ppermute | solution.py:233
  62.7 3.9 %copy-start.10 = (bf16[128,1024]{1,0:T(8,128)(2,1)}, bf16[128,1024]{1,0:T(8,128)(2,1)S(1)}, u32[]{:S(2)}) copy-start(bf16[128,1024]{1,0:T(8,128)(2,1)S(1)} %collective-permute-done.5.refs_6_) | copy-start | bytes 786436
  62.7 14.4 %collective-permute-start.7 = (bf16[64,1024]{1,0:T(8,128)(2,1)S(1)}, bf16[64,1024]{1,0:T(8,128)(2,1)S(1)}, u32[]{:S(2)}, u32[]{:S(2)}) collective-permute-start(bf16[64,1024]{1,0:T(8,128)(2,1)S(1)} %slice.9), channel_id=1, source_target_pairs={{0,224},{32,0},{64,32},{96,64},{128,96},{160,128},{192,160},{224,1... | collective-permute-start | bytes 393224 | tf_op jit(solution)/shard_map/ppermute | solution.py:234
  66.6 25.6 %all-to-all-start.2 = ((f32[16,72,256]{2,1,0:T(8,128)}), f32[16,72,256]{2,1,0:T(8,128)S(1)}, u32[]{:S(2)}, u32[]{:S(2)}) async-start(f32[16,72,256]{2,1,0:T(8,128)} %bitcast.7), calls=%async_computation.2 | async-start | bytes 2359296 | tf_op jit(solution)/shard_map/all_to_all | solution.py:254
  85.2 4.9 %collective-permute-start.8 = (bf16[4,128,1024]{2,1,0:T(8,128)(2,1)S(1)}, bf16[4,128,1024]{2,1,0:T(8,128)(2,1)S(1)}, u32[]{:S(2)}, u32[]{:S(2)}) collective-permute-start(bf16[4,128,1024]{2,1,0:T(8,128)(2,1)S(1)} %get-tuple-element.16), channel_id=1, source_target_pairs={{0,1},{1,0},{2,3},{3,2},{4,5},{5,4},{6,7},{7,6},{8,9},{9,8},{10,11... | collective-permute-start | bytes 3145736 | tf_op jit(solution)/shard_map/ppermute | solution.py:271
  100.0 6.0 %collective-permute-start.9 = (f32[16,64,256]{2,1,0:T(8,128)S(1)}, f32[16,64,256]{2,1,0:T(8,128)S(1)}, u32[]{:S(2)}, u32[]{:S(2)}) collective-permute-start(f32[16,64,256]{2,1,0:T(8,128)S(1)} %get-tuple-element.18), channel_id=1, source_target_pairs={{0,1},{1,0},{2,3},{3,2},{4,5},{5,4},{6,7},{7,6},{8,9},{9,8},{10,11... | collective-permute-start | bytes 3145736 | tf_op jit(solution)/shard_map/ppermute | solution.py:322
  107.8 23.1 %collective-permute-start.10 = (bf16[2048,1024]{1,0:T(8,128)(2,1)}, bf16[2048,1024]{1,0:T(8,128)(2,1)}, u32[]{:S(2)}, u32[]{:S(2)}) collective-permute-start(bf16[2048,1024]{1,0:T(8,128)(2,1)} %get-tuple-element.20.own_ref), channel_id=1, source_target_pairs={{0,1},{1,0},{2,3},{3,2},{4,5},{5,4},{6,7},{7,6},{8,9},{9,8},{10,11... | collective-permute-start | bytes 12582920 | tf_op jit(solution)/shard_map/ppermute | solution.py:356
  126.1 15.3 %all-to-all-start.4 = ((f32[16,16,256]{2,1,0:T(8,128)}), f32[16,16,256]{2,1,0:T(8,128)S(1)}, u32[]{:S(2)}, u32[]{:S(2)}) async-start(f32[16,16,256]{2,1,0:T(8,128)} %bitcast.15), calls=%async_computation.4 | async-start | bytes 524288 | tf_op jit(solution)/shard_map/all_to_all | solution.py:254
  129.6 1.3 collective-permute-start.11
  (10 other events, 8.7 us)
Sparse Core Ops, SparseCore 0:
  10.4 64.3 all-gather.1

commit v3 on v2

--- a/solution.py
+++ b/solution.py
@@ -13,28 +13,44 @@
 PAD = 8
 PARAMS = pltpu.CompilerParams(vmem_limit_bytes=24 * 1024 * 1024)
 LARGE = pltpu.CompilerParams(vmem_limit_bytes=48 * 1024 * 1024)
-
-
-def call(kernel, out_shape, *args, after=(), **kw):
-    count = len(args)
+ALL = pltpu.CompilerParams(vmem_limit_bytes=58 * 1024 * 1024)
+
+
+def call(kernel, out_shape, *args, after=(), carry=(), params=PARAMS, **kw):
+    count, outs = len(args), len(out_shape)
+    others = len(after) + len(carry)
 
     def body(*refs):
-        kernel(*refs[:count], *refs[count + len(after) :])
-
-    specs = [pl.BlockSpec(memory_space=pltpu.VMEM)] * count
-    specs += [pl.BlockSpec(memory_space=pl.ANY)] * len(after)
+        kernel(*refs[:count], *refs[count + others :][:outs], *refs[count + others + outs + len(carry) :])
+
+    anywhere = pl.BlockSpec(memory_space=pl.ANY)
+    vmem = pl.BlockSpec(memory_space=pltpu.VMEM)
     return pl.pallas_call(
-        body, out_shape=out_shape, in_specs=specs, compiler_params=PARAMS, **kw
-    )(*args, *after)
+        body,
+        out_shape=[*out_shape, *[sd(x.shape, x.dtype) for x in carry]],
+        in_specs=kw.pop("in_specs", [vmem] * count) + [anywhere] * others,
+        out_specs=[vmem] * outs + [anywhere] * len(carry),
+        input_output_aliases={count + len(after) + k: outs + k for k in range(len(carry))},
+        compiler_params=params,
+        **kw,
+    )(*args, *after, *carry)
 
 
 def sd(shape, dtype=F32):
     return jax.ShapeDtypeStruct(shape, dtype)
 
 
-def project_kernel(pieces, maps_ref, probes_ref, out_ref):
-    maps = maps_ref[...]
-    probes = probes_ref[...]
+def project_kernel(pieces, maps_ref, probes_ref, out_ref, maps_in, probes_in, arrived):
+    copies = [
+        pltpu.make_async_copy(maps_ref, maps_in, arrived.at[0]),
+        pltpu.make_async_copy(probes_ref, probes_in, arrived.at[1]),
+    ]
+    for copy in copies:
+        copy.start()
+    for copy in copies:
+        copy.wait()
+    maps = maps_in[...]
+    probes = probes_in[...]
     vox, cols = maps.shape[1], probes.shape[1]
     width = vox // pieces
     sums = jnp.sum(maps.astype(F32), axis=0, keepdims=True)
@@ -120,22 +136,29 @@
 
 
 def sort_kernel(shifts, pos_ref, *refs):
-    pieces, kept_ref, sent_ref = refs[:-2], refs[-2], refs[-1]
+    count = len(shifts)
+    pieces, (kept_ref, sent_ref, arrived) = refs[:count], refs[count:]
     groups = kept_ref.shape[0]
     total = 2 * groups
-    for (shift, start), piece in zip(shifts, pieces):
+    for k, ((shift, start), piece) in enumerate(zip(shifts, pieces)):
         group = lax.rem(pos_ref[2] + (shift + total), total)
         mine = group // groups == pos_ref[0]
         place = lax.rem(group, groups)
-        stop = start + piece.shape[0]
+        rows = piece.shape[0]
 
         @pl.when(mine)
-        def _(piece=piece, place=place, start=start, stop=stop):
-            kept_ref[place, start:stop, :] = piece[...]
+        def _(k=k, piece=piece, place=place, start=start, rows=rows):
+            target = kept_ref.at[place, pl.ds(start, rows)]
+            pltpu.make_async_copy(piece, target, arrived.at[k]).start()
 
         @pl.when(jnp.logical_not(mine))
-        def _(piece=piece, place=place, start=start, stop=stop):
-            sent_ref[place, start:stop, :] = piece[...]
+        def _(k=k, piece=piece, place=place, start=start, rows=rows):
+            target = sent_ref.at[place, pl.ds(start, rows)]
+            pltpu.make_async_copy(piece, target, arrived.at[k]).start()
+
+    for k, ((_, start), piece) in enumerate(zip(shifts, pieces)):
+        target = kept_ref.at[0, pl.ds(start, piece.shape[0])]
+        pltpu.make_async_copy(piece, target, arrived.at[k]).wait()
 
 
 def cross_kernel(subjects, copies, pos_ref, kept_ref, got_ref, _, out_ref, own_ref, __, full):
@@ -199,7 +222,7 @@
     basis_ref[...] = work[:, size:].T[:mine, :]
 
 
-def gram_kernel(vox_total, own_ref, other_ref, col_own_ref, col_other_ref, means_ref, out_ref, done_ref, cols):
+def gram_kernel(vox_total, own_ref, other_ref, col_own_ref, col_other_ref, means_ref, _, out_ref, done_ref, cols):
     half = own_ref.shape[1]
 
     @pl.when(pl.program_id(0) == 0)
@@ -219,20 +242,38 @@
         out_ref[pl.ds(a, rows, stride=groups), :] = tile[:, a * 128 : (a + 1) * 128]
 
 
-def ring_gather(block, axis, size):
-    ahead = [(i, (i + 1) % size) for i in range(size)]
-    back = [(i, (i - 1) % size) for i in range(size)]
-    found = [((0, 0), block)]
-    up = down = block
-    half = block.shape[0] // 2
-    for k in range(1, size // 2):
-        up = lax.ppermute(up, axis, ahead)
-        down = lax.ppermute(down, axis, back)
-        found += [((-k, 0), up), ((k, 0), down)]
-    far = size // 2
-    found += [((-far, 0), lax.ppermute(up[:half], axis, ahead))]
-    found += [((far, half), lax.ppermute(down[half:], axis, back))]
-    return found
+def gram_part(vox_total, groups, part, before, own, other, col_own, col_other, means):
+    rows, vox_half = own.shape
+    tall = min(512, rows // 2)
+    steps = rows // tall // 2
+    row_spec = pl.BlockSpec((tall, vox_half), lambda i: (i + part * steps, 0))
+    col_spec = pl.BlockSpec(col_own.shape, lambda i: (0, 0))
+    return pl.pallas_call(
+        functools.partial(gram_kernel, vox_total),
+        grid=(steps,),
+        in_specs=[
+            row_spec,
+            row_spec,
+            col_spec,
+            col_spec,
+            pl.BlockSpec(means.shape, lambda i: (0, 0)),
+            pl.BlockSpec(memory_space=pl.ANY),
+        ],
+        out_specs=[
+            pl.BlockSpec((tall * groups, 128), lambda i: (i + part * steps, 0)),
+            pl.BlockSpec((8, 128), lambda i: (0, 0)),
+        ],
+        out_shape=[sd((rows * groups, 128)), sd((8, 128))],
+        scratch_shapes=[pltpu.VMEM((col_own.shape[0], vox_total), BF16)],
+        input_output_aliases={} if before is None else {5: 0},
+        compiler_params=LARGE,
+    )(own, other, col_own, col_other, means, means if before is None else before)
+
+
+def ring_step(up, down, axis, size, hops=1):
+    ahead = [(i, (i + hops) % size) for i in range(size)]
+    back = [(i, (i - hops) % size) for i in range(size)]
+    return lax.ppermute(up, axis, ahead), lax.ppermute(down, axis, back)
 
 
 def shards(maps, probes):
@@ -254,44 +295,63 @@
         return lax.all_to_all(value, axis, 0, 0, tiled=True)
 
     row_maps = lax.all_gather(maps, "col", axis=0, tiled=True)
-    ring = ring_gather(maps, "row", row_count)
+    slice_rows = vox_half // col_count + PAD
+    up, down = ring_step(maps, maps, "row", row_count)
+    ring = [((0, 0), maps), ((-1, 0), up), ((1, 0), down)]
+    up, down = ring_step(up, down, "row", row_count)
+    (local,) = call(
+        functools.partial(project_kernel, col_count),
+        [sd((col_count * slice_rows, width))],
+        maps,
+        probes,
+        in_specs=[pl.BlockSpec(memory_space=pl.ANY)] * 2,
+        params=ALL,
+        scratch_shapes=[
+            pltpu.VMEM(maps.shape, BF16),
+            pltpu.VMEM(probes.shape, BF16),
+            pltpu.SemaphoreType.DMA((2,)),
+        ],
+    )
+    (part,) = call(
+        functools.partial(sum_repeat_kernel, col_count, row_count),
+        [sd((row_count * slice_rows, width))],
+        exchange(local, "col"),
+        after=[up, down],
+    )
+    whole, up, down = call(
+        functools.partial(centre_kernel, row_count, col_count, subjects),
+        [sd((col_count * slice_rows, width))],
+        exchange(part, "row"),
+        carry=[up, down],
+    )
+    weights = exchange(whole, "col")
+    ring += [((-2, 0), up), ((2, 0), down)]
+    half_block = sub_rows // 2
+    for k in range(3, row_count // 2):
+        ahead, back = ring_step(up, down, "row", row_count, k - 2)
+        ring += [((-k, 0), ahead), ((k, 0), back)]
+    far = row_count // 2
+    ahead, back = ring_step(up[:half_block], down[half_block:], "row", row_count, far - 2)
+    ring += [((-far, 0), ahead), ((far, half_block), back)]
     group_shape = (groups, sub_rows, vox_half)
-    whole_block = pl.BlockSpec(group_shape, lambda i, p: (0, 0, 0))
+    anywhere = pl.BlockSpec(memory_space=pl.ANY)
     col_kept, col_sent = pl.pallas_call(
         functools.partial(sort_kernel, [key for key, _ in ring]),
         grid_spec=pltpu.PrefetchScalarGridSpec(
             num_scalar_prefetch=1,
             grid=(1,),
-            in_specs=[pl.BlockSpec(piece.shape, lambda i, p: (0, 0)) for _, piece in ring],
-            out_specs=[whole_block, whole_block],
+            in_specs=[anywhere] * len(ring),
+            out_specs=[anywhere] * 2,
+            scratch_shapes=[pltpu.SemaphoreType.DMA((len(ring),))],
         ),
         out_shape=[sd(group_shape, BF16)] * 2,
-        compiler_params=PARAMS,
+        cost_estimate=pl.CostEstimate(flops=0, bytes_accessed=1024, transcendentals=0),
+        compiler_params=ALL,
     )(pos, *[piece for _, piece in ring])
     col_other = lax.ppermute(col_sent, "vox", swap)
 
-    slice_rows = vox_half // col_count + PAD
-    local = call(
-        functools.partial(project_kernel, col_count),
-        sd((col_count * slice_rows, width)),
-        maps,
-        probes,
-    )
-    part = call(
-        functools.partial(sum_repeat_kernel, col_count, row_count),
-        sd((row_count * slice_rows, width)),
-        exchange(local, "col"),
-        after=[piece for _, piece in ring[1:5]],
-    )
-    whole = call(
-        functools.partial(centre_kernel, row_count, col_count, subjects),
-        sd((col_count * slice_rows, width)),
-        exchange(part, "row"),
-    )
-    weights = exchange(whole, "col")
-
     half_rows = sub_rows // vox_count
-    step = 4 * sub_rows
+    step = min(4 * sub_rows, block_rows)
     half_spec = pl.BlockSpec((step // sub_rows, half_rows, width), lambda i, p: (i, 0, 0))
     kept, sent, mean, centered = pl.pallas_call(
         functools.partial(sketch_kernel, col_count, vox_total),
@@ -347,46 +407,26 @@
         input_output_aliases={3: 2},
         compiler_params=PARAMS,
     )(pos, kept, got, centered)
-    summed = call(
-        functools.partial(sum_repeat_kernel, copies, col_count),
-        sd((width, width)),
-        exchange(slices, ("row", "vox")),
-    )
-    cross = exchange(summed, "col")
     other = lax.ppermute(centered, "vox", swap)
     means = jnp.concatenate([mean, lax.ppermute(mean, "vox", swap)], axis=0)
     own_cols = groups * sub_rows
-    tall = 256
-    gram, done = pl.pallas_call(
-        functools.partial(gram_kernel, vox_total),
-        grid=(block_rows // tall,),
-        in_specs=[
-            pl.BlockSpec((tall, vox_half), lambda i: (i, 0)),
-            pl.BlockSpec((tall, vox_half), lambda i: (i, 0)),
-            pl.BlockSpec((own_cols, vox_half), lambda i: (0, 0)),
-            pl.BlockSpec((own_cols, vox_half), lambda i: (0, 0)),
-            pl.BlockSpec((2, vox_half), lambda i: (0, 0)),
-        ],
-        out_specs=[
-            pl.BlockSpec((tall * groups, 128), lambda i: (i, 0)),
-            pl.BlockSpec((8, 128), lambda i: (0, 0)),
-        ],
-        out_shape=[sd((block_rows * groups, 128)), sd((8, 128))],
-        scratch_shapes=[pltpu.VMEM((own_cols, vox_total), BF16)],
-        compiler_params=PARAMS,
-    )(
-        centered,
-        other,
-        col_kept.reshape(own_cols, vox_half),
-        col_other.reshape(own_cols, vox_half),
-        means,
-    )
+    flat = (own_cols, vox_half)
+    operands = (centered, other, col_kept.reshape(flat), col_other.reshape(flat), means)
+    gram, first = gram_part(vox_total, groups, 0, None, *operands)
+    (summed,) = call(
+        functools.partial(sum_repeat_kernel, copies, col_count),
+        [sd((width, width))],
+        exchange(slices, ("row", "vox")),
+        after=[first],
+    )
+    cross = exchange(summed, "col")
+    gram, second = gram_part(vox_total, groups, 1, gram, *operands)
     factor, basis = call(
         functools.partial(cholesky_kernel, 16),
         [sd((width, width)), sd((half_rows, width))],
         cross,
         own,
-        after=[done],
+        after=[second],
         scratch_shapes=[pltpu.VMEM((width, width + 128), F32)],
     )
     return gram.reshape(block_rows, groups, 1, sub_rows), basis, factor

time: 158 us -> 209 us (1.32)
  Pallas kernels: 33.4 us -> 99.3 us
  waiting for transfers between devices: 34.1 us -> 25 us
  local copies, waits for them, and re-layouts: 9.71 us -> 2.15 us
    pallas_call x1, Pallas kernels: 0.85 us -> 65.4 us  [shards(): pl.pallas_call(functools.partial(sort_kernel, [key for key, _ in ring]),...]
    ppermute x8, waiting for transfers between devices: 25.6 us -> 10.6 us  [ring_step(): return (lax.ppermute(up, axis, ahead), lax.ppermute(down, axis, back))]
    unnamed x34 -> x20, local copies, waits for them, and re-layouts: 9.69 us -> 2.13 us
    all_to_all x4, waiting for transfers between devices: 2.04 us -> 6.42 us  [exchange(): return lax.all_to_all(value, axis, 0, 0, tiled=True)]
    ppermute x1, starting transfers between devices: 3.7 us -> 0.33 us  [shards(): got = lax.ppermute(sent, 'vox', swap)]
    ppermute x1, starting transfers between devices: 2.59 us -> 5.69 us  [shards(): col_other = lax.ppermute(col_sent, 'vox', swap)]
    pallas_call x6 -> x7, Pallas kernels: 22.9 us -> 23.5 us  [the longest x5 12.6 us: call(): pl.pallas_call(body, out_shape=[*out_shape, *[sd(x.shape, x.dtype) for x...]
  transfers between devices with their start and end apart: 17 -> 17, of which waited for: 8 -> 8; matrix products, arithmetic and copies ran while one was open for 0% -> 0% of each run, Pallas kernels for 10% -> 38%
where the time goes in v3:
time: 209 us
  Pallas kernels  99.3 us (48%)
  starting transfers between devices  48.8 us (23%)
  waiting for transfers between devices  25 us (12%)
  blocking collectives  18.4 us (9%)
  between operations  14.2 us (7%)
  local copies, waits for them, and re-layouts  2.15 us (1%)
    pallas_call x1, Pallas kernels, shards(): pl.pallas_call(functools.partial(sort_kernel, [key for key, _ in ring]),...  65.4 us
    all_to_all x4, starting transfers between devices, exchange(): return lax.all_to_all(value, axis, 0, 0, tiled=True)  27.3 us
    all_to_all x1, blocking collectives, exchange(): return lax.all_to_all(value, axis, 0, 0, tiled=True)  18.4 us
    ppermute x8, starting transfers between devices, ring_step(): return (lax.ppermute(up, axis, ahead), lax.ppermute(down, axis, back))  14.7 us
    pallas_call x5, Pallas kernels, call(): pl.pallas_call(body, out_shape=[*out_shape, *[sd(x.shape, x.dtype) for x...  12.6 us
    pallas_call x2, Pallas kernels, gram_part(): pl.pallas_call(functools.partial(gram_kernel, vox_total), grid=(steps,),...  10.9 us
    ppermute x8, waiting for transfers between devices, ring_step(): return (lax.ppermute(up, axis, ahead), lax.ppermute(down, axis, back))  10.6 us
    pallas_call x1, Pallas kernels, shards(): pl.pallas_call(functools.partial(sketch_kernel, col_count, vox_total), gr...  7.93 us
  transfers between devices with their start and end apart: 17, of which 8 were waited for; matrix products, arithmetic and copies ran while one was open for 0% of the time, Pallas kernels for 38%

profile of v3, /device:TPU:1, one launch (start us, length us, event | category | flops | bytes accessed | tf_op | source)
XLA Modules:
  0.0 208.6 jit_solution(4728643694600467879)
XLA Ops:
  7.9 2.3 %shard_map.49 = f32[1152,256]{1,0:T(8,128)} custom-call(bf16[128,1024]{1,0:T(8,128)(2,1)} %refs_0_.3, bf16[128,256]{1,0:T(8,128)(2,1)} %refs_1_.1), custom_call_target="tpu_custom_call" | custom-call | tf_op jit(solution)/shard_map/pallas_call | solution.py:28
  10.2 7.6 %all-to-all-start = ((f32[16,72,256]{2,1,0:T(8,128)}), f32[16,72,256]{2,1,0:T(8,128)S(1)}, u32[]{:S(2)}, u32[]{:S(2)}) async-start(f32[16,72,256]{2,1,0:T(8,128)} %bitcast.28), calls=%async_computation | async-start | bytes 2359296 | tf_op jit(solution)/shard_map/all_to_all | solution.py:295
  19.5 4.0 %collective-permute-start.2 = (bf16[128,1024]{1,0:T(8,128)(2,1)}, bf16[128,1024]{1,0:T(8,128)(2,1)S(1)}, u32[]{:S(2)}, u32[]{:S(2)}) collective-permute-start(bf16[128,1024]{1,0:T(8,128)(2,1)} %refs_0_.3), channel_id=1, source_target_pairs={{0,224},{32,0},{64,32},{96,64},{128,96},{160,128},{192,160},{224,1... | collective-permute-start | bytes 786440 | tf_op jit(solution)/shard_map/ppermute | solution.py:276
  23.6 5.8 %collective-permute-done.refs_1_ = bf16[128,1024]{1,0:T(8,128)(2,1)S(1)} collective-permute-done((bf16[128,1024]{1,0:T(8,128)(2,1)}, bf16[128,1024]{1,0:T(8,128)(2,1)S(1)}, u32[]{:S(2)}, u32[]{:S(2)}) %collective-permute-start) | collective-permute-done | bytes 262176 | tf_op jit(solution)/shard_map/ppermute | solution.py:276
  29.4 2.7 %collective-permute-start.3 = (bf16[128,1024]{1,0:T(8,128)(2,1)S(1)}, bf16[128,1024]{1,0:T(8,128)(2,1)S(1)}, u32[]{:S(2)}, u32[]{:S(2)}) collective-permute-start(bf16[128,1024]{1,0:T(8,128)(2,1)S(1)} %collective-permute-done.2.refs_2_), channel_id=1, source_target_pairs={{0,224},{32,0},{64,32},{96,64},{128,96},{160,128},{192,160},{224,1... | collective-permute-start | bytes 786440 | tf_op jit(solution)/shard_map/ppermute | solution.py:276
  32.1 4.8 %collective-permute-done.1.refs_1_ = bf16[128,1024]{1,0:T(8,128)(2,1)S(1)} collective-permute-done((bf16[128,1024]{1,0:T(8,128)(2,1)S(1)}, bf16[128,1024]{1,0:T(8,128)(2,1)S(1)}, u32[]{:S(2)}, u32[]{:S(2)}) %collective-permute-start.1) | collective-permute-done | bytes 262176 | tf_op jit(solution)/shard_map/ppermute | solution.py:276
  37.0 18.4 %all_to_all.55 = f32[8,72,256]{2,1,0:T(8,128)S(1)} all-to-all(f32[8,72,256]{2,1,0:T(8,128)S(1)} %bitcast.24), channel_id=1, replica_groups=mesh['row'=8,'col'=16,'vox'=2] {'row'}, dimensions={0} | all-to-all | bytes 1179648 | tf_op jit(solution)/shard_map/all_to_all | solution.py:295
  56.8 2.4 %collective-permute-start.5 = (bf16[128,1024]{1,0:T(8,128)(2,1)S(1)}, bf16[128,1024]{1,0:T(8,128)(2,1)S(1)}, u32[]{:S(2)}, u32[]{:S(2)}) collective-permute-start(bf16[128,1024]{1,0:T(8,128)(2,1)S(1)} %get-tuple-element.23.refs_4_), channel_id=1, source_target_pairs={{0,224},{32,0},{64,32},{96,64},{128,96},{160,128},{192,160},{224,1... | collective-permute-start | bytes 786440 | tf_op jit(solution)/shard_map/ppermute | solution.py:276
  59.3 3.6 %collective-permute-start.7 = (bf16[64,1024]{1,0:T(8,128)(2,1)S(1)}, bf16[64,1024]{1,0:T(8,128)(2,1)S(1)}, u32[]{:S(2)}, u32[]{:S(2)}) collective-permute-start(bf16[64,1024]{1,0:T(8,128)(2,1)S(1)} %slice.7), channel_id=1, source_target_pairs={{0,192},{32,224},{64,0},{96,32},{128,64},{160,96},{192,128},{224,1... | collective-permute-start | bytes 393224 | tf_op jit(solution)/shard_map/ppermute | solution.py:276
  62.9 9.2 %all-to-all-start.2 = ((f32[16,72,256]{2,1,0:T(8,128)}), f32[16,72,256]{2,1,0:T(8,128)S(1)}, u32[]{:S(2)}, u32[]{:S(2)}) async-start(f32[16,72,256]{2,1,0:T(8,128)} %bitcast.7), calls=%async_computation.2 | async-start | bytes 2359296 | tf_op jit(solution)/shard_map/all_to_all | solution.py:295
  74.3 65.4 %shard_map.52 = (bf16[4,128,1024]{2,1,0:T(8,128)(2,1)}, bf16[4,128,1024]{2,1,0:T(8,128)(2,1)}) custom-call(s32[3]{0:T(128)} %pad_add_fusion.pos_ref, bf16[128,1024]{1,0:T(8,128)(2,1)} %refs_0_.3, bf16[128,1024]{1,0:T(8,128)(2,1)} %copy-done.4, bf16[128,1024]{1,0:T(8,128)(2,1)} %copy-done.5, bf16[128,1024]{1,0:T(8,128)(2,1)} %copy-done.1, ...), custom_call_target="tpu_custom_call" | custom-call | bytes 1024 | tf_op jit(solution)/shard_map/pallas_call | solution.py:338
  139.7 5.7 %collective-permute-start.8 = (bf16[4,128,1024]{2,1,0:T(8,128)(2,1)}, bf16[4,128,1024]{2,1,0:T(8,128)(2,1)S(1)}, u32[]{:S(2)}, u32[]{:S(2)}) collective-permute-start(bf16[4,128,1024]{2,1,0:T(8,128)(2,1)} %get-tuple-element.24), channel_id=1, source_target_pairs={{0,1},{1,0},{2,3},{3,2},{4,5},{5,4},{6,7},{7,6},{8,9},{9,8},{10,11... | collective-permute-start | bytes 3145736 | tf_op jit(solution)/shard_map/ppermute | solution.py:351
  145.4 2.5 %collective-permute-done.8._ = bf16[4,128,1024]{2,1,0:T(8,128)(2,1)S(1)} collective-permute-done((bf16[4,128,1024]{2,1,0:T(8,128)(2,1)}, bf16[4,128,1024]{2,1,0:T(8,128)(2,1)S(1)}, u32[]{:S(2)}, u32[]{:S(2)}) %collective-permute-start.8) | collective-permute-done | bytes 1048608 | tf_op jit(solution)/shard_map/ppermute | solution.py:351
  148.5 7.9 %shard_map.53 = (f32[16,64,256]{2,1,0:T(8,128)S(1)}, f32[16,64,256]{2,1,0:T(8,128)S(1)}, f32[1,1024]{1,0:T(1,128)S(1)}, bf16[2048,1024]{1,0:T(8,128)(2,1)}) custom-call(s32[3]{0:T(128)S(1)} %copy-done.3, bf16[2048,1024]{1,0:T(8,128)(2,1)} %all-gather.2.cloned.1.call-done.maps_ref, f32[1152,256]{1,0:T(8,128)S(1)} %bitcast.20, ...), custom_call_target="tpu_custom_call" | custom-call | tf_op jit(solution)/shard_map/pallas_call | solution.py:356
  156.8 2.3 %collective-permute-done.9.got_ref = f32[16,64,256]{2,1,0:T(8,128)S(1)} collective-permute-done((f32[16,64,256]{2,1,0:T(8,128)S(1)}, f32[16,64,256]{2,1,0:T(8,128)S(1)}, u32[]{:S(2)}, u32[]{:S(2)}) %collective-permute-start.9) | collective-permute-done | bytes 1048608 | tf_op jit(solution)/shard_map/ppermute | solution.py:382
  159.1 2.5 %shard_map.54 = (f32[256,256]{1,0:T(8,128)}, f32[64,256]{1,0:T(8,128)S(1)}, bf16[2048,1024]{1,0:T(8,128)(2,1)}) custom-call(s32[3]{0:T(128)S(1)} %copy-done.3, f32[16,64,256]{2,1,0:T(8,128)S(1)} %get-tuple-element.25.kept_ref, f32[16,64,256]{2,1,0:T(8,128)S(1)} %collective-permute-done.9.got_ref, ...), custom_call_target="tpu_custom_call", output_to_operand_aliasing={{2}: (3, {})} | custom-call | tf_op jit(solution)/shard_map/pallas_call | solution.py:385
  161.9 4.3 %all-to-all-start.3 = ((f32[16,16,256]{2,1,0:T(8,128)}), f32[16,16,256]{2,1,0:T(8,128)S(1)}, u32[]{:S(2)}, u32[]{:S(2)}) async-start(f32[16,16,256]{2,1,0:T(8,128)} %bitcast.13), calls=%async_computation.3 | async-start | bytes 524288 | tf_op jit(solution)/shard_map/all_to_all | solution.py:295
  166.6 2.2 %collective-permute-done.11 = f32[1,1024]{1,0:T(1,128)S(1)} collective-permute-done((f32[1,1024]{1,0:T(1,128)S(1)}, f32[1,1024]{1,0:T(1,128)S(1)}, u32[]{:S(2)}, u32[]{:S(2)}) %collective-permute-start.11) | collective-permute-done | bytes 4128 | tf_op jit(solution)/shard_map/ppermute | solution.py:411
  169.1 5.4 %shard_map.55 = (f32[8192,128]{1,0:T(8,128)}, f32[8,128]{1,0:T(8,128)S(1)}) custom-call(bf16[2048,1024]{1,0:T(8,128)(2,1)} %get-tuple-element.28.own_ref, bf16[2048,1024]{1,0:T(8,128)(2,1)} %collective-permute-done.10.other_ref, bf16[512,1024]{1,0:T(8,128)(2,1)S(1)} %bitcast.22, bf16[512,1024]{1,0:T(8,128)(2,1)S(1)} %bitcast.18, ...), custom_call_target="tpu_custom_call" | custom-call | tf_op jit(solution)/shard_map/pallas_call | solution.py:251
  174.5 3.4 %all-to-all-done.3 = f32[16,16,256]{2,1,0:T(8,128)S(1)} async-done(((f32[16,16,256]{2,1,0:T(8,128)}), f32[16,16,256]{2,1,0:T(8,128)S(1)}, u32[]{:S(2)}, u32[]{:S(2)}) %all-to-all-start.3) | async-done | bytes 262176 | tf_op jit(solution)/shard_map/all_to_all | solution.py:295
  178.7 6.3 %all-to-all-start.4 = ((f32[16,16,256]{2,1,0:T(8,128)}), f32[16,16,256]{2,1,0:T(8,128)S(1)}, u32[]{:S(2)}, u32[]{:S(2)}) async-start(f32[16,16,256]{2,1,0:T(8,128)} %bitcast.15), calls=%async_computation.4 | async-start | bytes 524288 | tf_op jit(solution)/shard_map/all_to_all | solution.py:295
  185.0 5.5 %shard_map.56 = (f32[8192,128]{1,0:T(8,128)}, f32[8,128]{1,0:T(8,128)S(1)}) custom-call(bf16[2048,1024]{1,0:T(8,128)(2,1)} %get-tuple-element.28.own_ref, bf16[2048,1024]{1,0:T(8,128)(2,1)} %collective-permute-done.10.other_ref, bf16[512,1024]{1,0:T(8,128)(2,1)S(1)} %bitcast.23, bf16[512,1024]{1,0:T(8,128)(2,1)S(1)} %bitcast.19, ...), custom_call_target="tpu_custom_call", output_to_operand_aliasing={{0}: (5, {})} | custom-call | tf_op jit(solution)/shard_map/pallas_call | solution.py:251
  190.4 3.0 %all-to-all-done.4 = f32[16,16,256]{2,1,0:T(8,128)S(1)} async-done(((f32[16,16,256]{2,1,0:T(8,128)}), f32[16,16,256]{2,1,0:T(8,128)S(1)}, u32[]{:S(2)}, u32[]{:S(2)}) %all-to-all-start.4) | async-done | bytes 262176 | tf_op jit(solution)/shard_map/all_to_all | solution.py:295
  193.5 8.3 %shard_map.58 = (f32[256,256]{1,0:T(8,128)}, f32[64,256]{1,0:T(8,128)}) custom-call(f32[256,256]{1,0:T(8,128)S(1)} %bitcast.27, f32[64,256]{1,0:T(8,128)S(1)} %get-tuple-element.35.refs_1_, f32[8,128]{1,0:T(8,128)S(1)} %get-tuple-element.36.refs_2_), custom_call_target="tpu_custom_call" | custom-call | tf_op jit(solution)/shard_map/pallas_call | solution.py:28
  (46 shorter events, 9.0 us)
Async XLA Ops:
  7.2 140.7 %all-gather.2.cloned.1.call-start = ((), (), s32[]{:S(2)}) async-start(), calls=%async_computation.5 | async-start | bytes 4456448 | tf_op jit(solution)/shard_map/all_gather | solution.py:297
  10.2 26.7 %all-to-all-start = ((f32[16,72,256]{2,1,0:T(8,128)}), f32[16,72,256]{2,1,0:T(8,128)S(1)}, u32[]{:S(2)}, u32[]{:S(2)}) async-start(f32[16,72,256]{2,1,0:T(8,128)} %bitcast.28), calls=%async_computation | async-start | bytes 2359296 | tf_op jit(solution)/shard_map/all_to_all | solution.py:295
  17.8 11.6 %collective-permute-start = (bf16[128,1024]{1,0:T(8,128)(2,1)}, bf16[128,1024]{1,0:T(8,128)(2,1)S(1)}, u32[]{:S(2)}, u32[]{:S(2)}) collective-permute-start(bf16[128,1024]{1,0:T(8,128)(2,1)} %refs_0_.3), channel_id=1, source_target_pairs={{0,32},{32,64},{64,96},{96,128},{128,160},{160,192},{192,224},{224... | collective-permute-start | bytes 786440 | tf_op jit(solution)/shard_map/ppermute | solution.py:276
  19.5 9.9 %collective-permute-start.2 = (bf16[128,1024]{1,0:T(8,128)(2,1)}, bf16[128,1024]{1,0:T(8,128)(2,1)S(1)}, u32[]{:S(2)}, u32[]{:S(2)}) collective-permute-start(bf16[128,1024]{1,0:T(8,128)(2,1)} %refs_0_.3), channel_id=1, source_target_pairs={{0,224},{32,0},{64,32},{96,64},{128,96},{160,128},{192,160},{224,1... | collective-permute-start | bytes 786440 | tf_op jit(solution)/shard_map/ppermute | solution.py:276
  29.4 43.4 %copy-start.4 = (bf16[128,1024]{1,0:T(8,128)(2,1)}, bf16[128,1024]{1,0:T(8,128)(2,1)S(1)}, u32[]{:S(2)}) copy-start(bf16[128,1024]{1,0:T(8,128)(2,1)S(1)} %collective-permute-done.refs_1_) | copy-start | bytes 786436
  29.4 7.5 %collective-permute-start.1 = (bf16[128,1024]{1,0:T(8,128)(2,1)S(1)}, bf16[128,1024]{1,0:T(8,128)(2,1)S(1)}, u32[]{:S(2)}, u32[]{:S(2)}) collective-permute-start(bf16[128,1024]{1,0:T(8,128)(2,1)S(1)} %collective-permute-done.refs_1_), channel_id=1, source_target_pairs={{0,32},{32,64},{64,96},{96,128},{128,160},{160,192},{192,224},{224... | collective-permute-start | bytes 786440 | tf_op jit(solution)/shard_map/ppermute | solution.py:276
  29.4 7.5 %copy-start.5 = (bf16[128,1024]{1,0:T(8,128)(2,1)}, bf16[128,1024]{1,0:T(8,128)(2,1)S(1)}, u32[]{:S(2)}) copy-start(bf16[128,1024]{1,0:T(8,128)(2,1)S(1)} %collective-permute-done.2.refs_2_) | copy-start | bytes 786436
  29.4 7.5 %collective-permute-start.3 = (bf16[128,1024]{1,0:T(8,128)(2,1)S(1)}, bf16[128,1024]{1,0:T(8,128)(2,1)S(1)}, u32[]{:S(2)}, u32[]{:S(2)}) collective-permute-start(bf16[128,1024]{1,0:T(8,128)(2,1)S(1)} %collective-permute-done.2.refs_2_), channel_id=1, source_target_pairs={{0,224},{32,0},{64,32},{96,64},{128,96},{160,128},{192,160},{224,1... | collective-permute-start | bytes 786440 | tf_op jit(solution)/shard_map/ppermute | solution.py:276
  56.5 16.3 %copy-start.1 = (bf16[128,1024]{1,0:T(8,128)(2,1)}, bf16[128,1024]{1,0:T(8,128)(2,1)S(1)}, u32[]{:S(2)}) copy-start(bf16[128,1024]{1,0:T(8,128)(2,1)S(1)} %get-tuple-element.22.refs_3_) | copy-start | bytes 786436
  56.5 16.3 %copy-start.2 = (bf16[128,1024]{1,0:T(8,128)(2,1)}, bf16[128,1024]{1,0:T(8,128)(2,1)S(1)}, u32[]{:S(2)}) copy-start(bf16[128,1024]{1,0:T(8,128)(2,1)S(1)} %get-tuple-element.23.refs_4_) | copy-start | bytes 786436
  56.5 16.2 %collective-permute-start.4 = (bf16[128,1024]{1,0:T(8,128)(2,1)S(1)}, bf16[128,1024]{1,0:T(8,128)(2,1)S(1)}, u32[]{:S(2)}, u32[]{:S(2)}) collective-permute-start(bf16[128,1024]{1,0:T(8,128)(2,1)S(1)} %get-tuple-element.22.refs_3_), channel_id=1, source_target_pairs={{0,32},{32,64},{64,96},{96,128},{128,160},{160,192},{192,224},{224... | collective-permute-start | bytes 786440 | tf_op jit(solution)/shard_map/ppermute | solution.py:276
  56.8 16.0 %collective-permute-start.5 = (bf16[128,1024]{1,0:T(8,128)(2,1)S(1)}, bf16[128,1024]{1,0:T(8,128)(2,1)S(1)}, u32[]{:S(2)}, u32[]{:S(2)}) collective-permute-start(bf16[128,1024]{1,0:T(8,128)(2,1)S(1)} %get-tuple-element.23.refs_4_), channel_id=1, source_target_pairs={{0,224},{32,0},{64,32},{96,64},{128,96},{160,128},{192,160},{224,1... | collective-permute-start | bytes 786440 | tf_op jit(solution)/shard_map/ppermute | solution.py:276
  59.3 13.5 %collective-permute-start.6 = (bf16[64,1024]{1,0:T(8,128)(2,1)S(1)}, bf16[64,1024]{1,0:T(8,128)(2,1)S(1)}, u32[]{:S(2)}, u32[]{:S(2)}) collective-permute-start(bf16[64,1024]{1,0:T(8,128)(2,1)S(1)} %slice.6), channel_id=1, source_target_pairs={{0,64},{32,96},{64,128},{96,160},{128,192},{160,224},{192,0},{224,... | collective-permute-start | bytes 393224 | tf_op jit(solution)/shard_map/ppermute | solution.py:276
  59.3 13.4 %collective-permute-start.7 = (bf16[64,1024]{1,0:T(8,128)(2,1)S(1)}, bf16[64,1024]{1,0:T(8,128)(2,1)S(1)}, u32[]{:S(2)}, u32[]{:S(2)}) collective-permute-start(bf16[64,1024]{1,0:T(8,128)(2,1)S(1)} %slice.7), channel_id=1, source_target_pairs={{0,192},{32,224},{64,0},{96,32},{128,64},{160,96},{192,128},{224,1... | collective-permute-start | bytes 393224 | tf_op jit(solution)/shard_map/ppermute | solution.py:276
  62.9 82.4 %all-to-all-start.2 = ((f32[16,72,256]{2,1,0:T(8,128)}), f32[16,72,256]{2,1,0:T(8,128)S(1)}, u32[]{:S(2)}, u32[]{:S(2)}) async-start(f32[16,72,256]{2,1,0:T(8,128)} %bitcast.7), calls=%async_computation.2 | async-start | bytes 2359296 | tf_op jit(solution)/shard_map/all_to_all | solution.py:295
  72.8 0.8 copy-start.6
  73.6 0.7 copy-start.7
  139.7 8.2 %collective-permute-start.8 = (bf16[4,128,1024]{2,1,0:T(8,128)(2,1)}, bf16[4,128,1024]{2,1,0:T(8,128)(2,1)S(1)}, u32[]{:S(2)}, u32[]{:S(2)}) collective-permute-start(bf16[4,128,1024]{2,1,0:T(8,128)(2,1)} %get-tuple-element.24), channel_id=1, source_target_pairs={{0,1},{1,0},{2,3},{3,2},{4,5},{5,4},{6,7},{7,6},{8,9},{9,8},{10,11... | collective-permute-start | bytes 3145736 | tf_op jit(solution)/shard_map/ppermute | solution.py:351
  156.4 12.7 %copy-start = (bf16[4,128,1024]{2,1,0:T(8,128)(2,1)S(1)}, bf16[4,128,1024]{2,1,0:T(8,128)(2,1)}, u32[]{:S(2)}) copy-start(bf16[4,128,1024]{2,1,0:T(8,128)(2,1)} %get-tuple-element.29) | copy-start | bytes 3145732
  156.4 2.7 %collective-permute-start.9 = (f32[16,64,256]{2,1,0:T(8,128)S(1)}, f32[16,64,256]{2,1,0:T(8,128)S(1)}, u32[]{:S(2)}, u32[]{:S(2)}) collective-permute-start(f32[16,64,256]{2,1,0:T(8,128)S(1)} %get-tuple-element.26), channel_id=1, source_target_pairs={{0,1},{1,0},{2,3},{3,2},{4,5},{5,4},{6,7},{7,6},{8,9},{9,8},{10,11... | collective-permute-start | bytes 3145736 | tf_op jit(solution)/shard_map/ppermute | solution.py:382
  161.6 7.5 %collective-permute-start.10 = (bf16[2048,1024]{1,0:T(8,128)(2,1)}, bf16[2048,1024]{1,0:T(8,128)(2,1)}, u32[]{:S(2)}, u32[]{:S(2)}) collective-permute-start(bf16[2048,1024]{1,0:T(8,128)(2,1)} %get-tuple-element.28.own_ref), channel_id=1, source_target_pairs={{0,1},{1,0},{2,3},{3,2},{4,5},{5,4},{6,7},{7,6},{8,9},{9,8},{10,11... | collective-permute-start | bytes 12582920 | tf_op jit(solution)/shard_map/ppermute | solution.py:410
  161.9 16.0 %all-to-all-start.3 = ((f32[16,16,256]{2,1,0:T(8,128)}), f32[16,16,256]{2,1,0:T(8,128)S(1)}, u32[]{:S(2)}, u32[]{:S(2)}) async-start(f32[16,16,256]{2,1,0:T(8,128)} %bitcast.13), calls=%async_computation.3 | async-start | bytes 524288 | tf_op jit(solution)/shard_map/all_to_all | solution.py:295
  166.2 2.5 %collective-permute-start.11 = (f32[1,1024]{1,0:T(1,128)S(1)}, f32[1,1024]{1,0:T(1,128)S(1)}, u32[]{:S(2)}, u32[]{:S(2)}) collective-permute-start(f32[1,1024]{1,0:T(1,128)S(1)} %get-tuple-element.30), channel_id=1, source_target_pairs={{0,1},{1,0},{2,3},{3,2},{4,5},{5,4},{6,7},{7,6},{8,9},{9,8},{10,11... | collective-permute-start | bytes 12296 | tf_op jit(solution)/shard_map/ppermute | solution.py:411
  178.7 14.8 %all-to-all-start.4 = ((f32[16,16,256]{2,1,0:T(8,128)}), f32[16,16,256]{2,1,0:T(8,128)S(1)}, u32[]{:S(2)}, u32[]{:S(2)}) async-start(f32[16,16,256]{2,1,0:T(8,128)} %bitcast.15), calls=%async_computation.4 | async-start | bytes 524288 | tf_op jit(solution)/shard_map/all_to_all | solution.py:295
  (3 other events, 2.0 us)
Sparse Core Ops, SparseCore 0:
  10.4 63.9 all-gather.1

commit v4 on v3

--- a/solution.py
+++ b/solution.py
@@ -72,7 +72,25 @@
         out_ref[k * rows : (k + 1) * rows, :] = total
 
 
-def centre_kernel(sources, copies, subjects, in_ref, out_ref):
+def centre_kernel(
+    sources,
+    copies,
+    subjects,
+    in_ref,
+    up1_ref,
+    down1_ref,
+    up2_ref,
+    down2_ref,
+    out_ref,
+    up_ref,
+    down_ref,
+):
+    sub_rows = up1_ref.shape[0]
+    half_block = sub_rows // 2
+    up_ref[:sub_rows, :] = up1_ref[...]
+    up_ref[sub_rows:, :] = up2_ref[:half_block, :]
+    down_ref[:sub_rows, :] = down1_ref[...]
+    down_ref[sub_rows:, :] = down2_ref[half_block:, :]
     rows = in_ref.shape[0] // sources
     width = rows - PAD
     total = in_ref[0:rows, :]
@@ -91,9 +109,9 @@
         out_ref[k * rows + width : k * rows + width + 1, :width] = mean
 
 
-def split_terms(value):
+def split_terms(value, count=3):
     terms = []
-    for _ in range(3):
+    for _ in range(count):
         term = value.astype(BF16)
         terms.append(term)
         value = value - term.astype(F32)
@@ -110,7 +128,7 @@
     def _():
         for k in range(pieces):
             w = w_ref[k * rows : k * rows + width, :] * (1.0 / vox_total)
-            for n, part in enumerate(split_terms(w)):
+            for n, part in enumerate(split_terms(w, 2)):
                 parts[n, k * width : (k + 1) * width, :] = part
         mean_ref[...] = jnp.concatenate(
             [w_ref[k * rows + width : k * rows + width + 1, :width] for k in range(pieces)], axis=1
@@ -120,7 +138,6 @@
     centered_ref[...] = centered
     total = jnp.dot(centered, parts[0], preferred_element_type=F32)
     total += jnp.dot(centered, parts[1], preferred_element_type=F32)
-    total += jnp.dot(centered, parts[2], preferred_element_type=F32)
     count, half = kept_ref.shape[0], kept_ref.shape[1]
     split = total.reshape(count, 2, half, total.shape[1])
 
@@ -135,30 +152,23 @@
         sent_ref[...] = split[:, 0]
 
 
-def sort_kernel(shifts, pos_ref, *refs):
-    count = len(shifts)
-    pieces, (kept_ref, sent_ref, arrived) = refs[:count], refs[count:]
+def sort_kernel(places, pos_ref, *refs):
+    pieces, kept_ref, sent_ref = refs[:-2], refs[-2], refs[-1]
     groups = kept_ref.shape[0]
     total = 2 * groups
-    for k, ((shift, start), piece) in enumerate(zip(shifts, pieces)):
+    for index, source, rows, shift, target in places:
         group = lax.rem(pos_ref[2] + (shift + total), total)
         mine = group // groups == pos_ref[0]
         place = lax.rem(group, groups)
-        rows = piece.shape[0]
+        piece = pieces[index]
 
         @pl.when(mine)
-        def _(k=k, piece=piece, place=place, start=start, rows=rows):
-            target = kept_ref.at[place, pl.ds(start, rows)]
-            pltpu.make_async_copy(piece, target, arrived.at[k]).start()
+        def _(piece=piece, source=source, rows=rows, place=place, target=target):
+            kept_ref[place, target : target + rows, :] = piece[source : source + rows, :]
 
         @pl.when(jnp.logical_not(mine))
-        def _(k=k, piece=piece, place=place, start=start, rows=rows):
-            target = sent_ref.at[place, pl.ds(start, rows)]
-            pltpu.make_async_copy(piece, target, arrived.at[k]).start()
-
-    for k, ((_, start), piece) in enumerate(zip(shifts, pieces)):
-        target = kept_ref.at[0, pl.ds(start, piece.shape[0])]
-        pltpu.make_async_copy(piece, target, arrived.at[k]).wait()
+        def _(piece=piece, source=source, rows=rows, place=place, target=target):
+            sent_ref[place, target : target + rows, :] = piece[source : source + rows, :]
 
 
 def cross_kernel(subjects, copies, pos_ref, kept_ref, got_ref, _, out_ref, own_ref, __, full):
@@ -296,9 +306,8 @@
 
     row_maps = lax.all_gather(maps, "col", axis=0, tiled=True)
     slice_rows = vox_half // col_count + PAD
-    up, down = ring_step(maps, maps, "row", row_count)
-    ring = [((0, 0), maps), ((-1, 0), up), ((1, 0), down)]
-    up, down = ring_step(up, down, "row", row_count)
+    up1, down1 = ring_step(maps, maps, "row", row_count)
+    up2, down2 = ring_step(up1, down1, "row", row_count)
     (local,) = call(
         functools.partial(project_kernel, col_count),
         [sd((col_count * slice_rows, width))],
@@ -316,38 +325,37 @@
         functools.partial(sum_repeat_kernel, col_count, row_count),
         [sd((row_count * slice_rows, width))],
         exchange(local, "col"),
-        after=[up, down],
-    )
+        after=[up1, down1, up2, down2],
+    )
+    half_block = sub_rows // 2
+    far_block = (sub_rows + half_block, vox_half)
     whole, up, down = call(
         functools.partial(centre_kernel, row_count, col_count, subjects),
-        [sd((col_count * slice_rows, width))],
+        [sd((col_count * slice_rows, width)), sd(far_block, BF16), sd(far_block, BF16)],
         exchange(part, "row"),
-        carry=[up, down],
+        up1,
+        down1,
+        up2,
+        down2,
     )
     weights = exchange(whole, "col")
-    ring += [((-2, 0), up), ((2, 0), down)]
-    half_block = sub_rows // 2
-    for k in range(3, row_count // 2):
-        ahead, back = ring_step(up, down, "row", row_count, k - 2)
-        ring += [((-k, 0), ahead), ((k, 0), back)]
-    far = row_count // 2
-    ahead, back = ring_step(up[:half_block], down[half_block:], "row", row_count, far - 2)
-    ring += [((-far, 0), ahead), ((far, half_block), back)]
+    up3, down3 = ring_step(up, down, "row", row_count, 2)
+    ring = [maps, up1, down1, up2, down2, up3, down3]
+    places = [(k, 0, sub_rows, shift, 0) for k, shift in enumerate((0, -1, 1, -2, 2, -3, 3))]
+    places += [(5, sub_rows, half_block, -4, 0), (6, sub_rows, half_block, 4, half_block)]
     group_shape = (groups, sub_rows, vox_half)
-    anywhere = pl.BlockSpec(memory_space=pl.ANY)
+    whole_block = pl.BlockSpec(group_shape, lambda i, p: (0, 0, 0))
     col_kept, col_sent = pl.pallas_call(
-        functools.partial(sort_kernel, [key for key, _ in ring]),
+        functools.partial(sort_kernel, places),
         grid_spec=pltpu.PrefetchScalarGridSpec(
             num_scalar_prefetch=1,
             grid=(1,),
-            in_specs=[anywhere] * len(ring),
-            out_specs=[anywhere] * 2,
-            scratch_shapes=[pltpu.SemaphoreType.DMA((len(ring),))],
+            in_specs=[pl.BlockSpec(piece.shape, lambda i, p: (0, 0)) for piece in ring],
+            out_specs=[whole_block, whole_block],
         ),
         out_shape=[sd(group_shape, BF16)] * 2,
-        cost_estimate=pl.CostEstimate(flops=0, bytes_accessed=1024, transcendentals=0),
         compiler_params=ALL,
-    )(pos, *[piece for _, piece in ring])
+    )(pos, *ring)
     col_other = lax.ppermute(col_sent, "vox", swap)
 
     half_rows = sub_rows // vox_count
@@ -369,7 +377,7 @@
                 pl.BlockSpec((1, vox_half), lambda i, p: (0, 0)),
                 pl.BlockSpec((step, vox_half), lambda i, p: (i, 0)),
             ],
-            scratch_shapes=[pltpu.VMEM((3, vox_half, width), BF16)],
+            scratch_shapes=[pltpu.VMEM((2, vox_half, width), BF16)],
         ),
         out_shape=[
             sd((col_count, half_rows, width)),

time: 209 us -> 151 us (0.72)
  Pallas kernels: 99.3 us -> 36.8 us
  starting transfers between devices: 48.8 us -> 54.1 us
    pallas_call x1, Pallas kernels: 65.4 us -> 3.9 us  [shards(): pl.pallas_call(functools.partial(sort_kernel, places), grid_spec=pltpu.Pr...]
    ppermute x1, starting transfers between devices: 0.33 us -> 4.03 us  [shards(): got = lax.ppermute(sent, 'vox', swap)]
    ppermute x1, starting transfers between devices: 5.69 us -> 9.28 us  [shards(): col_other = lax.ppermute(col_sent, 'vox', swap)]
    ppermute x8 -> x6, starting transfers between devices: 14.7 us -> 12 us  [ring_step(): return (lax.ppermute(up, axis, ahead), lax.ppermute(down, axis, back))]
    all_to_all x4, waiting for transfers between devices: 6.42 us -> 8.74 us  [exchange(): return lax.all_to_all(value, axis, 0, 0, tiled=True)]
    ppermute x8 -> x6, waiting for transfers between devices: 10.6 us -> 10.8 us  [ring_step(): return (lax.ppermute(up, axis, ahead), lax.ppermute(down, axis, back))]
  transfers between devices with their start and end apart: 17 -> 15, of which waited for: 8 -> 8; matrix products, arithmetic and copies ran while one was open for 0% -> 0% of each run, Pallas kernels for 38% -> 12%
where the time goes in v4:
time: 151 us
  starting transfers between devices  54.1 us (36%)
  Pallas kernels  36.8 us (24%)
  waiting for transfers between devices  25.9 us (17%)
  blocking collectives  18.4 us (12%)
  between operations  14.1 us (9%)
    all_to_all x4, starting transfers between devices, exchange(): return lax.all_to_all(value, axis, 0, 0, tiled=True)  28 us
    all_to_all x1, blocking collectives, exchange(): return lax.all_to_all(value, axis, 0, 0, tiled=True)  18.4 us
    pallas_call x5, Pallas kernels, call(): pl.pallas_call(body, out_shape=[*out_shape, *[sd(x.shape, x.dtype) for x...  12.6 us
    ppermute x6, starting transfers between devices, ring_step(): return (lax.ppermute(up, axis, ahead), lax.ppermute(down, axis, back))  12 us
    pallas_call x2, Pallas kernels, gram_part(): pl.pallas_call(functools.partial(gram_kernel, vox_total), grid=(steps,),...  10.9 us
    ppermute x6, waiting for transfers between devices, ring_step(): return (lax.ppermute(up, axis, ahead), lax.ppermute(down, axis, back))  10.8 us
    ppermute x1, starting transfers between devices, shards(): col_other = lax.ppermute(col_sent, 'vox', swap)  9.28 us
    all_to_all x4, waiting for transfers between devices, exchange(): return lax.all_to_all(value, axis, 0, 0, tiled=True)  8.74 us
  transfers between devices with their start and end apart: 15, of which 8 were waited for; matrix products, arithmetic and copies ran while one was open for 0% of the time, Pallas kernels for 12%

profile of v4, /device:TPU:1, one launch (start us, length us, event | category | flops | bytes accessed | tf_op | source)
XLA Modules:
  0.0 150.6 jit_solution(5924529545798532680)
XLA Ops:
  7.9 2.3 %shard_map.49 = f32[1152,256]{1,0:T(8,128)} custom-call(bf16[128,1024]{1,0:T(8,128)(2,1)} %refs_0_.3, bf16[128,256]{1,0:T(8,128)(2,1)} %refs_1_.1), custom_call_target="tpu_custom_call" | custom-call | tf_op jit(solution)/shard_map/pallas_call | solution.py:28
  10.2 7.6 %all-to-all-start = ((f32[16,72,256]{2,1,0:T(8,128)}), f32[16,72,256]{2,1,0:T(8,128)S(1)}, u32[]{:S(2)}, u32[]{:S(2)}) async-start(f32[16,72,256]{2,1,0:T(8,128)} %bitcast.28), calls=%async_computation | async-start | bytes 2359296 | tf_op jit(solution)/shard_map/all_to_all | solution.py:305
  17.8 1.7 %collective-permute-start = (bf16[128,1024]{1,0:T(8,128)(2,1)}, bf16[128,1024]{1,0:T(8,128)(2,1)S(1)}, u32[]{:S(2)}, u32[]{:S(2)}) collective-permute-start(bf16[128,1024]{1,0:T(8,128)(2,1)} %refs_0_.3), channel_id=1, source_target_pairs={{0,32},{32,64},{64,96},{96,128},{128,160},{160,192},{192,224},{224... | collective-permute-start | bytes 786440 | tf_op jit(solution)/shard_map/ppermute | solution.py:286
  19.5 4.0 %collective-permute-start.1 = (bf16[128,1024]{1,0:T(8,128)(2,1)}, bf16[128,1024]{1,0:T(8,128)(2,1)S(1)}, u32[]{:S(2)}, u32[]{:S(2)}) collective-permute-start(bf16[128,1024]{1,0:T(8,128)(2,1)} %refs_0_.3), channel_id=1, source_target_pairs={{0,224},{32,0},{64,32},{96,64},{128,96},{160,128},{192,160},{224,1... | collective-permute-start | bytes 786440 | tf_op jit(solution)/shard_map/ppermute | solution.py:286
  23.6 5.8 %collective-permute-done.refs_1_ = bf16[128,1024]{1,0:T(8,128)(2,1)S(1)} collective-permute-done((bf16[128,1024]{1,0:T(8,128)(2,1)}, bf16[128,1024]{1,0:T(8,128)(2,1)S(1)}, u32[]{:S(2)}, u32[]{:S(2)}) %collective-permute-start) | collective-permute-done | bytes 262176 | tf_op jit(solution)/shard_map/ppermute | solution.py:286
  29.4 2.7 %collective-permute-start.3 = (bf16[128,1024]{1,0:T(8,128)(2,1)S(1)}, bf16[128,1024]{1,0:T(8,128)(2,1)S(1)}, u32[]{:S(2)}, u32[]{:S(2)}) collective-permute-start(bf16[128,1024]{1,0:T(8,128)(2,1)S(1)} %collective-permute-done.1.refs_2_), channel_id=1, source_target_pairs={{0,224},{32,0},{64,32},{96,64},{128,96},{160,128},{192,160},{224,1... | collective-permute-start | bytes 786440 | tf_op jit(solution)/shard_map/ppermute | solution.py:286
  32.1 4.8 %collective-permute-done.2.refs_3_ = bf16[128,1024]{1,0:T(8,128)(2,1)S(1)} collective-permute-done((bf16[128,1024]{1,0:T(8,128)(2,1)S(1)}, bf16[128,1024]{1,0:T(8,128)(2,1)S(1)}, u32[]{:S(2)}, u32[]{:S(2)}) %collective-permute-start.2) | collective-permute-done | bytes 262176 | tf_op jit(solution)/shard_map/ppermute | solution.py:286
  37.0 18.4 %all_to_all.55 = f32[8,72,256]{2,1,0:T(8,128)S(1)} all-to-all(f32[8,72,256]{2,1,0:T(8,128)S(1)} %bitcast.25), channel_id=1, replica_groups=mesh['row'=8,'col'=16,'vox'=2] {'row'}, dimensions={0} | all-to-all | bytes 1179648 | tf_op jit(solution)/shard_map/all_to_all | solution.py:305
  57.0 3.1 %collective-permute-start.5 = (bf16[192,1024]{1,0:T(8,128)(2,1)S(1)}, bf16[192,1024]{1,0:T(8,128)(2,1)}, u32[]{:S(2)}, u32[]{:S(2)}) collective-permute-start(bf16[192,1024]{1,0:T(8,128)(2,1)S(1)} %get-tuple-element.23), channel_id=1, source_target_pairs={{0,192},{32,224},{64,0},{96,32},{128,64},{160,96},{192,128},{224,1... | collective-permute-start | bytes 1179656 | tf_op jit(solution)/shard_map/ppermute | solution.py:286
  60.1 9.2 %all-to-all-start.2 = ((f32[16,72,256]{2,1,0:T(8,128)}), f32[16,72,256]{2,1,0:T(8,128)S(1)}, u32[]{:S(2)}, u32[]{:S(2)}) async-start(f32[16,72,256]{2,1,0:T(8,128)} %bitcast.7), calls=%async_computation.2 | async-start | bytes 2359296 | tf_op jit(solution)/shard_map/all_to_all | solution.py:305
  70.2 3.9 %shard_map.52 = (bf16[4,128,1024]{2,1,0:T(8,128)(2,1)}, bf16[4,128,1024]{2,1,0:T(8,128)(2,1)}) custom-call(s32[3]{0:T(128)} %pad_add_fusion.pos_ref, bf16[128,1024]{1,0:T(8,128)(2,1)} %refs_0_.3, bf16[128,1024]{1,0:T(8,128)(2,1)} %copy-done.1, bf16[128,1024]{1,0:T(8,128)(2,1)} %copy-done.2, bf16[128,1024]{1,0:T(8,128)(2,1)} %copy-done.3, ...), custom_call_target="tpu_custom_call" | custom-call | tf_op jit(solution)/shard_map/pallas_call | solution.py:348
  74.1 9.3 %collective-permute-start.6 = (bf16[4,128,1024]{2,1,0:T(8,128)(2,1)}, bf16[4,128,1024]{2,1,0:T(8,128)(2,1)S(1)}, u32[]{:S(2)}, u32[]{:S(2)}) collective-permute-start(bf16[4,128,1024]{2,1,0:T(8,128)(2,1)} %get-tuple-element.24), channel_id=1, source_target_pairs={{0,1},{1,0},{2,3},{3,2},{4,5},{5,4},{6,7},{7,6},{8,9},{9,8},{10,11... | collective-permute-start | bytes 3145736 | tf_op jit(solution)/shard_map/ppermute | solution.py:359
  83.3 2.5 %collective-permute-done.6._ = bf16[4,128,1024]{2,1,0:T(8,128)(2,1)S(1)} collective-permute-done((bf16[4,128,1024]{2,1,0:T(8,128)(2,1)}, bf16[4,128,1024]{2,1,0:T(8,128)(2,1)S(1)}, u32[]{:S(2)}, u32[]{:S(2)}) %collective-permute-start.6) | collective-permute-done | bytes 1048608 | tf_op jit(solution)/shard_map/ppermute | solution.py:359
  86.5 7.0 %shard_map.53 = (f32[16,64,256]{2,1,0:T(8,128)S(1)}, f32[16,64,256]{2,1,0:T(8,128)S(1)}, f32[1,1024]{1,0:T(1,128)S(1)}, bf16[2048,1024]{1,0:T(8,128)(2,1)}) custom-call(s32[3]{0:T(128)S(1)} %copy-done.5, bf16[2048,1024]{1,0:T(8,128)(2,1)} %all-gather.2.cloned.1.call-done.maps_ref, f32[1152,256]{1,0:T(8,128)S(1)} %bitcast.20, ...), custom_call_target="tpu_custom_call" | custom-call | tf_op jit(solution)/shard_map/pallas_call | solution.py:364
  93.4 4.0 %collective-permute-start.7 = (f32[16,64,256]{2,1,0:T(8,128)S(1)}, f32[16,64,256]{2,1,0:T(8,128)S(1)}, u32[]{:S(2)}, u32[]{:S(2)}) collective-permute-start(f32[16,64,256]{2,1,0:T(8,128)S(1)} %get-tuple-element.26), channel_id=1, source_target_pairs={{0,1},{1,0},{2,3},{3,2},{4,5},{5,4},{6,7},{7,6},{8,9},{9,8},{10,11... | collective-permute-start | bytes 3145736 | tf_op jit(solution)/shard_map/ppermute | solution.py:390
  97.5 2.3 %collective-permute-done.7.got_ref = f32[16,64,256]{2,1,0:T(8,128)S(1)} collective-permute-done((f32[16,64,256]{2,1,0:T(8,128)S(1)}, f32[16,64,256]{2,1,0:T(8,128)S(1)}, u32[]{:S(2)}, u32[]{:S(2)}) %collective-permute-start.7) | collective-permute-done | bytes 1048608 | tf_op jit(solution)/shard_map/ppermute | solution.py:390
  99.8 2.5 %shard_map.54 = (f32[256,256]{1,0:T(8,128)}, f32[64,256]{1,0:T(8,128)S(1)}, bf16[2048,1024]{1,0:T(8,128)(2,1)}) custom-call(s32[3]{0:T(128)S(1)} %copy-done.5, f32[16,64,256]{2,1,0:T(8,128)S(1)} %get-tuple-element.25.kept_ref, f32[16,64,256]{2,1,0:T(8,128)S(1)} %collective-permute-done.7.got_ref, ...), custom_call_target="tpu_custom_call", output_to_operand_aliasing={{2}: (3, {})} | custom-call | tf_op jit(solution)/shard_map/pallas_call | solution.py:393
  102.6 7.7 %all-to-all-start.3 = ((f32[16,16,256]{2,1,0:T(8,128)}), f32[16,16,256]{2,1,0:T(8,128)S(1)}, u32[]{:S(2)}, u32[]{:S(2)}) async-start(f32[16,16,256]{2,1,0:T(8,128)} %bitcast.13), calls=%async_computation.3 | async-start | bytes 524288 | tf_op jit(solution)/shard_map/all_to_all | solution.py:305
  111.5 5.5 %shard_map.55 = (f32[8192,128]{1,0:T(8,128)}, f32[8,128]{1,0:T(8,128)S(1)}) custom-call(bf16[2048,1024]{1,0:T(8,128)(2,1)} %get-tuple-element.28.own_ref, bf16[2048,1024]{1,0:T(8,128)(2,1)} %collective-permute-done.8.other_ref, bf16[512,1024]{1,0:T(8,128)(2,1)S(1)} %bitcast.22, bf16[512,1024]{1,0:T(8,128)(2,1)S(1)} %bitcast.18, ...), custom_call_target="tpu_custom_call" | custom-call | tf_op jit(solution)/shard_map/pallas_call | solution.py:261
  117.0 5.0 %all-to-all-done.3 = f32[16,16,256]{2,1,0:T(8,128)S(1)} async-done(((f32[16,16,256]{2,1,0:T(8,128)}), f32[16,16,256]{2,1,0:T(8,128)S(1)}, u32[]{:S(2)}, u32[]{:S(2)}) %all-to-all-start.3) | async-done | bytes 262176 | tf_op jit(solution)/shard_map/all_to_all | solution.py:305
  122.7 3.5 %all-to-all-start.4 = ((f32[16,16,256]{2,1,0:T(8,128)}), f32[16,16,256]{2,1,0:T(8,128)S(1)}, u32[]{:S(2)}, u32[]{:S(2)}) async-start(f32[16,16,256]{2,1,0:T(8,128)} %bitcast.15), calls=%async_computation.4 | async-start | bytes 524288 | tf_op jit(solution)/shard_map/all_to_all | solution.py:305
  126.3 5.5 %shard_map.56 = (f32[8192,128]{1,0:T(8,128)}, f32[8,128]{1,0:T(8,128)S(1)}) custom-call(bf16[2048,1024]{1,0:T(8,128)(2,1)} %get-tuple-element.28.own_ref, bf16[2048,1024]{1,0:T(8,128)(2,1)} %collective-permute-done.8.other_ref, bf16[512,1024]{1,0:T(8,128)(2,1)S(1)} %bitcast.23, bf16[512,1024]{1,0:T(8,128)(2,1)S(1)} %bitcast.19, ...), custom_call_target="tpu_custom_call", output_to_operand_aliasing={{0}: (5, {})} | custom-call | tf_op jit(solution)/shard_map/pallas_call | solution.py:261
  131.7 3.7 %all-to-all-done.4 = f32[16,16,256]{2,1,0:T(8,128)S(1)} async-done(((f32[16,16,256]{2,1,0:T(8,128)}), f32[16,16,256]{2,1,0:T(8,128)S(1)}, u32[]{:S(2)}, u32[]{:S(2)}) %all-to-all-start.4) | async-done | bytes 262176 | tf_op jit(solution)/shard_map/all_to_all | solution.py:305
  135.5 8.3 %shard_map.58 = (f32[256,256]{1,0:T(8,128)}, f32[64,256]{1,0:T(8,128)}) custom-call(f32[256,256]{1,0:T(8,128)S(1)} %bitcast.27, f32[64,256]{1,0:T(8,128)S(1)} %get-tuple-element.35.refs_1_, f32[8,128]{1,0:T(8,128)S(1)} %get-tuple-element.36.refs_2_), custom_call_target="tpu_custom_call" | custom-call | tf_op jit(solution)/shard_map/pallas_call | solution.py:28
  (32 shorter events, 6.2 us)
Async XLA Ops:
  7.2 78.7 %all-gather.2.cloned.1.call-start = ((), (), s32[]{:S(2)}) async-start(), calls=%async_computation.5 | async-start | bytes 4456448 | tf_op jit(solution)/shard_map/all_gather | solution.py:307
  10.2 26.7 %all-to-all-start = ((f32[16,72,256]{2,1,0:T(8,128)}), f32[16,72,256]{2,1,0:T(8,128)S(1)}, u32[]{:S(2)}, u32[]{:S(2)}) async-start(f32[16,72,256]{2,1,0:T(8,128)} %bitcast.28), calls=%async_computation | async-start | bytes 2359296 | tf_op jit(solution)/shard_map/all_to_all | solution.py:305
  17.8 11.6 %collective-permute-start = (bf16[128,1024]{1,0:T(8,128)(2,1)}, bf16[128,1024]{1,0:T(8,128)(2,1)S(1)}, u32[]{:S(2)}, u32[]{:S(2)}) collective-permute-start(bf16[128,1024]{1,0:T(8,128)(2,1)} %refs_0_.3), channel_id=1, source_target_pairs={{0,32},{32,64},{64,96},{96,128},{128,160},{160,192},{192,224},{224... | collective-permute-start | bytes 786440 | tf_op jit(solution)/shard_map/ppermute | solution.py:286
  19.5 9.9 %collective-permute-start.1 = (bf16[128,1024]{1,0:T(8,128)(2,1)}, bf16[128,1024]{1,0:T(8,128)(2,1)S(1)}, u32[]{:S(2)}, u32[]{:S(2)}) collective-permute-start(bf16[128,1024]{1,0:T(8,128)(2,1)} %refs_0_.3), channel_id=1, source_target_pairs={{0,224},{32,0},{64,32},{96,64},{128,96},{160,128},{192,160},{224,1... | collective-permute-start | bytes 786440 | tf_op jit(solution)/shard_map/ppermute | solution.py:286
  29.4 40.7 %copy-start.1 = (bf16[128,1024]{1,0:T(8,128)(2,1)}, bf16[128,1024]{1,0:T(8,128)(2,1)S(1)}, u32[]{:S(2)}) copy-start(bf16[128,1024]{1,0:T(8,128)(2,1)S(1)} %collective-permute-done.refs_1_) | copy-start | bytes 786436
  29.4 7.5 %collective-permute-start.2 = (bf16[128,1024]{1,0:T(8,128)(2,1)S(1)}, bf16[128,1024]{1,0:T(8,128)(2,1)S(1)}, u32[]{:S(2)}, u32[]{:S(2)}) collective-permute-start(bf16[128,1024]{1,0:T(8,128)(2,1)S(1)} %collective-permute-done.refs_1_), channel_id=1, source_target_pairs={{0,32},{32,64},{64,96},{96,128},{128,160},{160,192},{192,224},{224... | collective-permute-start | bytes 786440 | tf_op jit(solution)/shard_map/ppermute | solution.py:286
  29.4 40.7 %copy-start.2 = (bf16[128,1024]{1,0:T(8,128)(2,1)}, bf16[128,1024]{1,0:T(8,128)(2,1)S(1)}, u32[]{:S(2)}) copy-start(bf16[128,1024]{1,0:T(8,128)(2,1)S(1)} %collective-permute-done.1.refs_2_) | copy-start | bytes 786436
  29.4 7.4 %collective-permute-start.3 = (bf16[128,1024]{1,0:T(8,128)(2,1)S(1)}, bf16[128,1024]{1,0:T(8,128)(2,1)S(1)}, u32[]{:S(2)}, u32[]{:S(2)}) collective-permute-start(bf16[128,1024]{1,0:T(8,128)(2,1)S(1)} %collective-permute-done.1.refs_2_), channel_id=1, source_target_pairs={{0,224},{32,0},{64,32},{96,64},{128,96},{160,128},{192,160},{224,1... | collective-permute-start | bytes 786440 | tf_op jit(solution)/shard_map/ppermute | solution.py:286
  36.9 33.3 %copy-start.3 = (bf16[128,1024]{1,0:T(8,128)(2,1)}, bf16[128,1024]{1,0:T(8,128)(2,1)S(1)}, u32[]{:S(2)}) copy-start(bf16[128,1024]{1,0:T(8,128)(2,1)S(1)} %collective-permute-done.2.refs_3_) | copy-start | bytes 786436
  36.9 33.3 %copy-start.4 = (bf16[128,1024]{1,0:T(8,128)(2,1)}, bf16[128,1024]{1,0:T(8,128)(2,1)S(1)}, u32[]{:S(2)}) copy-start(bf16[128,1024]{1,0:T(8,128)(2,1)S(1)} %collective-permute-done.3.refs_4_) | copy-start | bytes 786436
  56.5 13.4 %collective-permute-start.4 = (bf16[192,1024]{1,0:T(8,128)(2,1)S(1)}, bf16[192,1024]{1,0:T(8,128)(2,1)}, u32[]{:S(2)}, u32[]{:S(2)}) collective-permute-start(bf16[192,1024]{1,0:T(8,128)(2,1)S(1)} %get-tuple-element.22), channel_id=1, source_target_pairs={{0,64},{32,96},{64,128},{96,160},{128,192},{160,224},{192,0},{224,... | collective-permute-start | bytes 1179656 | tf_op jit(solution)/shard_map/ppermute | solution.py:286
  57.0 13.2 %collective-permute-start.5 = (bf16[192,1024]{1,0:T(8,128)(2,1)S(1)}, bf16[192,1024]{1,0:T(8,128)(2,1)}, u32[]{:S(2)}, u32[]{:S(2)}) collective-permute-start(bf16[192,1024]{1,0:T(8,128)(2,1)S(1)} %get-tuple-element.23), channel_id=1, source_target_pairs={{0,192},{32,224},{64,0},{96,32},{128,64},{160,96},{192,128},{224,1... | collective-permute-start | bytes 1179656 | tf_op jit(solution)/shard_map/ppermute | solution.py:286
  60.1 23.2 %all-to-all-start.2 = ((f32[16,72,256]{2,1,0:T(8,128)}), f32[16,72,256]{2,1,0:T(8,128)S(1)}, u32[]{:S(2)}, u32[]{:S(2)}) async-start(f32[16,72,256]{2,1,0:T(8,128)} %bitcast.7), calls=%async_computation.2 | async-start | bytes 2359296 | tf_op jit(solution)/shard_map/all_to_all | solution.py:305
  74.1 11.8 %collective-permute-start.6 = (bf16[4,128,1024]{2,1,0:T(8,128)(2,1)}, bf16[4,128,1024]{2,1,0:T(8,128)(2,1)S(1)}, u32[]{:S(2)}, u32[]{:S(2)}) collective-permute-start(bf16[4,128,1024]{2,1,0:T(8,128)(2,1)} %get-tuple-element.24), channel_id=1, source_target_pairs={{0,1},{1,0},{2,3},{3,2},{4,5},{5,4},{6,7},{7,6},{8,9},{9,8},{10,11... | collective-permute-start | bytes 3145736 | tf_op jit(solution)/shard_map/ppermute | solution.py:359
  85.8 0.6 copy-start.5
  93.4 18.1 %copy-start = (bf16[4,128,1024]{2,1,0:T(8,128)(2,1)S(1)}, bf16[4,128,1024]{2,1,0:T(8,128)(2,1)}, u32[]{:S(2)}) copy-start(bf16[4,128,1024]{2,1,0:T(8,128)(2,1)} %get-tuple-element.29) | copy-start | bytes 3145732
  93.4 6.3 %collective-permute-start.7 = (f32[16,64,256]{2,1,0:T(8,128)S(1)}, f32[16,64,256]{2,1,0:T(8,128)S(1)}, u32[]{:S(2)}, u32[]{:S(2)}) collective-permute-start(f32[16,64,256]{2,1,0:T(8,128)S(1)} %get-tuple-element.26), channel_id=1, source_target_pairs={{0,1},{1,0},{2,3},{3,2},{4,5},{5,4},{6,7},{7,6},{8,9},{9,8},{10,11... | collective-permute-start | bytes 3145736 | tf_op jit(solution)/shard_map/ppermute | solution.py:390
  102.2 9.3 %collective-permute-start.8 = (bf16[2048,1024]{1,0:T(8,128)(2,1)}, bf16[2048,1024]{1,0:T(8,128)(2,1)}, u32[]{:S(2)}, u32[]{:S(2)}) collective-permute-start(bf16[2048,1024]{1,0:T(8,128)(2,1)} %get-tuple-element.28.own_ref), channel_id=1, source_target_pairs={{0,1},{1,0},{2,3},{3,2},{4,5},{5,4},{6,7},{7,6},{8,9},{9,8},{10,11... | collective-permute-start | bytes 12582920 | tf_op jit(solution)/shard_map/ppermute | solution.py:418
  102.6 19.4 %all-to-all-start.3 = ((f32[16,16,256]{2,1,0:T(8,128)}), f32[16,16,256]{2,1,0:T(8,128)S(1)}, u32[]{:S(2)}, u32[]{:S(2)}) async-start(f32[16,16,256]{2,1,0:T(8,128)} %bitcast.13), calls=%async_computation.3 | async-start | bytes 524288 | tf_op jit(solution)/shard_map/all_to_all | solution.py:305
  110.3 1.2 collective-permute-start.9
  122.7 12.7 %all-to-all-start.4 = ((f32[16,16,256]{2,1,0:T(8,128)}), f32[16,16,256]{2,1,0:T(8,128)S(1)}, u32[]{:S(2)}, u32[]{:S(2)}) async-start(f32[16,16,256]{2,1,0:T(8,128)} %bitcast.15), calls=%async_computation.4 | async-start | bytes 524288 | tf_op jit(solution)/shard_map/all_to_all | solution.py:305
Sparse Core Ops, SparseCore 0:
  10.4 64.5 all-gather.1

commit v5 on v4

--- a/solution.py
+++ b/solution.py
@@ -119,7 +119,7 @@
 
 
 def sketch_kernel(
-    pieces, vox_total, pos_ref, maps_ref, w_ref, _, kept_ref, sent_ref, mean_ref, centered_ref, parts
+    pieces, vox_total, maps_ref, w_ref, _, kept_ref, sent_ref, mean_ref, centered_ref, parts
 ):
     rows = w_ref.shape[0] // pieces
     width = rows - PAD
@@ -141,24 +141,25 @@
     count, half = kept_ref.shape[0], kept_ref.shape[1]
     split = total.reshape(count, 2, half, total.shape[1])
 
-    @pl.when(pos_ref[0] == 0)
+    @pl.when(lax.axis_index("vox") == 0)
     def _():
         kept_ref[...] = split[:, 0]
         sent_ref[...] = split[:, 1]
 
-    @pl.when(pos_ref[0] == 1)
+    @pl.when(lax.axis_index("vox") == 1)
     def _():
         kept_ref[...] = split[:, 1]
         sent_ref[...] = split[:, 0]
 
 
-def sort_kernel(places, pos_ref, *refs):
-    pieces, kept_ref, sent_ref = refs[:-2], refs[-2], refs[-1]
+def sort_kernel(places, *refs):
+    pieces, (kept_ref, sent_ref, done_ref) = refs[:-3], refs[-3:]
+    done_ref[...] = jnp.zeros(done_ref.shape, F32)
     groups = kept_ref.shape[0]
     total = 2 * groups
     for index, source, rows, shift, target in places:
-        group = lax.rem(pos_ref[2] + (shift + total), total)
-        mine = group // groups == pos_ref[0]
+        group = lax.rem(lax.axis_index("row") + (shift + total), total)
+        mine = group // groups == lax.axis_index("vox")
         place = lax.rem(group, groups)
         piece = pieces[index]
 
@@ -171,14 +172,14 @@
             sent_ref[place, target : target + rows, :] = piece[source : source + rows, :]
 
 
-def cross_kernel(subjects, copies, pos_ref, kept_ref, got_ref, _, out_ref, own_ref, __, full):
+def cross_kernel(subjects, copies, kept_ref, got_ref, _, __, out_ref, own_ref, ___, ____, full):
     sketch = kept_ref[...] + got_ref[...]
     groups, half, cols = sketch.shape
     flat = sketch.reshape(groups * half, cols)
     full[...] = lax.dot_general(
         flat, flat, (((0,), (0,)), ((), ())), precision=HIGHEST, preferred_element_type=F32
     ) * (1.0 / subjects)
-    col = pos_ref[1]
+    col = lax.axis_index("col")
     rows = out_ref.shape[0] // copies
     piece = full[pl.ds(pl.multiple_of(col * rows, rows), rows), :]
     for k in range(copies):
@@ -296,9 +297,6 @@
     vox_total = vox_half * vox_count
     block_rows = sub_rows * col_count
     groups = row_count // vox_count
-    col_pos = lax.axis_index("col")
-    vox_pos = lax.axis_index("vox")
-    pos = jnp.stack([vox_pos, col_pos, lax.axis_index("row")]).astype(jnp.int32)
     swap = [(0, 1), (1, 0)]
 
     def exchange(value, axis):
@@ -344,41 +342,34 @@
     places = [(k, 0, sub_rows, shift, 0) for k, shift in enumerate((0, -1, 1, -2, 2, -3, 3))]
     places += [(5, sub_rows, half_block, -4, 0), (6, sub_rows, half_block, 4, half_block)]
     group_shape = (groups, sub_rows, vox_half)
-    whole_block = pl.BlockSpec(group_shape, lambda i, p: (0, 0, 0))
-    col_kept, col_sent = pl.pallas_call(
+    whole_block = pl.BlockSpec(group_shape, lambda i: (0, 0, 0))
+    col_kept, col_sent, sorted_blocks = pl.pallas_call(
         functools.partial(sort_kernel, places),
-        grid_spec=pltpu.PrefetchScalarGridSpec(
-            num_scalar_prefetch=1,
-            grid=(1,),
-            in_specs=[pl.BlockSpec(piece.shape, lambda i, p: (0, 0)) for piece in ring],
-            out_specs=[whole_block, whole_block],
-        ),
-        out_shape=[sd(group_shape, BF16)] * 2,
+        grid=(1,),
+        in_specs=[pl.BlockSpec(piece.shape, lambda i: (0, 0)) for piece in ring],
+        out_specs=[whole_block, whole_block, pl.BlockSpec((8, 128), lambda i: (0, 0))],
+        out_shape=[sd(group_shape, BF16), sd(group_shape, BF16), sd((8, 128))],
         compiler_params=ALL,
-    )(pos, *ring)
-    col_other = lax.ppermute(col_sent, "vox", swap)
+    )(*ring)
 
     half_rows = sub_rows // vox_count
     step = min(4 * sub_rows, block_rows)
-    half_spec = pl.BlockSpec((step // sub_rows, half_rows, width), lambda i, p: (i, 0, 0))
+    half_spec = pl.BlockSpec((step // sub_rows, half_rows, width), lambda i: (i, 0, 0))
     kept, sent, mean, centered = pl.pallas_call(
         functools.partial(sketch_kernel, col_count, vox_total),
-        grid_spec=pltpu.PrefetchScalarGridSpec(
-            num_scalar_prefetch=1,
-            grid=(block_rows // step,),
-            in_specs=[
-                pl.BlockSpec((step, vox_half), lambda i, p: (i, 0)),
-                pl.BlockSpec((col_count * slice_rows, width), lambda i, p: (0, 0)),
-                pl.BlockSpec(memory_space=pl.ANY),
-            ],
-            out_specs=[
-                half_spec,
-                half_spec,
-                pl.BlockSpec((1, vox_half), lambda i, p: (0, 0)),
-                pl.BlockSpec((step, vox_half), lambda i, p: (i, 0)),
-            ],
-            scratch_shapes=[pltpu.VMEM((2, vox_half, width), BF16)],
-        ),
+        grid=(block_rows // step,),
+        in_specs=[
+            pl.BlockSpec((step, vox_half), lambda i: (i, 0)),
+            pl.BlockSpec((col_count * slice_rows, width), lambda i: (0, 0)),
+            pl.BlockSpec(memory_space=pl.ANY),
+        ],
+        out_specs=[
+            half_spec,
+            half_spec,
+            pl.BlockSpec((1, vox_half), lambda i: (0, 0)),
+            pl.BlockSpec((step, vox_half), lambda i: (i, 0)),
+        ],
+        scratch_shapes=[pltpu.VMEM((2, vox_half, width), BF16)],
         out_shape=[
             sd((col_count, half_rows, width)),
             sd((col_count, half_rows, width)),
@@ -386,36 +377,37 @@
             sd((block_rows, vox_half), BF16),
         ],
         compiler_params=LARGE,
-    )(pos, row_maps, weights, col_other)
+    )(row_maps, weights, sorted_blocks)
     got = lax.ppermute(sent, "vox", swap)
     cross_rows = width // col_count
     copies = row_count * vox_count
-    slices, own, centered = pl.pallas_call(
+    slices, own, centered, col_sent = pl.pallas_call(
         functools.partial(cross_kernel, subjects, copies),
-        grid_spec=pltpu.PrefetchScalarGridSpec(
-            num_scalar_prefetch=1,
-            grid=(1,),
-            in_specs=[
-                pl.BlockSpec((col_count, half_rows, width), lambda i, p: (0, 0, 0)),
-                pl.BlockSpec((col_count, half_rows, width), lambda i, p: (0, 0, 0)),
-                pl.BlockSpec(memory_space=pl.ANY),
-            ],
-            out_specs=[
-                pl.BlockSpec((copies * cross_rows, width), lambda i, p: (0, 0)),
-                pl.BlockSpec((half_rows, width), lambda i, p: (0, 0)),
-                pl.BlockSpec(memory_space=pl.ANY),
-            ],
-            scratch_shapes=[pltpu.VMEM((width, width), F32)],
-        ),
+        grid=(1,),
+        in_specs=[
+            pl.BlockSpec((col_count, half_rows, width), lambda i: (0, 0, 0)),
+            pl.BlockSpec((col_count, half_rows, width), lambda i: (0, 0, 0)),
+            pl.BlockSpec(memory_space=pl.ANY),
+            pl.BlockSpec(memory_space=pl.ANY),
+        ],
+        out_specs=[
+            pl.BlockSpec((copies * cross_rows, width), lambda i: (0, 0)),
+            pl.BlockSpec((half_rows, width), lambda i: (0, 0)),
+            pl.BlockSpec(memory_space=pl.ANY),
+            pl.BlockSpec(memory_space=pl.ANY),
+        ],
+        scratch_shapes=[pltpu.VMEM((width, width), F32)],
         out_shape=[
             sd((copies * cross_rows, width)),
             sd((half_rows, width)),
             sd((block_rows, vox_half), BF16),
-        ],
-        input_output_aliases={3: 2},
-        compiler_params=PARAMS,
-    )(pos, kept, got, centered)
+            sd(group_shape, BF16),
+        ],
+        input_output_aliases={2: 2, 3: 3},
+        compiler_params=LARGE,
+    )(kept, got, centered, col_sent)
     other = lax.ppermute(centered, "vox", swap)
+    col_other = lax.ppermute(col_sent, "vox", swap)
     means = jnp.concatenate([mean, lax.ppermute(mean, "vox", swap)], axis=0)
     own_cols = groups * sub_rows
     flat = (own_cols, vox_half)

time: 151 us -> 151 us (level)
  waiting for transfers between devices: 25.9 us -> 37.6 us
  starting transfers between devices: 54.1 us -> 44.7 us
  Pallas kernels: 36.8 us -> 34.3 us
    ppermute x6, waiting for transfers between devices: 10.8 us -> 26.2 us  [ring_step(): return (lax.ppermute(up, axis, ahead), lax.ppermute(down, axis, back))]
    ppermute x1, starting transfers between devices: 9.28 us -> 0.13 us  [shards(): col_other = lax.ppermute(col_sent, 'vox', swap)]
    ppermute x1, waiting for transfers between devices: 2.49 us -> 0.01 us  [shards(): col_other = lax.ppermute(col_sent, 'vox', swap)]
    all_to_all x4, waiting for transfers between devices: 8.74 us -> 6.59 us  [exchange(): return lax.all_to_all(value, axis, 0, 0, tiled=True)]
    pallas_call x2, Pallas kernels: 6.38 us -> 4.39 us  [the longest x1 3.16 us: shards(): pl.pallas_call(functools.partial(sort_kernel, places), grid=(1,), in_spec...]
    ppermute x1, starting transfers between devices: 4.03 us -> 2.06 us  [shards(): got = lax.ppermute(sent, 'vox', swap)]
    all_to_all x4, starting transfers between devices: 28 us -> 29.6 us  [exchange(): return lax.all_to_all(value, axis, 0, 0, tiled=True)]
  transfers between devices with their start and end apart: 15 -> 15, of which waited for: 8 -> 9; matrix products, arithmetic and copies ran while one was open for 0% -> 0% of each run, Pallas kernels for 12% -> 12%
where the time goes in v5:
time: 151 us
  starting transfers between devices  44.7 us (30%)
  waiting for transfers between devices  37.6 us (25%)
  Pallas kernels  34.3 us (23%)
  blocking collectives  18.4 us (12%)
  between operations  14.2 us (9%)
  local copies, waits for them, and re-layouts  1.62 us (1%)
    all_to_all x4, starting transfers between devices, exchange(): return lax.all_to_all(value, axis, 0, 0, tiled=True)  29.6 us
    ppermute x6, waiting for transfers between devices, ring_step(): return (lax.ppermute(up, axis, ahead), lax.ppermute(down, axis, back))  26.2 us
    all_to_all x1, blocking collectives, exchange(): return lax.all_to_all(value, axis, 0, 0, tiled=True)  18.4 us
    pallas_call x5, Pallas kernels, call(): pl.pallas_call(body, out_shape=[*out_shape, *[sd(x.shape, x.dtype) for x...  12.6 us
    ppermute x6, starting transfers between devices, ring_step(): return (lax.ppermute(up, axis, ahead), lax.ppermute(down, axis, back))  12.1 us
    pallas_call x2, Pallas kernels, gram_part(): pl.pallas_call(functools.partial(gram_kernel, vox_total), grid=(steps,),...  10.9 us
    all_to_all x4, waiting for transfers between devices, exchange(): return lax.all_to_all(value, axis, 0, 0, tiled=True)  6.59 us
    pallas_call x1, Pallas kernels, shards(): pl.pallas_call(functools.partial(sketch_kernel, col_count, vox_total), gr...  6.42 us
  transfers between devices with their start and end apart: 15, of which 9 were waited for; matrix products, arithmetic and copies ran while one was open for 0% of the time, Pallas kernels for 12%

profile of v5, /device:TPU:1, one launch (start us, length us, event | category | flops | bytes accessed | tf_op | source)
XLA Modules:
  0.0 150.8 jit_solution(9601221990583067367)
XLA Ops:
  7.9 2.3 %shard_map.49 = f32[1152,256]{1,0:T(8,128)} custom-call(bf16[128,1024]{1,0:T(8,128)(2,1)} %refs_0_.3, bf16[128,256]{1,0:T(8,128)(2,1)} %refs_1_.1), custom_call_target="tpu_custom_call" | custom-call | tf_op jit(solution)/shard_map/pallas_call | solution.py:28
  10.2 7.6 %all-to-all-start = ((f32[16,72,256]{2,1,0:T(8,128)}), f32[16,72,256]{2,1,0:T(8,128)S(1)}, u32[]{:S(2)}, u32[]{:S(2)}) async-start(f32[16,72,256]{2,1,0:T(8,128)} %bitcast.26), calls=%async_computation | async-start | bytes 2359296 | tf_op jit(solution)/shard_map/all_to_all | solution.py:303
  17.8 1.7 %collective-permute-start = (bf16[128,1024]{1,0:T(8,128)(2,1)}, bf16[128,1024]{1,0:T(8,128)(2,1)S(1)}, u32[]{:S(2)}, u32[]{:S(2)}) collective-permute-start(bf16[128,1024]{1,0:T(8,128)(2,1)} %refs_0_.3), channel_id=1, source_target_pairs={{0,32},{32,64},{64,96},{96,128},{128,160},{160,192},{192,224},{224... | collective-permute-start | bytes 786440 | tf_op jit(solution)/shard_map/ppermute | solution.py:287
  19.5 4.0 %collective-permute-start.1 = (bf16[128,1024]{1,0:T(8,128)(2,1)}, bf16[128,1024]{1,0:T(8,128)(2,1)S(1)}, u32[]{:S(2)}, u32[]{:S(2)}) collective-permute-start(bf16[128,1024]{1,0:T(8,128)(2,1)} %refs_0_.3), channel_id=1, source_target_pairs={{0,224},{32,0},{64,32},{96,64},{128,96},{160,128},{192,160},{224,1... | collective-permute-start | bytes 786440 | tf_op jit(solution)/shard_map/ppermute | solution.py:287
  23.6 5.8 %collective-permute-done.refs_1_ = bf16[128,1024]{1,0:T(8,128)(2,1)S(1)} collective-permute-done((bf16[128,1024]{1,0:T(8,128)(2,1)}, bf16[128,1024]{1,0:T(8,128)(2,1)S(1)}, u32[]{:S(2)}, u32[]{:S(2)}) %collective-permute-start) | collective-permute-done | bytes 262176 | tf_op jit(solution)/shard_map/ppermute | solution.py:287
  29.4 2.7 %collective-permute-start.3 = (bf16[128,1024]{1,0:T(8,128)(2,1)S(1)}, bf16[128,1024]{1,0:T(8,128)(2,1)S(1)}, u32[]{:S(2)}, u32[]{:S(2)}) collective-permute-start(bf16[128,1024]{1,0:T(8,128)(2,1)S(1)} %collective-permute-done.1.refs_2_), channel_id=1, source_target_pairs={{0,224},{32,0},{64,32},{96,64},{128,96},{160,128},{192,160},{224,1... | collective-permute-start | bytes 786440 | tf_op jit(solution)/shard_map/ppermute | solution.py:287
  32.1 4.8 %collective-permute-done.2.refs_3_ = bf16[128,1024]{1,0:T(8,128)(2,1)S(1)} collective-permute-done((bf16[128,1024]{1,0:T(8,128)(2,1)S(1)}, bf16[128,1024]{1,0:T(8,128)(2,1)S(1)}, u32[]{:S(2)}, u32[]{:S(2)}) %collective-permute-start.2) | collective-permute-done | bytes 262176 | tf_op jit(solution)/shard_map/ppermute | solution.py:287
  37.0 18.4 %all_to_all.55 = f32[8,72,256]{2,1,0:T(8,128)S(1)} all-to-all(f32[8,72,256]{2,1,0:T(8,128)S(1)} %bitcast.22), channel_id=1, replica_groups=mesh['row'=8,'col'=16,'vox'=2] {'row'}, dimensions={0} | all-to-all | bytes 1179648 | tf_op jit(solution)/shard_map/all_to_all | solution.py:303
  56.5 9.2 %all-to-all-start.2 = ((f32[16,72,256]{2,1,0:T(8,128)}), f32[16,72,256]{2,1,0:T(8,128)S(1)}, u32[]{:S(2)}, u32[]{:S(2)}) async-start(f32[16,72,256]{2,1,0:T(8,128)} %bitcast.4), calls=%async_computation.2 | async-start | bytes 2359296 | tf_op jit(solution)/shard_map/all_to_all | solution.py:303
  66.1 3.3 %collective-permute-start.5 = (bf16[192,1024]{1,0:T(8,128)(2,1)S(1)}, bf16[192,1024]{1,0:T(8,128)(2,1)S(1)}, u32[]{:S(2)}, u32[]{:S(2)}) collective-permute-start(bf16[192,1024]{1,0:T(8,128)(2,1)S(1)} %get-tuple-element.25), channel_id=1, source_target_pairs={{0,192},{32,224},{64,0},{96,32},{128,64},{160,96},{192,128},{224,1... | collective-permute-start | bytes 1179656 | tf_op jit(solution)/shard_map/ppermute | solution.py:287
  69.4 13.1 %collective-permute-done.4.refs_5_ = bf16[192,1024]{1,0:T(8,128)(2,1)S(1)} collective-permute-done((bf16[192,1024]{1,0:T(8,128)(2,1)S(1)}, bf16[192,1024]{1,0:T(8,128)(2,1)S(1)}, u32[]{:S(2)}, u32[]{:S(2)}) %collective-permute-start.4) | collective-permute-done | bytes 393248 | tf_op jit(solution)/shard_map/ppermute | solution.py:287
  82.5 2.6 %collective-permute-done.5.refs_6_ = bf16[192,1024]{1,0:T(8,128)(2,1)S(1)} collective-permute-done((bf16[192,1024]{1,0:T(8,128)(2,1)S(1)}, bf16[192,1024]{1,0:T(8,128)(2,1)S(1)}, u32[]{:S(2)}, u32[]{:S(2)}) %collective-permute-start.5) | collective-permute-done | bytes 393248 | tf_op jit(solution)/shard_map/ppermute | solution.py:287
  85.8 3.2 %shard_map.52 = (bf16[4,128,1024]{2,1,0:T(8,128)(2,1)}, bf16[4,128,1024]{2,1,0:T(8,128)(2,1)}, f32[8,128]{1,0:T(8,128)}) custom-call(bf16[128,1024]{1,0:T(8,128)(2,1)} %refs_0_.3, bf16[128,1024]{1,0:T(8,128)(2,1)} %copy-done.1, bf16[128,1024]{1,0:T(8,128)(2,1)} %copy-done.2, bf16[128,1024]{1,0:T(8,128)(2,1)} %copy-done.3, bf16[128,1024]{1,0:T(8,128)(2,1)} %copy-done.4, ...), custom_call_target="tpu_custom_call" | custom-call | tf_op jit(solution)/shard_map/pallas_call | solution.py:346
  89.7 6.4 %shard_map.53 = (f32[16,64,256]{2,1,0:T(8,128)S(1)}, f32[16,64,256]{2,1,0:T(8,128)S(1)}, f32[1,1024]{1,0:T(1,128)S(1)}, bf16[2048,1024]{1,0:T(8,128)(2,1)}) custom-call(bf16[2048,1024]{1,0:T(8,128)(2,1)} %all-gather.2.cloned.1.call-done.maps_ref, f32[1152,256]{1,0:T(8,128)S(1)} %bitcast.15, f32[8,128]{1,0:T(8,128)S(1)} %copy-done.7), custom_call_target="tpu_custom_call" | custom-call | tf_op jit(solution)/shard_map/pallas_call | solution.py:358
  96.2 2.1 %collective-permute-start.6 = (f32[16,64,256]{2,1,0:T(8,128)S(1)}, f32[16,64,256]{2,1,0:T(8,128)S(1)}, u32[]{:S(2)}, u32[]{:S(2)}) collective-permute-start(f32[16,64,256]{2,1,0:T(8,128)S(1)} %get-tuple-element.28), channel_id=1, source_target_pairs={{0,1},{1,0},{2,3},{3,2},{4,5},{5,4},{6,7},{7,6},{8,9},{9,8},{10,11... | collective-permute-start | bytes 3145736 | tf_op jit(solution)/shard_map/ppermute | solution.py:381
  98.2 2.3 %collective-permute-done.6.got_ref = f32[16,64,256]{2,1,0:T(8,128)S(1)} collective-permute-done((f32[16,64,256]{2,1,0:T(8,128)S(1)}, f32[16,64,256]{2,1,0:T(8,128)S(1)}, u32[]{:S(2)}, u32[]{:S(2)}) %collective-permute-start.6) | collective-permute-done | bytes 1048608 | tf_op jit(solution)/shard_map/ppermute | solution.py:381
  102.5 6.2 %all-to-all-start.3 = ((f32[16,16,256]{2,1,0:T(8,128)}), f32[16,16,256]{2,1,0:T(8,128)S(1)}, u32[]{:S(2)}, u32[]{:S(2)}) async-start(f32[16,16,256]{2,1,0:T(8,128)} %bitcast.25), calls=%async_computation.3 | async-start | bytes 524288 | tf_op jit(solution)/shard_map/all_to_all | solution.py:303
  109.0 1.5 collective-permute-done.9
  110.9 5.4 %shard_map.55 = (f32[8192,128]{1,0:T(8,128)}, f32[8,128]{1,0:T(8,128)S(1)}) custom-call(bf16[2048,1024]{1,0:T(8,128)(2,1)} %get-tuple-element.31.own_ref, bf16[2048,1024]{1,0:T(8,128)(2,1)} %collective-permute-done.7.other_ref, bf16[512,1024]{1,0:T(8,128)(2,1)S(1)} %bitcast.17, bf16[512,1024]{1,0:T(8,128)(2,1)S(1)} %bitcast.19, ...), custom_call_target="tpu_custom_call" | custom-call | tf_op jit(solution)/shard_map/pallas_call | solution.py:262
  116.3 4.1 %all-to-all-done.3 = f32[16,16,256]{2,1,0:T(8,128)S(1)} async-done(((f32[16,16,256]{2,1,0:T(8,128)}), f32[16,16,256]{2,1,0:T(8,128)S(1)}, u32[]{:S(2)}, u32[]{:S(2)}) %all-to-all-start.3) | async-done | bytes 262176 | tf_op jit(solution)/shard_map/all_to_all | solution.py:303
  121.1 6.6 %all-to-all-start.4 = ((f32[16,16,256]{2,1,0:T(8,128)}), f32[16,16,256]{2,1,0:T(8,128)S(1)}, u32[]{:S(2)}, u32[]{:S(2)}) async-start(f32[16,16,256]{2,1,0:T(8,128)} %bitcast.12), calls=%async_computation.4 | async-start | bytes 524288 | tf_op jit(solution)/shard_map/all_to_all | solution.py:303
  127.7 5.5 %shard_map.56 = (f32[8192,128]{1,0:T(8,128)}, f32[8,128]{1,0:T(8,128)S(1)}) custom-call(bf16[2048,1024]{1,0:T(8,128)(2,1)} %get-tuple-element.31.own_ref, bf16[2048,1024]{1,0:T(8,128)(2,1)} %collective-permute-done.7.other_ref, bf16[512,1024]{1,0:T(8,128)(2,1)S(1)} %bitcast.18, bf16[512,1024]{1,0:T(8,128)(2,1)S(1)} %bitcast.20, ...), custom_call_target="tpu_custom_call", output_to_operand_aliasing={{0}: (5, {})} | custom-call | tf_op jit(solution)/shard_map/pallas_call | solution.py:262
  133.2 2.5 %all-to-all-done.4 = f32[16,16,256]{2,1,0:T(8,128)S(1)} async-done(((f32[16,16,256]{2,1,0:T(8,128)}), f32[16,16,256]{2,1,0:T(8,128)S(1)}, u32[]{:S(2)}, u32[]{:S(2)}) %all-to-all-start.4) | async-done | bytes 262176 | tf_op jit(solution)/shard_map/all_to_all | solution.py:303
  135.7 8.3 %shard_map.58 = (f32[256,256]{1,0:T(8,128)}, f32[64,256]{1,0:T(8,128)}) custom-call(f32[256,256]{1,0:T(8,128)S(1)} %bitcast.24, f32[64,256]{1,0:T(8,128)S(1)} %get-tuple-element.39.refs_1_, f32[8,128]{1,0:T(8,128)S(1)} %get-tuple-element.40.refs_2_), custom_call_target="tpu_custom_call" | custom-call | tf_op jit(solution)/shard_map/pallas_call | solution.py:28
  (39 shorter events, 7.2 us)
Async XLA Ops:
  7.2 81.8 %all-gather.2.cloned.1.call-start = ((), (), s32[]{:S(2)}) async-start(), calls=%async_computation.5 | async-start | bytes 4456448 | tf_op jit(solution)/shard_map/all_gather | solution.py:305
  10.2 26.7 %all-to-all-start = ((f32[16,72,256]{2,1,0:T(8,128)}), f32[16,72,256]{2,1,0:T(8,128)S(1)}, u32[]{:S(2)}, u32[]{:S(2)}) async-start(f32[16,72,256]{2,1,0:T(8,128)} %bitcast.26), calls=%async_computation | async-start | bytes 2359296 | tf_op jit(solution)/shard_map/all_to_all | solution.py:303
  17.8 11.6 %collective-permute-start = (bf16[128,1024]{1,0:T(8,128)(2,1)}, bf16[128,1024]{1,0:T(8,128)(2,1)S(1)}, u32[]{:S(2)}, u32[]{:S(2)}) collective-permute-start(bf16[128,1024]{1,0:T(8,128)(2,1)} %refs_0_.3), channel_id=1, source_target_pairs={{0,32},{32,64},{64,96},{96,128},{128,160},{160,192},{192,224},{224... | collective-permute-start | bytes 786440 | tf_op jit(solution)/shard_map/ppermute | solution.py:287
  19.5 9.9 %collective-permute-start.1 = (bf16[128,1024]{1,0:T(8,128)(2,1)}, bf16[128,1024]{1,0:T(8,128)(2,1)S(1)}, u32[]{:S(2)}, u32[]{:S(2)}) collective-permute-start(bf16[128,1024]{1,0:T(8,128)(2,1)} %refs_0_.3), channel_id=1, source_target_pairs={{0,224},{32,0},{64,32},{96,64},{128,96},{160,128},{192,160},{224,1... | collective-permute-start | bytes 786440 | tf_op jit(solution)/shard_map/ppermute | solution.py:287
  29.4 55.6 %copy-start.1 = (bf16[128,1024]{1,0:T(8,128)(2,1)}, bf16[128,1024]{1,0:T(8,128)(2,1)S(1)}, u32[]{:S(2)}) copy-start(bf16[128,1024]{1,0:T(8,128)(2,1)S(1)} %collective-permute-done.refs_1_) | copy-start | bytes 786436
  29.4 7.5 %collective-permute-start.2 = (bf16[128,1024]{1,0:T(8,128)(2,1)S(1)}, bf16[128,1024]{1,0:T(8,128)(2,1)S(1)}, u32[]{:S(2)}, u32[]{:S(2)}) collective-permute-start(bf16[128,1024]{1,0:T(8,128)(2,1)S(1)} %collective-permute-done.refs_1_), channel_id=1, source_target_pairs={{0,32},{32,64},{64,96},{96,128},{128,160},{160,192},{192,224},{224... | collective-permute-start | bytes 786440 | tf_op jit(solution)/shard_map/ppermute | solution.py:287
  29.4 55.6 %copy-start.2 = (bf16[128,1024]{1,0:T(8,128)(2,1)}, bf16[128,1024]{1,0:T(8,128)(2,1)S(1)}, u32[]{:S(2)}) copy-start(bf16[128,1024]{1,0:T(8,128)(2,1)S(1)} %collective-permute-done.1.refs_2_) | copy-start | bytes 786436
  29.4 7.4 %collective-permute-start.3 = (bf16[128,1024]{1,0:T(8,128)(2,1)S(1)}, bf16[128,1024]{1,0:T(8,128)(2,1)S(1)}, u32[]{:S(2)}, u32[]{:S(2)}) collective-permute-start(bf16[128,1024]{1,0:T(8,128)(2,1)S(1)} %collective-permute-done.1.refs_2_), channel_id=1, source_target_pairs={{0,224},{32,0},{64,32},{96,64},{128,96},{160,128},{192,160},{224,1... | collective-permute-start | bytes 786440 | tf_op jit(solution)/shard_map/ppermute | solution.py:287
  36.9 48.1 %copy-start.3 = (bf16[128,1024]{1,0:T(8,128)(2,1)}, bf16[128,1024]{1,0:T(8,128)(2,1)S(1)}, u32[]{:S(2)}) copy-start(bf16[128,1024]{1,0:T(8,128)(2,1)S(1)} %collective-permute-done.2.refs_3_) | copy-start | bytes 786436
  36.9 48.1 %copy-start.4 = (bf16[128,1024]{1,0:T(8,128)(2,1)}, bf16[128,1024]{1,0:T(8,128)(2,1)S(1)}, u32[]{:S(2)}) copy-start(bf16[128,1024]{1,0:T(8,128)(2,1)S(1)} %collective-permute-done.3.refs_4_) | copy-start | bytes 786436
  56.5 32.4 %all-to-all-start.2 = ((f32[16,72,256]{2,1,0:T(8,128)}), f32[16,72,256]{2,1,0:T(8,128)S(1)}, u32[]{:S(2)}, u32[]{:S(2)}) async-start(f32[16,72,256]{2,1,0:T(8,128)} %bitcast.4), calls=%async_computation.2 | async-start | bytes 2359296 | tf_op jit(solution)/shard_map/all_to_all | solution.py:303
  65.7 16.7 %collective-permute-start.4 = (bf16[192,1024]{1,0:T(8,128)(2,1)S(1)}, bf16[192,1024]{1,0:T(8,128)(2,1)S(1)}, u32[]{:S(2)}, u32[]{:S(2)}) collective-permute-start(bf16[192,1024]{1,0:T(8,128)(2,1)S(1)} %get-tuple-element.24), channel_id=1, source_target_pairs={{0,64},{32,96},{64,128},{96,160},{128,192},{160,224},{192,0},{224,... | collective-permute-start | bytes 1179656 | tf_op jit(solution)/shard_map/ppermute | solution.py:287
  66.1 18.9 %collective-permute-start.5 = (bf16[192,1024]{1,0:T(8,128)(2,1)S(1)}, bf16[192,1024]{1,0:T(8,128)(2,1)S(1)}, u32[]{:S(2)}, u32[]{:S(2)}) collective-permute-start(bf16[192,1024]{1,0:T(8,128)(2,1)S(1)} %get-tuple-element.25), channel_id=1, source_target_pairs={{0,192},{32,224},{64,0},{96,32},{128,64},{160,96},{192,128},{224,1... | collective-permute-start | bytes 1179656 | tf_op jit(solution)/shard_map/ppermute | solution.py:287
  82.4 2.6 %copy-start.8 = (bf16[192,1024]{1,0:T(8,128)(2,1)}, bf16[192,1024]{1,0:T(8,128)(2,1)S(1)}, u32[]{:S(2)}) copy-start(bf16[192,1024]{1,0:T(8,128)(2,1)S(1)} %collective-permute-done.4.refs_5_) | copy-start | bytes 1179652
  85.0 0.7 copy-start.9
  88.9 11.6 %copy-start.5 = (bf16[4,128,1024]{2,1,0:T(8,128)(2,1)S(1)}, bf16[4,128,1024]{2,1,0:T(8,128)(2,1)}, u32[]{:S(2)}) copy-start(bf16[4,128,1024]{2,1,0:T(8,128)(2,1)} %get-tuple-element.30.__) | copy-start | bytes 3145732
  89.0 0.8 copy-start.7
  96.2 14.7 %copy-start = (bf16[4,128,1024]{2,1,0:T(8,128)(2,1)S(1)}, bf16[4,128,1024]{2,1,0:T(8,128)(2,1)}, u32[]{:S(2)}) copy-start(bf16[4,128,1024]{2,1,0:T(8,128)(2,1)} %get-tuple-element.32) | copy-start | bytes 3145732
  96.2 4.3 %collective-permute-start.6 = (f32[16,64,256]{2,1,0:T(8,128)S(1)}, f32[16,64,256]{2,1,0:T(8,128)S(1)}, u32[]{:S(2)}, u32[]{:S(2)}) collective-permute-start(f32[16,64,256]{2,1,0:T(8,128)S(1)} %get-tuple-element.28), channel_id=1, source_target_pairs={{0,1},{1,0},{2,3},{3,2},{4,5},{5,4},{6,7},{7,6},{8,9},{9,8},{10,11... | collective-permute-start | bytes 3145736 | tf_op jit(solution)/shard_map/ppermute | solution.py:381
  101.8 9.1 %collective-permute-start.7 = (bf16[2048,1024]{1,0:T(8,128)(2,1)}, bf16[2048,1024]{1,0:T(8,128)(2,1)}, u32[]{:S(2)}, u32[]{:S(2)}) collective-permute-start(bf16[2048,1024]{1,0:T(8,128)(2,1)} %get-tuple-element.31.own_ref), channel_id=1, source_target_pairs={{0,1},{1,0},{2,3},{3,2},{4,5},{5,4},{6,7},{7,6},{8,9},{9,8},{10,11... | collective-permute-start | bytes 12582920 | tf_op jit(solution)/shard_map/ppermute | solution.py:409
  102.2 8.3 %collective-permute-start.8 = (bf16[4,128,1024]{2,1,0:T(8,128)(2,1)S(1)}, bf16[4,128,1024]{2,1,0:T(8,128)(2,1)S(1)}, u32[]{:S(2)}, u32[]{:S(2)}) collective-permute-start(bf16[4,128,1024]{2,1,0:T(8,128)(2,1)S(1)} %get-tuple-element.33), channel_id=1, source_target_pairs={{0,1},{1,0},{2,3},{3,2},{4,5},{5,4},{6,7},{7,6},{8,9},{9,8},{10,11... | collective-permute-start | bytes 3145736 | tf_op jit(solution)/shard_map/ppermute | solution.py:410
  102.5 17.9 %all-to-all-start.3 = ((f32[16,16,256]{2,1,0:T(8,128)}), f32[16,16,256]{2,1,0:T(8,128)S(1)}, u32[]{:S(2)}, u32[]{:S(2)}) async-start(f32[16,16,256]{2,1,0:T(8,128)} %bitcast.25), calls=%async_computation.3 | async-start | bytes 524288 | tf_op jit(solution)/shard_map/all_to_all | solution.py:303
  108.7 1.9 %collective-permute-start.9 = (f32[1,1024]{1,0:T(1,128)S(1)}, f32[1,1024]{1,0:T(1,128)S(1)}, u32[]{:S(2)}, u32[]{:S(2)}) collective-permute-start(f32[1,1024]{1,0:T(1,128)S(1)} %get-tuple-element.34), channel_id=1, source_target_pairs={{0,1},{1,0},{2,3},{3,2},{4,5},{5,4},{6,7},{7,6},{8,9},{9,8},{10,11... | collective-permute-start | bytes 12296 | tf_op jit(solution)/shard_map/ppermute | solution.py:411
  121.1 14.6 %all-to-all-start.4 = ((f32[16,16,256]{2,1,0:T(8,128)}), f32[16,16,256]{2,1,0:T(8,128)S(1)}, u32[]{:S(2)}, u32[]{:S(2)}) async-start(f32[16,16,256]{2,1,0:T(8,128)} %bitcast.12), calls=%async_computation.4 | async-start | bytes 524288 | tf_op jit(solution)/shard_map/all_to_all | solution.py:303
  (1 other events, 0.7 us)
Sparse Core Ops, SparseCore 0:
  10.4 69.1 all-gather.1

commit v6 on v5

--- a/solution.py
+++ b/solution.py
@@ -13,6 +13,7 @@
 PAD = 8
 PARAMS = pltpu.CompilerParams(vmem_limit_bytes=24 * 1024 * 1024)
 LARGE = pltpu.CompilerParams(vmem_limit_bytes=48 * 1024 * 1024)
+SORT = pltpu.CompilerParams(vmem_limit_bytes=50 * 1024 * 1024)
 ALL = pltpu.CompilerParams(vmem_limit_bytes=58 * 1024 * 1024)
 
 
@@ -72,25 +73,7 @@
         out_ref[k * rows : (k + 1) * rows, :] = total
 
 
-def centre_kernel(
-    sources,
-    copies,
-    subjects,
-    in_ref,
-    up1_ref,
-    down1_ref,
-    up2_ref,
-    down2_ref,
-    out_ref,
-    up_ref,
-    down_ref,
-):
-    sub_rows = up1_ref.shape[0]
-    half_block = sub_rows // 2
-    up_ref[:sub_rows, :] = up1_ref[...]
-    up_ref[sub_rows:, :] = up2_ref[:half_block, :]
-    down_ref[:sub_rows, :] = down1_ref[...]
-    down_ref[sub_rows:, :] = down2_ref[half_block:, :]
+def centre_kernel(sources, copies, subjects, in_ref, out_ref):
     rows = in_ref.shape[0] // sources
     width = rows - PAD
     total = in_ref[0:rows, :]
@@ -326,21 +309,18 @@
         after=[up1, down1, up2, down2],
     )
     half_block = sub_rows // 2
-    far_block = (sub_rows + half_block, vox_half)
-    whole, up, down = call(
+    whole, up2, down2 = call(
         functools.partial(centre_kernel, row_count, col_count, subjects),
-        [sd((col_count * slice_rows, width)), sd(far_block, BF16), sd(far_block, BF16)],
+        [sd((col_count * slice_rows, width))],
         exchange(part, "row"),
-        up1,
-        down1,
-        up2,
-        down2,
+        carry=[up2, down2],
     )
     weights = exchange(whole, "col")
-    up3, down3 = ring_step(up, down, "row", row_count, 2)
-    ring = [maps, up1, down1, up2, down2, up3, down3]
+    up3, down3 = ring_step(up2, down2, "row", row_count)
+    up4, down4 = ring_step(up2[:half_block], down2[half_block:], "row", row_count, 2)
+    ring = [maps, up1, down1, up2, down2, up3, down3, up4, down4]
     places = [(k, 0, sub_rows, shift, 0) for k, shift in enumerate((0, -1, 1, -2, 2, -3, 3))]
-    places += [(5, sub_rows, half_block, -4, 0), (6, sub_rows, half_block, 4, half_block)]
+    places += [(7, 0, half_block, -4, 0), (8, 0, half_block, 4, half_block)]
     group_shape = (groups, sub_rows, vox_half)
     whole_block = pl.BlockSpec(group_shape, lambda i: (0, 0, 0))
     col_kept, col_sent, sorted_blocks = pl.pallas_call(
@@ -349,7 +329,7 @@
         in_specs=[pl.BlockSpec(piece.shape, lambda i: (0, 0)) for piece in ring],
         out_specs=[whole_block, whole_block, pl.BlockSpec((8, 128), lambda i: (0, 0))],
         out_shape=[sd(group_shape, BF16), sd(group_shape, BF16), sd((8, 128))],
-        compiler_params=ALL,
+        compiler_params=SORT,
     )(*ring)
 
     half_rows = sub_rows // vox_count

time: 151 us -> 148 us (0.980)
  Pallas kernels: 34.3 us -> 32 us
  waiting for transfers between devices: 37.6 us -> 35.5 us
  starting transfers between devices: 44.7 us -> 46.6 us
    ppermute x6 -> x8, waiting for transfers between devices: 26.2 us -> 16.2 us  [ring_step(): return (lax.ppermute(up, axis, ahead), lax.ppermute(down, axis, back))]
    all_to_all x4, waiting for transfers between devices: 6.59 us -> 15.1 us  [exchange(): return lax.all_to_all(value, axis, 0, 0, tiled=True)]
    ppermute x6 -> x8, starting transfers between devices: 12.1 us -> 14.8 us  [ring_step(): return (lax.ppermute(up, axis, ahead), lax.ppermute(down, axis, back))]
    all_to_all x4, starting transfers between devices: 29.6 us -> 27.1 us  [exchange(): return lax.all_to_all(value, axis, 0, 0, tiled=True)]
    pallas_call x1, Pallas kernels: 3.16 us -> 1.32 us  [shards(): pl.pallas_call(functools.partial(sort_kernel, places), grid=(1,), in_spec...]
    ppermute x1, starting transfers between devices: 2.06 us -> 3.73 us  [shards(): got = lax.ppermute(sent, 'vox', swap)]
  transfers between devices with their start and end apart: 15 -> 17, of which waited for: 9 -> 9; matrix products, arithmetic and copies ran while one was open for 0% -> 0% of each run, Pallas kernels for 12% -> 10%
where the time goes in v6:
time: 148 us
  starting transfers between devices  46.6 us (31%)
  waiting for transfers between devices  35.5 us (24%)
  Pallas kernels  32 us (22%)
  blocking collectives  18.3 us (12%)
  between operations  14.1 us (10%)
    all_to_all x4, starting transfers between devices, exchange(): return lax.all_to_all(value, axis, 0, 0, tiled=True)  27.1 us
    all_to_all x1, blocking collectives, exchange(): return lax.all_to_all(value, axis, 0, 0, tiled=True)  18.3 us
    ppermute x8, waiting for transfers between devices, ring_step(): return (lax.ppermute(up, axis, ahead), lax.ppermute(down, axis, back))  16.2 us
    all_to_all x4, waiting for transfers between devices, exchange(): return lax.all_to_all(value, axis, 0, 0, tiled=True)  15.1 us
    ppermute x8, starting transfers between devices, ring_step(): return (lax.ppermute(up, axis, ahead), lax.ppermute(down, axis, back))  14.8 us
    pallas_call x5, Pallas kernels, call(): pl.pallas_call(body, out_shape=[*out_shape, *[sd(x.shape, x.dtype) for x...  11.5 us
    pallas_call x2, Pallas kernels, gram_part(): pl.pallas_call(functools.partial(gram_kernel, vox_total), grid=(steps,),...  10.9 us
    pallas_call x1, Pallas kernels, shards(): pl.pallas_call(functools.partial(sketch_kernel, col_count, vox_total), gr...  6.31 us
  transfers between devices with their start and end apart: 17, of which 9 were waited for; matrix products, arithmetic and copies ran while one was open for 0% of the time, Pallas kernels for 10%

profile of v6, /device:TPU:1, one launch (start us, length us, event | category | flops | bytes accessed | tf_op | source)
XLA Modules:
  0.0 147.6 jit_solution(15139273148188528614)
XLA Ops:
  7.9 2.3 %shard_map.49 = f32[1152,256]{1,0:T(8,128)} custom-call(bf16[128,1024]{1,0:T(8,128)(2,1)} %refs_0_.3, bf16[128,256]{1,0:T(8,128)(2,1)} %refs_1_.1), custom_call_target="tpu_custom_call" | custom-call | tf_op jit(solution)/shard_map/pallas_call | solution.py:29
  10.2 7.6 %all-to-all-start = ((f32[16,72,256]{2,1,0:T(8,128)}), f32[16,72,256]{2,1,0:T(8,128)S(1)}, u32[]{:S(2)}, u32[]{:S(2)}) async-start(f32[16,72,256]{2,1,0:T(8,128)} %bitcast.26), calls=%async_computation | async-start | bytes 2359296 | tf_op jit(solution)/shard_map/all_to_all | solution.py:286
  17.8 1.7 %collective-permute-start = (bf16[128,1024]{1,0:T(8,128)(2,1)}, bf16[128,1024]{1,0:T(8,128)(2,1)S(1)}, u32[]{:S(2)}, u32[]{:S(2)}) collective-permute-start(bf16[128,1024]{1,0:T(8,128)(2,1)} %refs_0_.3), channel_id=1, source_target_pairs={{0,32},{32,64},{64,96},{96,128},{128,160},{160,192},{192,224},{224... | collective-permute-start | bytes 786440 | tf_op jit(solution)/shard_map/ppermute | solution.py:270
  19.5 4.0 %collective-permute-start.1 = (bf16[128,1024]{1,0:T(8,128)(2,1)}, bf16[128,1024]{1,0:T(8,128)(2,1)S(1)}, u32[]{:S(2)}, u32[]{:S(2)}) collective-permute-start(bf16[128,1024]{1,0:T(8,128)(2,1)} %refs_0_.3), channel_id=1, source_target_pairs={{0,224},{32,0},{64,32},{96,64},{128,96},{160,128},{192,160},{224,1... | collective-permute-start | bytes 786440 | tf_op jit(solution)/shard_map/ppermute | solution.py:270
  23.6 5.8 %collective-permute-done.refs_1_ = bf16[128,1024]{1,0:T(8,128)(2,1)S(1)} collective-permute-done((bf16[128,1024]{1,0:T(8,128)(2,1)}, bf16[128,1024]{1,0:T(8,128)(2,1)S(1)}, u32[]{:S(2)}, u32[]{:S(2)}) %collective-permute-start) | collective-permute-done | bytes 262176 | tf_op jit(solution)/shard_map/ppermute | solution.py:270
  29.4 2.7 %collective-permute-start.3 = (bf16[128,1024]{1,0:T(8,128)(2,1)S(1)}, bf16[128,1024]{1,0:T(8,128)(2,1)S(1)}, u32[]{:S(2)}, u32[]{:S(2)}) collective-permute-start(bf16[128,1024]{1,0:T(8,128)(2,1)S(1)} %collective-permute-done.1.refs_2_), channel_id=1, source_target_pairs={{0,224},{32,0},{64,32},{96,64},{128,96},{160,128},{192,160},{224,1... | collective-permute-start | bytes 786440 | tf_op jit(solution)/shard_map/ppermute | solution.py:270
  32.1 4.9 %collective-permute-done.2.refs_3_.refs_1_ = bf16[128,1024]{1,0:T(8,128)(2,1)S(1)} collective-permute-done((bf16[128,1024]{1,0:T(8,128)(2,1)S(1)}, bf16[128,1024]{1,0:T(8,128)(2,1)S(1)}, u32[]{:S(2)}, u32[]{:S(2)}) %collective-permute-start.2) | collective-permute-done | bytes 262176 | tf_op jit(solution)/shard_map/ppermute | solution.py:270
  37.1 18.3 %all_to_all.55 = f32[8,72,256]{2,1,0:T(8,128)S(1)} all-to-all(f32[8,72,256]{2,1,0:T(8,128)S(1)} %bitcast.22), channel_id=1, replica_groups=mesh['row'=8,'col'=16,'vox'=2] {'row'}, dimensions={0} | all-to-all | bytes 1179648 | tf_op jit(solution)/shard_map/all_to_all | solution.py:286
  56.5 9.2 %all-to-all-start.2 = ((f32[16,72,256]{2,1,0:T(8,128)}), f32[16,72,256]{2,1,0:T(8,128)S(1)}, u32[]{:S(2)}, u32[]{:S(2)}) async-start(f32[16,72,256]{2,1,0:T(8,128)} %bitcast.23), calls=%async_computation.2 | async-start | bytes 2359296 | tf_op jit(solution)/shard_map/all_to_all | solution.py:286
  65.8 2.7 %collective-permute-start.5 = (bf16[128,1024]{1,0:T(8,128)(2,1)S(1)}, bf16[128,1024]{1,0:T(8,128)(2,1)S(1)}, u32[]{:S(2)}, u32[]{:S(2)}) collective-permute-start(bf16[128,1024]{1,0:T(8,128)(2,1)S(1)} %get-tuple-element.25.refs_4_), channel_id=1, source_target_pairs={{0,224},{32,0},{64,32},{96,64},{128,96},{160,128},{192,160},{224,1... | collective-permute-start | bytes 786440 | tf_op jit(solution)/shard_map/ppermute | solution.py:270
  68.6 3.6 %collective-permute-start.7 = (bf16[64,1024]{1,0:T(8,128)(2,1)S(1)}, bf16[64,1024]{1,0:T(8,128)(2,1)S(1)}, u32[]{:S(2)}, u32[]{:S(2)}) collective-permute-start(bf16[64,1024]{1,0:T(8,128)(2,1)S(1)} %slice.7), channel_id=1, source_target_pairs={{0,192},{32,224},{64,0},{96,32},{128,64},{160,96},{192,128},{224,1... | collective-permute-start | bytes 393224 | tf_op jit(solution)/shard_map/ppermute | solution.py:270
  72.2 5.4 %collective-permute-done.6.refs_7_ = bf16[64,1024]{1,0:T(8,128)(2,1)S(1)} collective-permute-done((bf16[64,1024]{1,0:T(8,128)(2,1)S(1)}, bf16[64,1024]{1,0:T(8,128)(2,1)S(1)}, u32[]{:S(2)}, u32[]{:S(2)}) %collective-permute-start.6) | collective-permute-done | bytes 131104 | tf_op jit(solution)/shard_map/ppermute | solution.py:270
  79.0 7.5 %all-to-all-done.2 = f32[16,72,256]{2,1,0:T(8,128)S(1)} async-done(((f32[16,72,256]{2,1,0:T(8,128)}), f32[16,72,256]{2,1,0:T(8,128)S(1)}, u32[]{:S(2)}, u32[]{:S(2)}) %all-to-all-start.2) | async-done | bytes 1179680 | tf_op jit(solution)/shard_map/all_to_all | solution.py:286
  86.4 6.3 %shard_map.53 = (f32[16,64,256]{2,1,0:T(8,128)S(1)}, f32[16,64,256]{2,1,0:T(8,128)S(1)}, f32[1,1024]{1,0:T(1,128)S(1)}, bf16[2048,1024]{1,0:T(8,128)(2,1)}) custom-call(bf16[2048,1024]{1,0:T(8,128)(2,1)} %all-gather.2.cloned.1.call-done.maps_ref, f32[1152,256]{1,0:T(8,128)S(1)} %bitcast.15, f32[8,128]{1,0:T(8,128)S(1)} %get-tuple-element.26._), custom_call_target="tpu_custom_call" | custom-call | tf_op jit(solution)/shard_map/pallas_call | solution.py:338
  92.8 3.7 %collective-permute-start.8 = (f32[16,64,256]{2,1,0:T(8,128)S(1)}, f32[16,64,256]{2,1,0:T(8,128)S(1)}, u32[]{:S(2)}, u32[]{:S(2)}) collective-permute-start(f32[16,64,256]{2,1,0:T(8,128)S(1)} %get-tuple-element.28), channel_id=1, source_target_pairs={{0,1},{1,0},{2,3},{3,2},{4,5},{5,4},{6,7},{7,6},{8,9},{9,8},{10,11... | collective-permute-start | bytes 3145736 | tf_op jit(solution)/shard_map/ppermute | solution.py:361
  96.5 2.3 %collective-permute-done.8.got_ref = f32[16,64,256]{2,1,0:T(8,128)S(1)} collective-permute-done((f32[16,64,256]{2,1,0:T(8,128)S(1)}, f32[16,64,256]{2,1,0:T(8,128)S(1)}, u32[]{:S(2)}, u32[]{:S(2)}) %collective-permute-start.8) | collective-permute-done | bytes 1048608 | tf_op jit(solution)/shard_map/ppermute | solution.py:361
  98.8 1.9 %shard_map.54 = (f32[256,256]{1,0:T(8,128)}, f32[64,256]{1,0:T(8,128)S(1)}, bf16[2048,1024]{1,0:T(8,128)(2,1)}, bf16[4,128,1024]{2,1,0:T(8,128)(2,1)}) custom-call(f32[16,64,256]{2,1,0:T(8,128)S(1)} %get-tuple-element.27.kept_ref, f32[16,64,256]{2,1,0:T(8,128)S(1)} %collective-permute-done.8.got_ref, ...), custom_call_target="tpu_custom_call", output_to_operand_aliasing={{2}: (2, {}), {3}: (3, {})} | custom-call | tf_op jit(solution)/shard_map/pallas_call | solution.py:364
  101.2 6.8 %all-to-all-start.3 = ((f32[16,16,256]{2,1,0:T(8,128)}), f32[16,16,256]{2,1,0:T(8,128)S(1)}, u32[]{:S(2)}, u32[]{:S(2)}) async-start(f32[16,16,256]{2,1,0:T(8,128)} %bitcast.10), calls=%async_computation.3 | async-start | bytes 524288 | tf_op jit(solution)/shard_map/all_to_all | solution.py:286
  109.7 5.4 %shard_map.55 = (f32[8192,128]{1,0:T(8,128)}, f32[8,128]{1,0:T(8,128)S(1)}) custom-call(bf16[2048,1024]{1,0:T(8,128)(2,1)} %get-tuple-element.31.own_ref, bf16[2048,1024]{1,0:T(8,128)(2,1)} %collective-permute-done.9.other_ref, bf16[512,1024]{1,0:T(8,128)(2,1)S(1)} %bitcast.17, bf16[512,1024]{1,0:T(8,128)(2,1)S(1)} %bitcast.19, ...), custom_call_target="tpu_custom_call" | custom-call | tf_op jit(solution)/shard_map/pallas_call | solution.py:245
  115.1 4.6 %all-to-all-done.3 = f32[16,16,256]{2,1,0:T(8,128)S(1)} async-done(((f32[16,16,256]{2,1,0:T(8,128)}), f32[16,16,256]{2,1,0:T(8,128)S(1)}, u32[]{:S(2)}, u32[]{:S(2)}) %all-to-all-start.3) | async-done | bytes 262176 | tf_op jit(solution)/shard_map/all_to_all | solution.py:286
  120.5 3.5 %all-to-all-start.4 = ((f32[16,16,256]{2,1,0:T(8,128)}), f32[16,16,256]{2,1,0:T(8,128)S(1)}, u32[]{:S(2)}, u32[]{:S(2)}) async-start(f32[16,16,256]{2,1,0:T(8,128)} %bitcast.12), calls=%async_computation.4 | async-start | bytes 524288 | tf_op jit(solution)/shard_map/all_to_all | solution.py:286
  124.0 5.5 %shard_map.56 = (f32[8192,128]{1,0:T(8,128)}, f32[8,128]{1,0:T(8,128)S(1)}) custom-call(bf16[2048,1024]{1,0:T(8,128)(2,1)} %get-tuple-element.31.own_ref, bf16[2048,1024]{1,0:T(8,128)(2,1)} %collective-permute-done.9.other_ref, bf16[512,1024]{1,0:T(8,128)(2,1)S(1)} %bitcast.18, bf16[512,1024]{1,0:T(8,128)(2,1)S(1)} %bitcast.20, ...), custom_call_target="tpu_custom_call", output_to_operand_aliasing={{0}: (5, {})} | custom-call | tf_op jit(solution)/shard_map/pallas_call | solution.py:245
  129.5 3.0 %all-to-all-done.4 = f32[16,16,256]{2,1,0:T(8,128)S(1)} async-done(((f32[16,16,256]{2,1,0:T(8,128)}), f32[16,16,256]{2,1,0:T(8,128)S(1)}, u32[]{:S(2)}, u32[]{:S(2)}) %all-to-all-start.4) | async-done | bytes 262176 | tf_op jit(solution)/shard_map/all_to_all | solution.py:286
  132.5 8.3 %shard_map.58 = (f32[256,256]{1,0:T(8,128)}, f32[64,256]{1,0:T(8,128)}) custom-call(f32[256,256]{1,0:T(8,128)S(1)} %bitcast.25, f32[64,256]{1,0:T(8,128)S(1)} %get-tuple-element.39.refs_1_, f32[8,128]{1,0:T(8,128)S(1)} %get-tuple-element.40.refs_2_), custom_call_target="tpu_custom_call" | custom-call | tf_op jit(solution)/shard_map/pallas_call | solution.py:29
  (29 shorter events, 6.4 us)
Async XLA Ops:
  7.2 79.3 %all-gather.2.cloned.1.call-start = ((), (), s32[]{:S(2)}) async-start(), calls=%async_computation.5 | async-start | bytes 4456448 | tf_op jit(solution)/shard_map/all_gather | solution.py:288
  10.2 26.8 %all-to-all-start = ((f32[16,72,256]{2,1,0:T(8,128)}), f32[16,72,256]{2,1,0:T(8,128)S(1)}, u32[]{:S(2)}, u32[]{:S(2)}) async-start(f32[16,72,256]{2,1,0:T(8,128)} %bitcast.26), calls=%async_computation | async-start | bytes 2359296 | tf_op jit(solution)/shard_map/all_to_all | solution.py:286
  17.8 59.8 %copy-start = (bf16[128,1024]{1,0:T(8,128)(2,1)S(1)}, bf16[128,1024]{1,0:T(8,128)(2,1)}, u32[]{:S(2)}) copy-start(bf16[128,1024]{1,0:T(8,128)(2,1)} %refs_0_.3) | copy-start | bytes 786436
  17.8 11.6 %collective-permute-start = (bf16[128,1024]{1,0:T(8,128)(2,1)}, bf16[128,1024]{1,0:T(8,128)(2,1)S(1)}, u32[]{:S(2)}, u32[]{:S(2)}) collective-permute-start(bf16[128,1024]{1,0:T(8,128)(2,1)} %refs_0_.3), channel_id=1, source_target_pairs={{0,32},{32,64},{64,96},{96,128},{128,160},{160,192},{192,224},{224... | collective-permute-start | bytes 786440 | tf_op jit(solution)/shard_map/ppermute | solution.py:270
  19.5 9.9 %collective-permute-start.1 = (bf16[128,1024]{1,0:T(8,128)(2,1)}, bf16[128,1024]{1,0:T(8,128)(2,1)S(1)}, u32[]{:S(2)}, u32[]{:S(2)}) collective-permute-start(bf16[128,1024]{1,0:T(8,128)(2,1)} %refs_0_.3), channel_id=1, source_target_pairs={{0,224},{32,0},{64,32},{96,64},{128,96},{160,128},{192,160},{224,1... | collective-permute-start | bytes 786440 | tf_op jit(solution)/shard_map/ppermute | solution.py:270
  29.4 7.6 %collective-permute-start.2 = (bf16[128,1024]{1,0:T(8,128)(2,1)S(1)}, bf16[128,1024]{1,0:T(8,128)(2,1)S(1)}, u32[]{:S(2)}, u32[]{:S(2)}) collective-permute-start(bf16[128,1024]{1,0:T(8,128)(2,1)S(1)} %collective-permute-done.refs_1_), channel_id=1, source_target_pairs={{0,32},{32,64},{64,96},{96,128},{128,160},{160,192},{192,224},{224... | collective-permute-start | bytes 786440 | tf_op jit(solution)/shard_map/ppermute | solution.py:270
  29.4 7.6 %collective-permute-start.3 = (bf16[128,1024]{1,0:T(8,128)(2,1)S(1)}, bf16[128,1024]{1,0:T(8,128)(2,1)S(1)}, u32[]{:S(2)}, u32[]{:S(2)}) collective-permute-start(bf16[128,1024]{1,0:T(8,128)(2,1)S(1)} %collective-permute-done.1.refs_2_), channel_id=1, source_target_pairs={{0,224},{32,0},{64,32},{96,64},{128,96},{160,128},{192,160},{224,1... | collective-permute-start | bytes 786440 | tf_op jit(solution)/shard_map/ppermute | solution.py:270
  55.5 1.0 copy-start.1
  56.5 29.9 %all-to-all-start.2 = ((f32[16,72,256]{2,1,0:T(8,128)}), f32[16,72,256]{2,1,0:T(8,128)S(1)}, u32[]{:S(2)}, u32[]{:S(2)}) async-start(f32[16,72,256]{2,1,0:T(8,128)} %bitcast.23), calls=%async_computation.2 | async-start | bytes 2359296 | tf_op jit(solution)/shard_map/all_to_all | solution.py:286
  65.7 11.9 %collective-permute-start.4 = (bf16[128,1024]{1,0:T(8,128)(2,1)S(1)}, bf16[128,1024]{1,0:T(8,128)(2,1)S(1)}, u32[]{:S(2)}, u32[]{:S(2)}) collective-permute-start(bf16[128,1024]{1,0:T(8,128)(2,1)S(1)} %get-tuple-element.24.refs_3_), channel_id=1, source_target_pairs={{0,32},{32,64},{64,96},{96,128},{128,160},{160,192},{192,224},{224... | collective-permute-start | bytes 786440 | tf_op jit(solution)/shard_map/ppermute | solution.py:270
  65.8 11.8 %collective-permute-start.5 = (bf16[128,1024]{1,0:T(8,128)(2,1)S(1)}, bf16[128,1024]{1,0:T(8,128)(2,1)S(1)}, u32[]{:S(2)}, u32[]{:S(2)}) collective-permute-start(bf16[128,1024]{1,0:T(8,128)(2,1)S(1)} %get-tuple-element.25.refs_4_), channel_id=1, source_target_pairs={{0,224},{32,0},{64,32},{96,64},{128,96},{160,128},{192,160},{224,1... | collective-permute-start | bytes 786440 | tf_op jit(solution)/shard_map/ppermute | solution.py:270
  68.5 9.1 %collective-permute-start.6 = (bf16[64,1024]{1,0:T(8,128)(2,1)S(1)}, bf16[64,1024]{1,0:T(8,128)(2,1)S(1)}, u32[]{:S(2)}, u32[]{:S(2)}) collective-permute-start(bf16[64,1024]{1,0:T(8,128)(2,1)S(1)} %slice.6), channel_id=1, source_target_pairs={{0,64},{32,96},{64,128},{96,160},{128,192},{160,224},{192,0},{224,... | collective-permute-start | bytes 393224 | tf_op jit(solution)/shard_map/ppermute | solution.py:270
  68.6 9.0 %collective-permute-start.7 = (bf16[64,1024]{1,0:T(8,128)(2,1)S(1)}, bf16[64,1024]{1,0:T(8,128)(2,1)S(1)}, u32[]{:S(2)}, u32[]{:S(2)}) collective-permute-start(bf16[64,1024]{1,0:T(8,128)(2,1)S(1)} %slice.7), channel_id=1, source_target_pairs={{0,192},{32,224},{64,0},{96,32},{128,64},{160,96},{192,128},{224,1... | collective-permute-start | bytes 393224 | tf_op jit(solution)/shard_map/ppermute | solution.py:270
  92.8 6.0 %collective-permute-start.8 = (f32[16,64,256]{2,1,0:T(8,128)S(1)}, f32[16,64,256]{2,1,0:T(8,128)S(1)}, u32[]{:S(2)}, u32[]{:S(2)}) collective-permute-start(f32[16,64,256]{2,1,0:T(8,128)S(1)} %get-tuple-element.28), channel_id=1, source_target_pairs={{0,1},{1,0},{2,3},{3,2},{4,5},{5,4},{6,7},{7,6},{8,9},{9,8},{10,11... | collective-permute-start | bytes 3145736 | tf_op jit(solution)/shard_map/ppermute | solution.py:361
  100.7 9.0 %collective-permute-start.9 = (bf16[2048,1024]{1,0:T(8,128)(2,1)}, bf16[2048,1024]{1,0:T(8,128)(2,1)}, u32[]{:S(2)}, u32[]{:S(2)}) collective-permute-start(bf16[2048,1024]{1,0:T(8,128)(2,1)} %get-tuple-element.31.own_ref), channel_id=1, source_target_pairs={{0,1},{1,0},{2,3},{3,2},{4,5},{5,4},{6,7},{7,6},{8,9},{9,8},{10,11... | collective-permute-start | bytes 12582920 | tf_op jit(solution)/shard_map/ppermute | solution.py:389
  101.1 8.3 %collective-permute-start.10 = (bf16[4,128,1024]{2,1,0:T(8,128)(2,1)}, bf16[4,128,1024]{2,1,0:T(8,128)(2,1)S(1)}, u32[]{:S(2)}, u32[]{:S(2)}) collective-permute-start(bf16[4,128,1024]{2,1,0:T(8,128)(2,1)} %get-tuple-element.33), channel_id=1, source_target_pairs={{0,1},{1,0},{2,3},{3,2},{4,5},{5,4},{6,7},{7,6},{8,9},{9,8},{10,11... | collective-permute-start | bytes 3145736 | tf_op jit(solution)/shard_map/ppermute | solution.py:390
  101.2 18.5 %all-to-all-start.3 = ((f32[16,16,256]{2,1,0:T(8,128)}), f32[16,16,256]{2,1,0:T(8,128)S(1)}, u32[]{:S(2)}, u32[]{:S(2)}) async-start(f32[16,16,256]{2,1,0:T(8,128)} %bitcast.10), calls=%async_computation.3 | async-start | bytes 524288 | tf_op jit(solution)/shard_map/all_to_all | solution.py:286
  108.0 1.3 collective-permute-start.11
  120.5 12.0 %all-to-all-start.4 = ((f32[16,16,256]{2,1,0:T(8,128)}), f32[16,16,256]{2,1,0:T(8,128)S(1)}, u32[]{:S(2)}, u32[]{:S(2)}) async-start(f32[16,16,256]{2,1,0:T(8,128)} %bitcast.12), calls=%async_computation.4 | async-start | bytes 524288 | tf_op jit(solution)/shard_map/all_to_all | solution.py:286
Sparse Core Ops, SparseCore 0:
  10.4 69.1 all-gather.1

commit v7 on v6

--- a/solution.py
+++ b/solution.py
@@ -155,7 +155,7 @@
             sent_ref[place, target : target + rows, :] = piece[source : source + rows, :]
 
 
-def cross_kernel(subjects, copies, kept_ref, got_ref, _, __, out_ref, own_ref, ___, ____, full):
+def cross_kernel(subjects, kept_ref, got_ref, mean_ref, _, __, out_ref, own_ref, ___, ____, full):
     sketch = kept_ref[...] + got_ref[...]
     groups, half, cols = sketch.shape
     flat = sketch.reshape(groups * half, cols)
@@ -163,11 +163,24 @@
         flat, flat, (((0,), (0,)), ((), ())), precision=HIGHEST, preferred_element_type=F32
     ) * (1.0 / subjects)
     col = lax.axis_index("col")
-    rows = out_ref.shape[0] // copies
-    piece = full[pl.ds(pl.multiple_of(col * rows, rows), rows), :]
+    rows = out_ref.shape[0] - PAD
+    out_ref[:rows, :] = full[pl.ds(pl.multiple_of(col * rows, rows), rows), :]
+    out_ref[rows:, :] = jnp.zeros((PAD, cols), F32)
+    for k in range(mean_ref.shape[1] // cols):
+        out_ref[rows + k : rows + k + 1, :] = mean_ref[:, k * cols : (k + 1) * cols]
+    own_ref[...] = kept_ref[col] + got_ref[col]
+
+
+def pair_kernel(copies, mine_ref, got_ref, out_ref, means_ref):
+    rows = mine_ref.shape[0] - PAD
+    cols = mine_ref.shape[1]
+    total = mine_ref[:rows, :] + got_ref[:rows, :]
     for k in range(copies):
-        out_ref[k * rows : (k + 1) * rows, :] = piece
-    own_ref[...] = kept_ref[col] + got_ref[col]
+        out_ref[k * rows : (k + 1) * rows, :] = total
+    for n, ref in enumerate((mine_ref, got_ref)):
+        for k in range(means_ref.shape[1] // cols):
+            row = ref[rows + k : rows + k + 1, :]
+            means_ref[n : n + 1, k * cols : (k + 1) * cols] = row
 
 
 def cholesky_kernel(block, cross_ref, own_ref, factor_ref, basis_ref, work):
@@ -360,43 +373,50 @@
     )(row_maps, weights, sorted_blocks)
     got = lax.ppermute(sent, "vox", swap)
     cross_rows = width // col_count
-    copies = row_count * vox_count
+    slice_shape = (cross_rows + PAD, width)
     slices, own, centered, col_sent = pl.pallas_call(
-        functools.partial(cross_kernel, subjects, copies),
+        functools.partial(cross_kernel, subjects),
         grid=(1,),
         in_specs=[
             pl.BlockSpec((col_count, half_rows, width), lambda i: (0, 0, 0)),
             pl.BlockSpec((col_count, half_rows, width), lambda i: (0, 0, 0)),
+            pl.BlockSpec((1, vox_half), lambda i: (0, 0)),
             pl.BlockSpec(memory_space=pl.ANY),
             pl.BlockSpec(memory_space=pl.ANY),
         ],
         out_specs=[
-            pl.BlockSpec((copies * cross_rows, width), lambda i: (0, 0)),
+            pl.BlockSpec(slice_shape, lambda i: (0, 0)),
             pl.BlockSpec((half_rows, width), lambda i: (0, 0)),
             pl.BlockSpec(memory_space=pl.ANY),
             pl.BlockSpec(memory_space=pl.ANY),
         ],
         scratch_shapes=[pltpu.VMEM((width, width), F32)],
         out_shape=[
-            sd((copies * cross_rows, width)),
+            sd(slice_shape),
             sd((half_rows, width)),
             sd((block_rows, vox_half), BF16),
             sd(group_shape, BF16),
         ],
-        input_output_aliases={2: 2, 3: 3},
+        input_output_aliases={3: 2, 4: 3},
         compiler_params=LARGE,
-    )(kept, got, centered, col_sent)
+    )(kept, got, mean, centered, col_sent)
+    shared, means = call(
+        functools.partial(pair_kernel, row_count),
+        [sd((row_count * cross_rows, width)), sd((vox_count, vox_half))],
+        slices,
+        lax.ppermute(slices, "vox", swap),
+    )
+
     other = lax.ppermute(centered, "vox", swap)
     col_other = lax.ppermute(col_sent, "vox", swap)
-    means = jnp.concatenate([mean, lax.ppermute(mean, "vox", swap)], axis=0)
     own_cols = groups * sub_rows
     flat = (own_cols, vox_half)
     operands = (centered, other, col_kept.reshape(flat), col_other.reshape(flat), means)
     gram, first = gram_part(vox_total, groups, 0, None, *operands)
     (summed,) = call(
-        functools.partial(sum_repeat_kernel, copies, col_count),
+        functools.partial(sum_repeat_kernel, row_count, col_count),
         [sd((width, width))],
-        exchange(slices, ("row", "vox")),
+        exchange(shared, "row"),
         after=[first],
     )
     cross = exchange(summed, "col")

time: 148 us -> 150 us (1.014)
  waiting for transfers between devices: 35.5 us -> 39.2 us
  starting transfers between devices: 46.6 us -> 44.8 us
    ppermute x1, waiting for transfers between devices: 0.98 us -> 6.61 us  [shards(): lax.ppermute(slices, 'vox', swap)]
    all_to_all x4, waiting for transfers between devices: 15.1 us -> 12.8 us  [exchange(): return lax.all_to_all(value, axis, 0, 0, tiled=True)]
    pallas_call x5 -> x6, Pallas kernels: 11.5 us -> 12.2 us  [call(): pl.pallas_call(body, out_shape=[*out_shape, *[sd(x.shape, x.dtype) for x...]
where the time goes in v7:
time: 150 us; the launch traced here: 149 us
  starting transfers between devices  44.8 us (30%)
  waiting for transfers between devices  39.2 us (26%)
  Pallas kernels  32 us (21%)
  blocking collectives  18.3 us (12%)
  between operations  14.1 us (9%)
    all_to_all x4, starting transfers between devices, exchange(): return lax.all_to_all(value, axis, 0, 0, tiled=True)  26.4 us
    all_to_all x1, blocking collectives, exchange(): return lax.all_to_all(value, axis, 0, 0, tiled=True)  18.3 us
    ppermute x8, waiting for transfers between devices, ring_step(): return (lax.ppermute(up, axis, ahead), lax.ppermute(down, axis, back))  16.8 us
    ppermute x8, starting transfers between devices, ring_step(): return (lax.ppermute(up, axis, ahead), lax.ppermute(down, axis, back))  13.6 us
    all_to_all x4, waiting for transfers between devices, exchange(): return lax.all_to_all(value, axis, 0, 0, tiled=True)  12.8 us
    pallas_call x6, Pallas kernels, call(): pl.pallas_call(body, out_shape=[*out_shape, *[sd(x.shape, x.dtype) for x...  12.2 us
    pallas_call x2, Pallas kernels, gram_part(): pl.pallas_call(functools.partial(gram_kernel, vox_total), grid=(steps,),...  10.9 us
    ppermute x1, waiting for transfers between devices, shards(): lax.ppermute(slices, 'vox', swap)  6.61 us
  transfers between devices with their start and end apart: 17, of which 9 were waited for; matrix products, arithmetic and copies ran while one was open for 0% of the time, Pallas kernels for 10%

profile of v7, /device:TPU:1, one launch (start us, length us, event | category | flops | bytes accessed | tf_op | source)
XLA Modules:
  0.0 149.5 jit_solution(13112300654352022342)
XLA Ops:
  7.9 2.3 %shard_map.49 = f32[1152,256]{1,0:T(8,128)} custom-call(bf16[128,1024]{1,0:T(8,128)(2,1)} %refs_0_.3, bf16[128,256]{1,0:T(8,128)(2,1)} %refs_1_.1), custom_call_target="tpu_custom_call" | custom-call | tf_op jit(solution)/shard_map/pallas_call | solution.py:29
  10.2 7.6 %all-to-all-start = ((f32[16,72,256]{2,1,0:T(8,128)}), f32[16,72,256]{2,1,0:T(8,128)S(1)}, u32[]{:S(2)}, u32[]{:S(2)}) async-start(f32[16,72,256]{2,1,0:T(8,128)} %bitcast.26), calls=%async_computation | async-start | bytes 2359296 | tf_op jit(solution)/shard_map/all_to_all | solution.py:299
  17.8 1.7 %collective-permute-start = (bf16[128,1024]{1,0:T(8,128)(2,1)}, bf16[128,1024]{1,0:T(8,128)(2,1)S(1)}, u32[]{:S(2)}, u32[]{:S(2)}) collective-permute-start(bf16[128,1024]{1,0:T(8,128)(2,1)} %refs_0_.3), channel_id=1, source_target_pairs={{0,32},{32,64},{64,96},{96,128},{128,160},{160,192},{192,224},{224... | collective-permute-start | bytes 786440 | tf_op jit(solution)/shard_map/ppermute | solution.py:283
  19.5 4.0 %collective-permute-start.1 = (bf16[128,1024]{1,0:T(8,128)(2,1)}, bf16[128,1024]{1,0:T(8,128)(2,1)S(1)}, u32[]{:S(2)}, u32[]{:S(2)}) collective-permute-start(bf16[128,1024]{1,0:T(8,128)(2,1)} %refs_0_.3), channel_id=1, source_target_pairs={{0,224},{32,0},{64,32},{96,64},{128,96},{160,128},{192,160},{224,1... | collective-permute-start | bytes 786440 | tf_op jit(solution)/shard_map/ppermute | solution.py:283
  23.6 5.8 %collective-permute-done.refs_1_ = bf16[128,1024]{1,0:T(8,128)(2,1)S(1)} collective-permute-done((bf16[128,1024]{1,0:T(8,128)(2,1)}, bf16[128,1024]{1,0:T(8,128)(2,1)S(1)}, u32[]{:S(2)}, u32[]{:S(2)}) %collective-permute-start) | collective-permute-done | bytes 262176 | tf_op jit(solution)/shard_map/ppermute | solution.py:283
  29.4 2.7 %collective-permute-start.3 = (bf16[128,1024]{1,0:T(8,128)(2,1)S(1)}, bf16[128,1024]{1,0:T(8,128)(2,1)S(1)}, u32[]{:S(2)}, u32[]{:S(2)}) collective-permute-start(bf16[128,1024]{1,0:T(8,128)(2,1)S(1)} %collective-permute-done.1.refs_2_), channel_id=1, source_target_pairs={{0,224},{32,0},{64,32},{96,64},{128,96},{160,128},{192,160},{224,1... | collective-permute-start | bytes 786440 | tf_op jit(solution)/shard_map/ppermute | solution.py:283
  32.1 4.9 %collective-permute-done.2.refs_3_.refs_1_ = bf16[128,1024]{1,0:T(8,128)(2,1)S(1)} collective-permute-done((bf16[128,1024]{1,0:T(8,128)(2,1)S(1)}, bf16[128,1024]{1,0:T(8,128)(2,1)S(1)}, u32[]{:S(2)}, u32[]{:S(2)}) %collective-permute-start.2) | collective-permute-done | bytes 262176 | tf_op jit(solution)/shard_map/ppermute | solution.py:283
  37.1 18.3 %all_to_all.55 = f32[8,72,256]{2,1,0:T(8,128)S(1)} all-to-all(f32[8,72,256]{2,1,0:T(8,128)S(1)} %bitcast.22), channel_id=1, replica_groups=mesh['row'=8,'col'=16,'vox'=2] {'row'}, dimensions={0} | all-to-all | bytes 1179648 | tf_op jit(solution)/shard_map/all_to_all | solution.py:299
  56.5 9.2 %all-to-all-start.2 = ((f32[16,72,256]{2,1,0:T(8,128)}), f32[16,72,256]{2,1,0:T(8,128)S(1)}, u32[]{:S(2)}, u32[]{:S(2)}) async-start(f32[16,72,256]{2,1,0:T(8,128)} %bitcast.23), calls=%async_computation.2 | async-start | bytes 2359296 | tf_op jit(solution)/shard_map/all_to_all | solution.py:299
  65.8 2.7 %collective-permute-start.5 = (bf16[128,1024]{1,0:T(8,128)(2,1)S(1)}, bf16[128,1024]{1,0:T(8,128)(2,1)S(1)}, u32[]{:S(2)}, u32[]{:S(2)}) collective-permute-start(bf16[128,1024]{1,0:T(8,128)(2,1)S(1)} %get-tuple-element.27.refs_4_), channel_id=1, source_target_pairs={{0,224},{32,0},{64,32},{96,64},{128,96},{160,128},{192,160},{224,1... | collective-permute-start | bytes 786440 | tf_op jit(solution)/shard_map/ppermute | solution.py:283
  68.8 2.2 %collective-permute-start.6 = (bf16[64,1024]{1,0:T(8,128)(2,1)S(1)}, bf16[64,1024]{1,0:T(8,128)(2,1)S(1)}, u32[]{:S(2)}, u32[]{:S(2)}) collective-permute-start(bf16[64,1024]{1,0:T(8,128)(2,1)S(1)} %slice.6), channel_id=1, source_target_pairs={{0,64},{32,96},{64,128},{96,160},{128,192},{160,224},{192,0},{224,... | collective-permute-start | bytes 393224 | tf_op jit(solution)/shard_map/ppermute | solution.py:283
  71.0 4.6 %collective-permute-done.7.refs_8_ = bf16[64,1024]{1,0:T(8,128)(2,1)S(1)} collective-permute-done((bf16[64,1024]{1,0:T(8,128)(2,1)S(1)}, bf16[64,1024]{1,0:T(8,128)(2,1)S(1)}, u32[]{:S(2)}, u32[]{:S(2)}) %collective-permute-start.7) | collective-permute-done | bytes 131104 | tf_op jit(solution)/shard_map/ppermute | solution.py:283
  78.4 8.0 %all-to-all-done.2 = f32[16,72,256]{2,1,0:T(8,128)S(1)} async-done(((f32[16,72,256]{2,1,0:T(8,128)}), f32[16,72,256]{2,1,0:T(8,128)S(1)}, u32[]{:S(2)}, u32[]{:S(2)}) %all-to-all-start.2) | async-done | bytes 1179680 | tf_op jit(solution)/shard_map/all_to_all | solution.py:299
  86.4 6.3 %shard_map.53 = (f32[16,64,256]{2,1,0:T(8,128)S(1)}, f32[16,64,256]{2,1,0:T(8,128)S(1)}, f32[1,1024]{1,0:T(1,128)S(1)}, bf16[2048,1024]{1,0:T(8,128)(2,1)}) custom-call(bf16[2048,1024]{1,0:T(8,128)(2,1)} %all-gather.2.cloned.1.call-done.maps_ref, f32[1152,256]{1,0:T(8,128)S(1)} %bitcast.15, f32[8,128]{1,0:T(8,128)S(1)} %get-tuple-element.28._), custom_call_target="tpu_custom_call" | custom-call | tf_op jit(solution)/shard_map/pallas_call | solution.py:351
  92.8 3.7 %collective-permute-start.8 = (f32[16,64,256]{2,1,0:T(8,128)S(1)}, f32[16,64,256]{2,1,0:T(8,128)S(1)}, u32[]{:S(2)}, u32[]{:S(2)}) collective-permute-start(f32[16,64,256]{2,1,0:T(8,128)S(1)} %get-tuple-element.30), channel_id=1, source_target_pairs={{0,1},{1,0},{2,3},{3,2},{4,5},{5,4},{6,7},{7,6},{8,9},{9,8},{10,11... | collective-permute-start | bytes 3145736 | tf_op jit(solution)/shard_map/ppermute | solution.py:374
  96.5 2.3 %collective-permute-done.8.got_ref = f32[16,64,256]{2,1,0:T(8,128)S(1)} collective-permute-done((f32[16,64,256]{2,1,0:T(8,128)S(1)}, f32[16,64,256]{2,1,0:T(8,128)S(1)}, u32[]{:S(2)}, u32[]{:S(2)}) %collective-permute-start.8) | collective-permute-done | bytes 1048608 | tf_op jit(solution)/shard_map/ppermute | solution.py:374
  101.0 6.6 %collective-permute-done.11.refs_1_ = f32[24,256]{1,0:T(8,128)S(1)} collective-permute-done((f32[24,256]{1,0:T(8,128)S(1)}, f32[24,256]{1,0:T(8,128)S(1)}, u32[]{:S(2)}, u32[]{:S(2)}) %collective-permute-start.11) | collective-permute-done | bytes 24608 | tf_op jit(solution)/shard_map/ppermute | solution.py:407
  108.3 6.1 %all-to-all-start.3 = ((f32[8,16,256]{2,1,0:T(8,128)}), f32[8,16,256]{2,1,0:T(8,128)S(1)}, u32[]{:S(2)}, u32[]{:S(2)}) async-start(f32[8,16,256]{2,1,0:T(8,128)} %bitcast.10), calls=%async_computation.3 | async-start | bytes 262144 | tf_op jit(solution)/shard_map/all_to_all | solution.py:299
  114.5 5.5 %shard_map.56 = (f32[8192,128]{1,0:T(8,128)}, f32[8,128]{1,0:T(8,128)S(1)}) custom-call(bf16[2048,1024]{1,0:T(8,128)(2,1)} %get-tuple-element.34.own_ref, bf16[2048,1024]{1,0:T(8,128)(2,1)} %collective-permute-done.9.other_ref, bf16[512,1024]{1,0:T(8,128)(2,1)S(1)} %bitcast.17, bf16[512,1024]{1,0:T(8,128)(2,1)S(1)} %bitcast.19, ...), custom_call_target="tpu_custom_call" | custom-call | tf_op jit(solution)/shard_map/pallas_call | solution.py:258
  119.9 2.9 %all-to-all-done.3 = f32[8,16,256]{2,1,0:T(8,128)S(1)} async-done(((f32[8,16,256]{2,1,0:T(8,128)}), f32[8,16,256]{2,1,0:T(8,128)S(1)}, u32[]{:S(2)}, u32[]{:S(2)}) %all-to-all-start.3) | async-done | bytes 131104 | tf_op jit(solution)/shard_map/all_to_all | solution.py:299
  123.5 3.5 %all-to-all-start.4 = ((f32[16,16,256]{2,1,0:T(8,128)}), f32[16,16,256]{2,1,0:T(8,128)S(1)}, u32[]{:S(2)}, u32[]{:S(2)}) async-start(f32[16,16,256]{2,1,0:T(8,128)} %bitcast.12), calls=%async_computation.4 | async-start | bytes 524288 | tf_op jit(solution)/shard_map/all_to_all | solution.py:299
  127.1 5.5 %shard_map.57 = (f32[8192,128]{1,0:T(8,128)}, f32[8,128]{1,0:T(8,128)S(1)}) custom-call(bf16[2048,1024]{1,0:T(8,128)(2,1)} %get-tuple-element.34.own_ref, bf16[2048,1024]{1,0:T(8,128)(2,1)} %collective-permute-done.9.other_ref, bf16[512,1024]{1,0:T(8,128)(2,1)S(1)} %bitcast.18, bf16[512,1024]{1,0:T(8,128)(2,1)S(1)} %bitcast.20, ...), custom_call_target="tpu_custom_call", output_to_operand_aliasing={{0}: (5, {})} | custom-call | tf_op jit(solution)/shard_map/pallas_call | solution.py:258
  132.5 1.8 %all-to-all-done.4 = f32[16,16,256]{2,1,0:T(8,128)S(1)} async-done(((f32[16,16,256]{2,1,0:T(8,128)}), f32[16,16,256]{2,1,0:T(8,128)S(1)}, u32[]{:S(2)}, u32[]{:S(2)}) %all-to-all-start.4) | async-done | bytes 262176 | tf_op jit(solution)/shard_map/all_to_all | solution.py:299
  134.4 8.3 %shard_map.59 = (f32[256,256]{1,0:T(8,128)}, f32[64,256]{1,0:T(8,128)}) custom-call(f32[256,256]{1,0:T(8,128)S(1)} %bitcast.24, f32[64,256]{1,0:T(8,128)S(1)} %get-tuple-element.43.refs_1_, f32[8,128]{1,0:T(8,128)S(1)} %get-tuple-element.44.refs_2_), custom_call_target="tpu_custom_call" | custom-call | tf_op jit(solution)/shard_map/pallas_call | solution.py:29
  (29 shorter events, 8.8 us)
Async XLA Ops:
  7.2 79.3 %all-gather.2.cloned.1.call-start = ((), (), s32[]{:S(2)}) async-start(), calls=%async_computation.5 | async-start | bytes 4456448 | tf_op jit(solution)/shard_map/all_gather | solution.py:301
  10.2 26.8 %all-to-all-start = ((f32[16,72,256]{2,1,0:T(8,128)}), f32[16,72,256]{2,1,0:T(8,128)S(1)}, u32[]{:S(2)}, u32[]{:S(2)}) async-start(f32[16,72,256]{2,1,0:T(8,128)} %bitcast.26), calls=%async_computation | async-start | bytes 2359296 | tf_op jit(solution)/shard_map/all_to_all | solution.py:299
  17.8 59.3 %copy-start = (bf16[128,1024]{1,0:T(8,128)(2,1)S(1)}, bf16[128,1024]{1,0:T(8,128)(2,1)}, u32[]{:S(2)}) copy-start(bf16[128,1024]{1,0:T(8,128)(2,1)} %refs_0_.3) | copy-start | bytes 786436
  17.8 11.6 %collective-permute-start = (bf16[128,1024]{1,0:T(8,128)(2,1)}, bf16[128,1024]{1,0:T(8,128)(2,1)S(1)}, u32[]{:S(2)}, u32[]{:S(2)}) collective-permute-start(bf16[128,1024]{1,0:T(8,128)(2,1)} %refs_0_.3), channel_id=1, source_target_pairs={{0,32},{32,64},{64,96},{96,128},{128,160},{160,192},{192,224},{224... | collective-permute-start | bytes 786440 | tf_op jit(solution)/shard_map/ppermute | solution.py:283
  19.5 9.9 %collective-permute-start.1 = (bf16[128,1024]{1,0:T(8,128)(2,1)}, bf16[128,1024]{1,0:T(8,128)(2,1)S(1)}, u32[]{:S(2)}, u32[]{:S(2)}) collective-permute-start(bf16[128,1024]{1,0:T(8,128)(2,1)} %refs_0_.3), channel_id=1, source_target_pairs={{0,224},{32,0},{64,32},{96,64},{128,96},{160,128},{192,160},{224,1... | collective-permute-start | bytes 786440 | tf_op jit(solution)/shard_map/ppermute | solution.py:283
  29.4 7.6 %collective-permute-start.2 = (bf16[128,1024]{1,0:T(8,128)(2,1)S(1)}, bf16[128,1024]{1,0:T(8,128)(2,1)S(1)}, u32[]{:S(2)}, u32[]{:S(2)}) collective-permute-start(bf16[128,1024]{1,0:T(8,128)(2,1)S(1)} %collective-permute-done.refs_1_), channel_id=1, source_target_pairs={{0,32},{32,64},{64,96},{96,128},{128,160},{160,192},{192,224},{224... | collective-permute-start | bytes 786440 | tf_op jit(solution)/shard_map/ppermute | solution.py:283
  29.4 7.6 %collective-permute-start.3 = (bf16[128,1024]{1,0:T(8,128)(2,1)S(1)}, bf16[128,1024]{1,0:T(8,128)(2,1)S(1)}, u32[]{:S(2)}, u32[]{:S(2)}) collective-permute-start(bf16[128,1024]{1,0:T(8,128)(2,1)S(1)} %collective-permute-done.1.refs_2_), channel_id=1, source_target_pairs={{0,224},{32,0},{64,32},{96,64},{128,96},{160,128},{192,160},{224,1... | collective-permute-start | bytes 786440 | tf_op jit(solution)/shard_map/ppermute | solution.py:283
  55.5 1.0 copy-start.1
  56.5 29.9 %all-to-all-start.2 = ((f32[16,72,256]{2,1,0:T(8,128)}), f32[16,72,256]{2,1,0:T(8,128)S(1)}, u32[]{:S(2)}, u32[]{:S(2)}) async-start(f32[16,72,256]{2,1,0:T(8,128)} %bitcast.23), calls=%async_computation.2 | async-start | bytes 2359296 | tf_op jit(solution)/shard_map/all_to_all | solution.py:299
  65.7 11.3 %collective-permute-start.4 = (bf16[128,1024]{1,0:T(8,128)(2,1)S(1)}, bf16[128,1024]{1,0:T(8,128)(2,1)S(1)}, u32[]{:S(2)}, u32[]{:S(2)}) collective-permute-start(bf16[128,1024]{1,0:T(8,128)(2,1)S(1)} %get-tuple-element.26.refs_3_), channel_id=1, source_target_pairs={{0,32},{32,64},{64,96},{96,128},{128,160},{160,192},{192,224},{224... | collective-permute-start | bytes 786440 | tf_op jit(solution)/shard_map/ppermute | solution.py:283
  65.8 11.3 %collective-permute-start.5 = (bf16[128,1024]{1,0:T(8,128)(2,1)S(1)}, bf16[128,1024]{1,0:T(8,128)(2,1)S(1)}, u32[]{:S(2)}, u32[]{:S(2)}) collective-permute-start(bf16[128,1024]{1,0:T(8,128)(2,1)S(1)} %get-tuple-element.27.refs_4_), channel_id=1, source_target_pairs={{0,224},{32,0},{64,32},{96,64},{128,96},{160,128},{192,160},{224,1... | collective-permute-start | bytes 786440 | tf_op jit(solution)/shard_map/ppermute | solution.py:283
  68.5 7.1 %collective-permute-start.7 = (bf16[64,1024]{1,0:T(8,128)(2,1)S(1)}, bf16[64,1024]{1,0:T(8,128)(2,1)S(1)}, u32[]{:S(2)}, u32[]{:S(2)}) collective-permute-start(bf16[64,1024]{1,0:T(8,128)(2,1)S(1)} %slice.7), channel_id=1, source_target_pairs={{0,192},{32,224},{64,0},{96,32},{128,64},{160,96},{192,128},{224,1... | collective-permute-start | bytes 393224 | tf_op jit(solution)/shard_map/ppermute | solution.py:283
  68.8 8.3 %collective-permute-start.6 = (bf16[64,1024]{1,0:T(8,128)(2,1)S(1)}, bf16[64,1024]{1,0:T(8,128)(2,1)S(1)}, u32[]{:S(2)}, u32[]{:S(2)}) collective-permute-start(bf16[64,1024]{1,0:T(8,128)(2,1)S(1)} %slice.6), channel_id=1, source_target_pairs={{0,64},{32,96},{64,128},{96,160},{128,192},{160,224},{192,0},{224,... | collective-permute-start | bytes 393224 | tf_op jit(solution)/shard_map/ppermute | solution.py:283
  92.8 6.0 %collective-permute-start.8 = (f32[16,64,256]{2,1,0:T(8,128)S(1)}, f32[16,64,256]{2,1,0:T(8,128)S(1)}, u32[]{:S(2)}, u32[]{:S(2)}) collective-permute-start(f32[16,64,256]{2,1,0:T(8,128)S(1)} %get-tuple-element.30), channel_id=1, source_target_pairs={{0,1},{1,0},{2,3},{3,2},{4,5},{5,4},{6,7},{7,6},{8,9},{9,8},{10,11... | collective-permute-start | bytes 3145736 | tf_op jit(solution)/shard_map/ppermute | solution.py:374
  100.0 14.4 %collective-permute-start.9 = (bf16[2048,1024]{1,0:T(8,128)(2,1)}, bf16[2048,1024]{1,0:T(8,128)(2,1)}, u32[]{:S(2)}, u32[]{:S(2)}) collective-permute-start(bf16[2048,1024]{1,0:T(8,128)(2,1)} %get-tuple-element.34.own_ref), channel_id=1, source_target_pairs={{0,1},{1,0},{2,3},{3,2},{4,5},{5,4},{6,7},{7,6},{8,9},{9,8},{10,11... | collective-permute-start | bytes 12582920 | tf_op jit(solution)/shard_map/ppermute | solution.py:410
  100.5 13.9 %collective-permute-start.10 = (bf16[4,128,1024]{2,1,0:T(8,128)(2,1)}, bf16[4,128,1024]{2,1,0:T(8,128)(2,1)S(1)}, u32[]{:S(2)}, u32[]{:S(2)}) collective-permute-start(bf16[4,128,1024]{2,1,0:T(8,128)(2,1)} %get-tuple-element.36), channel_id=1, source_target_pairs={{0,1},{1,0},{2,3},{3,2},{4,5},{5,4},{6,7},{7,6},{8,9},{9,8},{10,11... | collective-permute-start | bytes 3145736 | tf_op jit(solution)/shard_map/ppermute | solution.py:411
  100.6 7.0 %collective-permute-start.11 = (f32[24,256]{1,0:T(8,128)S(1)}, f32[24,256]{1,0:T(8,128)S(1)}, u32[]{:S(2)}, u32[]{:S(2)}) collective-permute-start(f32[24,256]{1,0:T(8,128)S(1)} %get-tuple-element.37.refs_0_), channel_id=1, source_target_pairs={{0,1},{1,0},{2,3},{3,2},{4,5},{5,4},{6,7},{7,6},{8,9},{9,8},{10,11... | collective-permute-start | bytes 73736 | tf_op jit(solution)/shard_map/ppermute | solution.py:407
  108.3 14.5 %all-to-all-start.3 = ((f32[8,16,256]{2,1,0:T(8,128)}), f32[8,16,256]{2,1,0:T(8,128)S(1)}, u32[]{:S(2)}, u32[]{:S(2)}) async-start(f32[8,16,256]{2,1,0:T(8,128)} %bitcast.10), calls=%async_computation.3 | async-start | bytes 262144 | tf_op jit(solution)/shard_map/all_to_all | solution.py:299
  123.5 10.8 %all-to-all-start.4 = ((f32[16,16,256]{2,1,0:T(8,128)}), f32[16,16,256]{2,1,0:T(8,128)S(1)}, u32[]{:S(2)}, u32[]{:S(2)}) async-start(f32[16,16,256]{2,1,0:T(8,128)} %bitcast.12), calls=%async_computation.4 | async-start | bytes 524288 | tf_op jit(solution)/shard_map/all_to_all | solution.py:299
Sparse Core Ops, SparseCore 0:
  10.4 69.1 all-gather.1

commit v8 on v7

--- a/solution.py
+++ b/solution.py
@@ -155,7 +155,7 @@
             sent_ref[place, target : target + rows, :] = piece[source : source + rows, :]
 
 
-def cross_kernel(subjects, kept_ref, got_ref, mean_ref, _, __, out_ref, own_ref, ___, ____, full):
+def cross_kernel(subjects, kept_ref, got_ref, mean_ref, out_ref, own_ref, full):
     sketch = kept_ref[...] + got_ref[...]
     groups, half, cols = sketch.shape
     flat = sketch.reshape(groups * half, cols)
@@ -374,37 +374,32 @@
     got = lax.ppermute(sent, "vox", swap)
     cross_rows = width // col_count
     slice_shape = (cross_rows + PAD, width)
-    slices, own, centered, col_sent = pl.pallas_call(
+    slices, own = pl.pallas_call(
         functools.partial(cross_kernel, subjects),
         grid=(1,),
         in_specs=[
             pl.BlockSpec((col_count, half_rows, width), lambda i: (0, 0, 0)),
             pl.BlockSpec((col_count, half_rows, width), lambda i: (0, 0, 0)),
             pl.BlockSpec((1, vox_half), lambda i: (0, 0)),
-            pl.BlockSpec(memory_space=pl.ANY),
-            pl.BlockSpec(memory_space=pl.ANY),
         ],
         out_specs=[
             pl.BlockSpec(slice_shape, lambda i: (0, 0)),
             pl.BlockSpec((half_rows, width), lambda i: (0, 0)),
-            pl.BlockSpec(memory_space=pl.ANY),
-            pl.BlockSpec(memory_space=pl.ANY),
         ],
         scratch_shapes=[pltpu.VMEM((width, width), F32)],
         out_shape=[
             sd(slice_shape),
             sd((half_rows, width)),
-            sd((block_rows, vox_half), BF16),
-            sd(group_shape, BF16),
-        ],
-        input_output_aliases={3: 2, 4: 3},
+        ],
         compiler_params=LARGE,
-    )(kept, got, mean, centered, col_sent)
-    shared, means = call(
+    )(kept, got, mean)
+    shared, means, centered, col_sent = call(
         functools.partial(pair_kernel, row_count),
         [sd((row_count * cross_rows, width)), sd((vox_count, vox_half))],
         slices,
         lax.ppermute(slices, "vox", swap),
+        carry=[centered, col_sent],
+        params=LARGE,
     )
 
     other = lax.ppermute(centered, "vox", swap)

time: 150 us -> 145 us (0.967)
  waiting for transfers between devices: 39.2 us -> 33.1 us
    ppermute x1, waiting for transfers between devices: 6.61 us -> 0.85 us  [shards(): lax.ppermute(slices, 'vox', swap)]
    all_to_all x4, waiting for transfers between devices: 12.8 us -> 10 us  [exchange(): return lax.all_to_all(value, axis, 0, 0, tiled=True)]
  transfers between devices with their start and end apart: 17 -> 17, of which waited for: 9 -> 11; matrix products, arithmetic and copies ran while one was open for 0% -> 0% of each run, Pallas kernels for 10% -> 10%
where the time goes in v8:
time: 145 us; the launch traced here: 143 us
  starting transfers between devices  44.8 us (31%)
  waiting for transfers between devices  33.1 us (23%)
  Pallas kernels  32 us (22%)
  blocking collectives  18.3 us (13%)
  between operations  14.1 us (10%)
    all_to_all x4, starting transfers between devices, exchange(): return lax.all_to_all(value, axis, 0, 0, tiled=True)  26.4 us
    all_to_all x1, blocking collectives, exchange(): return lax.all_to_all(value, axis, 0, 0, tiled=True)  18.3 us
    ppermute x8, waiting for transfers between devices, ring_step(): return (lax.ppermute(up, axis, ahead), lax.ppermute(down, axis, back))  16.8 us
    ppermute x8, starting transfers between devices, ring_step(): return (lax.ppermute(up, axis, ahead), lax.ppermute(down, axis, back))  13.6 us
    pallas_call x6, Pallas kernels, call(): pl.pallas_call(body, out_shape=[*out_shape, *[sd(x.shape, x.dtype) for x...  12.2 us
    pallas_call x2, Pallas kernels, gram_part(): pl.pallas_call(functools.partial(gram_kernel, vox_total), grid=(steps,),...  10.9 us
    all_to_all x4, waiting for transfers between devices, exchange(): return lax.all_to_all(value, axis, 0, 0, tiled=True)  10 us
    pallas_call x1, Pallas kernels, shards(): pl.pallas_call(functools.partial(sketch_kernel, col_count, vox_total), gr...  6.33 us
  transfers between devices with their start and end apart: 17, of which 11 were waited for; matrix products, arithmetic and copies ran while one was open for 0% of the time, Pallas kernels for 10%

profile of v8, /device:TPU:1, one launch (start us, length us, event | category | flops | bytes accessed | tf_op | source)
XLA Modules:
  0.0 143.3 jit_solution(12429470190312039043)
XLA Ops:
  7.9 2.3 %shard_map.49 = f32[1152,256]{1,0:T(8,128)} custom-call(bf16[128,1024]{1,0:T(8,128)(2,1)} %refs_0_.3, bf16[128,256]{1,0:T(8,128)(2,1)} %refs_1_.1), custom_call_target="tpu_custom_call" | custom-call | tf_op jit(solution)/shard_map/pallas_call | solution.py:29
  10.2 7.6 %all-to-all-start = ((f32[16,72,256]{2,1,0:T(8,128)}), f32[16,72,256]{2,1,0:T(8,128)S(1)}, u32[]{:S(2)}, u32[]{:S(2)}) async-start(f32[16,72,256]{2,1,0:T(8,128)} %bitcast.26), calls=%async_computation | async-start | bytes 2359296 | tf_op jit(solution)/shard_map/all_to_all | solution.py:299
  17.8 1.7 %collective-permute-start = (bf16[128,1024]{1,0:T(8,128)(2,1)}, bf16[128,1024]{1,0:T(8,128)(2,1)S(1)}, u32[]{:S(2)}, u32[]{:S(2)}) collective-permute-start(bf16[128,1024]{1,0:T(8,128)(2,1)} %refs_0_.3), channel_id=1, source_target_pairs={{0,32},{32,64},{64,96},{96,128},{128,160},{160,192},{192,224},{224... | collective-permute-start | bytes 786440 | tf_op jit(solution)/shard_map/ppermute | solution.py:283
  19.5 4.0 %collective-permute-start.1 = (bf16[128,1024]{1,0:T(8,128)(2,1)}, bf16[128,1024]{1,0:T(8,128)(2,1)S(1)}, u32[]{:S(2)}, u32[]{:S(2)}) collective-permute-start(bf16[128,1024]{1,0:T(8,128)(2,1)} %refs_0_.3), channel_id=1, source_target_pairs={{0,224},{32,0},{64,32},{96,64},{128,96},{160,128},{192,160},{224,1... | collective-permute-start | bytes 786440 | tf_op jit(solution)/shard_map/ppermute | solution.py:283
  23.6 5.8 %collective-permute-done.refs_1_ = bf16[128,1024]{1,0:T(8,128)(2,1)S(1)} collective-permute-done((bf16[128,1024]{1,0:T(8,128)(2,1)}, bf16[128,1024]{1,0:T(8,128)(2,1)S(1)}, u32[]{:S(2)}, u32[]{:S(2)}) %collective-permute-start) | collective-permute-done | bytes 262176 | tf_op jit(solution)/shard_map/ppermute | solution.py:283
  29.4 2.7 %collective-permute-start.3 = (bf16[128,1024]{1,0:T(8,128)(2,1)S(1)}, bf16[128,1024]{1,0:T(8,128)(2,1)S(1)}, u32[]{:S(2)}, u32[]{:S(2)}) collective-permute-start(bf16[128,1024]{1,0:T(8,128)(2,1)S(1)} %collective-permute-done.1.refs_2_), channel_id=1, source_target_pairs={{0,224},{32,0},{64,32},{96,64},{128,96},{160,128},{192,160},{224,1... | collective-permute-start | bytes 786440 | tf_op jit(solution)/shard_map/ppermute | solution.py:283
  32.1 4.9 %collective-permute-done.2.refs_3_.refs_1_ = bf16[128,1024]{1,0:T(8,128)(2,1)S(1)} collective-permute-done((bf16[128,1024]{1,0:T(8,128)(2,1)S(1)}, bf16[128,1024]{1,0:T(8,128)(2,1)S(1)}, u32[]{:S(2)}, u32[]{:S(2)}) %collective-permute-start.2) | collective-permute-done | bytes 262176 | tf_op jit(solution)/shard_map/ppermute | solution.py:283
  37.1 18.3 %all_to_all.55 = f32[8,72,256]{2,1,0:T(8,128)S(1)} all-to-all(f32[8,72,256]{2,1,0:T(8,128)S(1)} %bitcast.22), channel_id=1, replica_groups=mesh['row'=8,'col'=16,'vox'=2] {'row'}, dimensions={0} | all-to-all | bytes 1179648 | tf_op jit(solution)/shard_map/all_to_all | solution.py:299
  56.5 9.2 %all-to-all-start.2 = ((f32[16,72,256]{2,1,0:T(8,128)}), f32[16,72,256]{2,1,0:T(8,128)S(1)}, u32[]{:S(2)}, u32[]{:S(2)}) async-start(f32[16,72,256]{2,1,0:T(8,128)} %bitcast.23), calls=%async_computation.2 | async-start | bytes 2359296 | tf_op jit(solution)/shard_map/all_to_all | solution.py:299
  65.8 2.7 %collective-permute-start.5 = (bf16[128,1024]{1,0:T(8,128)(2,1)S(1)}, bf16[128,1024]{1,0:T(8,128)(2,1)S(1)}, u32[]{:S(2)}, u32[]{:S(2)}) collective-permute-start(bf16[128,1024]{1,0:T(8,128)(2,1)S(1)} %get-tuple-element.27.refs_4_), channel_id=1, source_target_pairs={{0,224},{32,0},{64,32},{96,64},{128,96},{160,128},{192,160},{224,1... | collective-permute-start | bytes 786440 | tf_op jit(solution)/shard_map/ppermute | solution.py:283
  68.8 2.2 %collective-permute-start.6 = (bf16[64,1024]{1,0:T(8,128)(2,1)S(1)}, bf16[64,1024]{1,0:T(8,128)(2,1)S(1)}, u32[]{:S(2)}, u32[]{:S(2)}) collective-permute-start(bf16[64,1024]{1,0:T(8,128)(2,1)S(1)} %slice.6), channel_id=1, source_target_pairs={{0,64},{32,96},{64,128},{96,160},{128,192},{160,224},{192,0},{224,... | collective-permute-start | bytes 393224 | tf_op jit(solution)/shard_map/ppermute | solution.py:283
  71.0 4.6 %collective-permute-done.7.refs_8_ = bf16[64,1024]{1,0:T(8,128)(2,1)S(1)} collective-permute-done((bf16[64,1024]{1,0:T(8,128)(2,1)S(1)}, bf16[64,1024]{1,0:T(8,128)(2,1)S(1)}, u32[]{:S(2)}, u32[]{:S(2)}) %collective-permute-start.7) | collective-permute-done | bytes 131104 | tf_op jit(solution)/shard_map/ppermute | solution.py:283
  75.6 1.5 %collective-permute-done.6.refs_7_ = bf16[64,1024]{1,0:T(8,128)(2,1)S(1)} collective-permute-done((bf16[64,1024]{1,0:T(8,128)(2,1)S(1)}, bf16[64,1024]{1,0:T(8,128)(2,1)S(1)}, u32[]{:S(2)}, u32[]{:S(2)}) %collective-permute-start.6) | collective-permute-done | bytes 131104 | tf_op jit(solution)/shard_map/ppermute | solution.py:283
  77.1 1.3 shard_map.52
  78.4 8.0 %all-to-all-done.2 = f32[16,72,256]{2,1,0:T(8,128)S(1)} async-done(((f32[16,72,256]{2,1,0:T(8,128)}), f32[16,72,256]{2,1,0:T(8,128)S(1)}, u32[]{:S(2)}, u32[]{:S(2)}) %all-to-all-start.2) | async-done | bytes 1179680 | tf_op jit(solution)/shard_map/all_to_all | solution.py:299
  86.4 6.3 %shard_map.53 = (f32[16,64,256]{2,1,0:T(8,128)S(1)}, f32[16,64,256]{2,1,0:T(8,128)S(1)}, f32[1,1024]{1,0:T(1,128)S(1)}, bf16[2048,1024]{1,0:T(8,128)(2,1)}) custom-call(bf16[2048,1024]{1,0:T(8,128)(2,1)} %all-gather.2.cloned.1.call-done.maps_ref, f32[1152,256]{1,0:T(8,128)S(1)} %bitcast.15, f32[8,128]{1,0:T(8,128)S(1)} %get-tuple-element.28._), custom_call_target="tpu_custom_call" | custom-call | tf_op jit(solution)/shard_map/pallas_call | solution.py:351
  92.8 3.7 %collective-permute-start.8 = (f32[16,64,256]{2,1,0:T(8,128)S(1)}, f32[16,64,256]{2,1,0:T(8,128)S(1)}, u32[]{:S(2)}, u32[]{:S(2)}) collective-permute-start(f32[16,64,256]{2,1,0:T(8,128)S(1)} %get-tuple-element.30), channel_id=1, source_target_pairs={{0,1},{1,0},{2,3},{3,2},{4,5},{5,4},{6,7},{7,6},{8,9},{9,8},{10,11... | collective-permute-start | bytes 3145736 | tf_op jit(solution)/shard_map/ppermute | solution.py:374
  96.5 2.3 %collective-permute-done.8.got_ref = f32[16,64,256]{2,1,0:T(8,128)S(1)} collective-permute-done((f32[16,64,256]{2,1,0:T(8,128)S(1)}, f32[16,64,256]{2,1,0:T(8,128)S(1)}, u32[]{:S(2)}, u32[]{:S(2)}) %collective-permute-start.8) | collective-permute-done | bytes 1048608 | tf_op jit(solution)/shard_map/ppermute | solution.py:374
  102.5 6.1 %all-to-all-start.3 = ((f32[8,16,256]{2,1,0:T(8,128)}), f32[8,16,256]{2,1,0:T(8,128)S(1)}, u32[]{:S(2)}, u32[]{:S(2)}) async-start(f32[8,16,256]{2,1,0:T(8,128)} %bitcast.10), calls=%async_computation.3 | async-start | bytes 262144 | tf_op jit(solution)/shard_map/all_to_all | solution.py:299
  111.0 5.4 %shard_map.56 = (f32[8192,128]{1,0:T(8,128)}, f32[8,128]{1,0:T(8,128)S(1)}) custom-call(bf16[2048,1024]{1,0:T(8,128)(2,1)} %get-tuple-element.35.own_ref, bf16[2048,1024]{1,0:T(8,128)(2,1)} %collective-permute-done.10.other_ref, bf16[512,1024]{1,0:T(8,128)(2,1)S(1)} %bitcast.17, bf16[512,1024]{1,0:T(8,128)(2,1)S(1)} %bitcast.19, ...), custom_call_target="tpu_custom_call" | custom-call | tf_op jit(solution)/shard_map/pallas_call | solution.py:258
  117.3 3.5 %all-to-all-start.4 = ((f32[16,16,256]{2,1,0:T(8,128)}), f32[16,16,256]{2,1,0:T(8,128)S(1)}, u32[]{:S(2)}, u32[]{:S(2)}) async-start(f32[16,16,256]{2,1,0:T(8,128)} %bitcast.12), calls=%async_computation.4 | async-start | bytes 524288 | tf_op jit(solution)/shard_map/all_to_all | solution.py:299
  120.9 5.5 %shard_map.57 = (f32[8192,128]{1,0:T(8,128)}, f32[8,128]{1,0:T(8,128)S(1)}) custom-call(bf16[2048,1024]{1,0:T(8,128)(2,1)} %get-tuple-element.35.own_ref, bf16[2048,1024]{1,0:T(8,128)(2,1)} %collective-permute-done.10.other_ref, bf16[512,1024]{1,0:T(8,128)(2,1)S(1)} %bitcast.18, bf16[512,1024]{1,0:T(8,128)(2,1)S(1)} %bitcast.20, ...), custom_call_target="tpu_custom_call", output_to_operand_aliasing={{0}: (5, {})} | custom-call | tf_op jit(solution)/shard_map/pallas_call | solution.py:258
  126.3 1.9 %all-to-all-done.4 = f32[16,16,256]{2,1,0:T(8,128)S(1)} async-done(((f32[16,16,256]{2,1,0:T(8,128)}), f32[16,16,256]{2,1,0:T(8,128)S(1)}, u32[]{:S(2)}, u32[]{:S(2)}) %all-to-all-start.4) | async-done | bytes 262176 | tf_op jit(solution)/shard_map/all_to_all | solution.py:299
  128.2 8.3 %shard_map.59 = (f32[256,256]{1,0:T(8,128)}, f32[64,256]{1,0:T(8,128)}) custom-call(f32[256,256]{1,0:T(8,128)S(1)} %bitcast.24, f32[64,256]{1,0:T(8,128)S(1)} %get-tuple-element.43.refs_1_, f32[8,128]{1,0:T(8,128)S(1)} %get-tuple-element.44.refs_2_), custom_call_target="tpu_custom_call" | custom-call | tf_op jit(solution)/shard_map/pallas_call | solution.py:29
  (29 shorter events, 9.3 us)
Async XLA Ops:
  7.2 79.3 %all-gather.2.cloned.1.call-start = ((), (), s32[]{:S(2)}) async-start(), calls=%async_computation.5 | async-start | bytes 4456448 | tf_op jit(solution)/shard_map/all_gather | solution.py:301
  10.2 26.8 %all-to-all-start = ((f32[16,72,256]{2,1,0:T(8,128)}), f32[16,72,256]{2,1,0:T(8,128)S(1)}, u32[]{:S(2)}, u32[]{:S(2)}) async-start(f32[16,72,256]{2,1,0:T(8,128)} %bitcast.26), calls=%async_computation | async-start | bytes 2359296 | tf_op jit(solution)/shard_map/all_to_all | solution.py:299
  17.8 59.3 %copy-start = (bf16[128,1024]{1,0:T(8,128)(2,1)S(1)}, bf16[128,1024]{1,0:T(8,128)(2,1)}, u32[]{:S(2)}) copy-start(bf16[128,1024]{1,0:T(8,128)(2,1)} %refs_0_.3) | copy-start | bytes 786436
  17.8 11.6 %collective-permute-start = (bf16[128,1024]{1,0:T(8,128)(2,1)}, bf16[128,1024]{1,0:T(8,128)(2,1)S(1)}, u32[]{:S(2)}, u32[]{:S(2)}) collective-permute-start(bf16[128,1024]{1,0:T(8,128)(2,1)} %refs_0_.3), channel_id=1, source_target_pairs={{0,32},{32,64},{64,96},{96,128},{128,160},{160,192},{192,224},{224... | collective-permute-start | bytes 786440 | tf_op jit(solution)/shard_map/ppermute | solution.py:283
  19.5 9.9 %collective-permute-start.1 = (bf16[128,1024]{1,0:T(8,128)(2,1)}, bf16[128,1024]{1,0:T(8,128)(2,1)S(1)}, u32[]{:S(2)}, u32[]{:S(2)}) collective-permute-start(bf16[128,1024]{1,0:T(8,128)(2,1)} %refs_0_.3), channel_id=1, source_target_pairs={{0,224},{32,0},{64,32},{96,64},{128,96},{160,128},{192,160},{224,1... | collective-permute-start | bytes 786440 | tf_op jit(solution)/shard_map/ppermute | solution.py:283
  29.4 7.6 %collective-permute-start.2 = (bf16[128,1024]{1,0:T(8,128)(2,1)S(1)}, bf16[128,1024]{1,0:T(8,128)(2,1)S(1)}, u32[]{:S(2)}, u32[]{:S(2)}) collective-permute-start(bf16[128,1024]{1,0:T(8,128)(2,1)S(1)} %collective-permute-done.refs_1_), channel_id=1, source_target_pairs={{0,32},{32,64},{64,96},{96,128},{128,160},{160,192},{192,224},{224... | collective-permute-start | bytes 786440 | tf_op jit(solution)/shard_map/ppermute | solution.py:283
  29.4 7.6 %collective-permute-start.3 = (bf16[128,1024]{1,0:T(8,128)(2,1)S(1)}, bf16[128,1024]{1,0:T(8,128)(2,1)S(1)}, u32[]{:S(2)}, u32[]{:S(2)}) collective-permute-start(bf16[128,1024]{1,0:T(8,128)(2,1)S(1)} %collective-permute-done.1.refs_2_), channel_id=1, source_target_pairs={{0,224},{32,0},{64,32},{96,64},{128,96},{160,128},{192,160},{224,1... | collective-permute-start | bytes 786440 | tf_op jit(solution)/shard_map/ppermute | solution.py:283
  55.5 1.0 copy-start.1
  56.5 29.9 %all-to-all-start.2 = ((f32[16,72,256]{2,1,0:T(8,128)}), f32[16,72,256]{2,1,0:T(8,128)S(1)}, u32[]{:S(2)}, u32[]{:S(2)}) async-start(f32[16,72,256]{2,1,0:T(8,128)} %bitcast.23), calls=%async_computation.2 | async-start | bytes 2359296 | tf_op jit(solution)/shard_map/all_to_all | solution.py:299
  65.7 11.3 %collective-permute-start.4 = (bf16[128,1024]{1,0:T(8,128)(2,1)S(1)}, bf16[128,1024]{1,0:T(8,128)(2,1)S(1)}, u32[]{:S(2)}, u32[]{:S(2)}) collective-permute-start(bf16[128,1024]{1,0:T(8,128)(2,1)S(1)} %get-tuple-element.26.refs_3_), channel_id=1, source_target_pairs={{0,32},{32,64},{64,96},{96,128},{128,160},{160,192},{192,224},{224... | collective-permute-start | bytes 786440 | tf_op jit(solution)/shard_map/ppermute | solution.py:283
  65.8 11.3 %collective-permute-start.5 = (bf16[128,1024]{1,0:T(8,128)(2,1)S(1)}, bf16[128,1024]{1,0:T(8,128)(2,1)S(1)}, u32[]{:S(2)}, u32[]{:S(2)}) collective-permute-start(bf16[128,1024]{1,0:T(8,128)(2,1)S(1)} %get-tuple-element.27.refs_4_), channel_id=1, source_target_pairs={{0,224},{32,0},{64,32},{96,64},{128,96},{160,128},{192,160},{224,1... | collective-permute-start | bytes 786440 | tf_op jit(solution)/shard_map/ppermute | solution.py:283
  68.5 7.1 %collective-permute-start.7 = (bf16[64,1024]{1,0:T(8,128)(2,1)S(1)}, bf16[64,1024]{1,0:T(8,128)(2,1)S(1)}, u32[]{:S(2)}, u32[]{:S(2)}) collective-permute-start(bf16[64,1024]{1,0:T(8,128)(2,1)S(1)} %slice.7), channel_id=1, source_target_pairs={{0,192},{32,224},{64,0},{96,32},{128,64},{160,96},{192,128},{224,1... | collective-permute-start | bytes 393224 | tf_op jit(solution)/shard_map/ppermute | solution.py:283
  68.8 8.3 %collective-permute-start.6 = (bf16[64,1024]{1,0:T(8,128)(2,1)S(1)}, bf16[64,1024]{1,0:T(8,128)(2,1)S(1)}, u32[]{:S(2)}, u32[]{:S(2)}) collective-permute-start(bf16[64,1024]{1,0:T(8,128)(2,1)S(1)} %slice.6), channel_id=1, source_target_pairs={{0,64},{32,96},{64,128},{96,160},{128,192},{160,224},{192,0},{224,... | collective-permute-start | bytes 393224 | tf_op jit(solution)/shard_map/ppermute | solution.py:283
  92.8 6.0 %collective-permute-start.8 = (f32[16,64,256]{2,1,0:T(8,128)S(1)}, f32[16,64,256]{2,1,0:T(8,128)S(1)}, u32[]{:S(2)}, u32[]{:S(2)}) collective-permute-start(f32[16,64,256]{2,1,0:T(8,128)S(1)} %get-tuple-element.30), channel_id=1, source_target_pairs={{0,1},{1,0},{2,3},{3,2},{4,5},{5,4},{6,7},{7,6},{8,9},{9,8},{10,11... | collective-permute-start | bytes 3145736 | tf_op jit(solution)/shard_map/ppermute | solution.py:374
  100.0 1.3 collective-permute-start.9
  102.0 9.0 %collective-permute-start.10 = (bf16[2048,1024]{1,0:T(8,128)(2,1)}, bf16[2048,1024]{1,0:T(8,128)(2,1)}, u32[]{:S(2)}, u32[]{:S(2)}) collective-permute-start(bf16[2048,1024]{1,0:T(8,128)(2,1)} %get-tuple-element.35.own_ref), channel_id=1, source_target_pairs={{0,1},{1,0},{2,3},{3,2},{4,5},{5,4},{6,7},{7,6},{8,9},{9,8},{10,11... | collective-permute-start | bytes 12582920 | tf_op jit(solution)/shard_map/ppermute | solution.py:405
  102.4 7.5 %collective-permute-start.11 = (bf16[4,128,1024]{2,1,0:T(8,128)(2,1)}, bf16[4,128,1024]{2,1,0:T(8,128)(2,1)S(1)}, u32[]{:S(2)}, u32[]{:S(2)}) collective-permute-start(bf16[4,128,1024]{2,1,0:T(8,128)(2,1)} %get-tuple-element.37), channel_id=1, source_target_pairs={{0,1},{1,0},{2,3},{3,2},{4,5},{5,4},{6,7},{7,6},{8,9},{9,8},{10,11... | collective-permute-start | bytes 3145736 | tf_op jit(solution)/shard_map/ppermute | solution.py:406
  102.5 14.1 %all-to-all-start.3 = ((f32[8,16,256]{2,1,0:T(8,128)}), f32[8,16,256]{2,1,0:T(8,128)S(1)}, u32[]{:S(2)}, u32[]{:S(2)}) async-start(f32[8,16,256]{2,1,0:T(8,128)} %bitcast.10), calls=%async_computation.3 | async-start | bytes 262144 | tf_op jit(solution)/shard_map/all_to_all | solution.py:299
  117.3 10.9 %all-to-all-start.4 = ((f32[16,16,256]{2,1,0:T(8,128)}), f32[16,16,256]{2,1,0:T(8,128)S(1)}, u32[]{:S(2)}, u32[]{:S(2)}) async-start(f32[16,16,256]{2,1,0:T(8,128)} %bitcast.12), calls=%async_computation.4 | async-start | bytes 524288 | tf_op jit(solution)/shard_map/all_to_all | solution.py:299
Sparse Core Ops, SparseCore 0:
  10.4 69.1 all-gather.1
